TPU v7x, 32 devices: a whole 2x2x4 slice. The times are simulated.
32 devices in a mesh: req: 8 (over z, y), exp: 4 (over x, core).
Axes of the slice: x: 2, y: 2, z: 4, core: 2. Of those that a mesh axis runs over, the one named last changes fastest.
Arguments:
- hidden_in: bfloat16 [2048, 2048], P(('req', 'exp')), may hold values from -6 to 6
- query_in: bfloat16 [2048, 2048], P('req', 'exp'), may hold values from -6 to 6
- key_in: bfloat16 [2048, 2048], P('req', 'exp'), may hold values from -6 to 6
- value_in: bfloat16 [2048, 2048], P('req', 'exp'), may hold values from -24 to 24
- query_gain: float32 [128], replicated, may hold values from 0.5 to 2.5
- key_gain: float32 [128], replicated, may hold values from 0.5 to 2.5
- cache_keys: bfloat16 [16, 32, 2048], P('req', None, 'exp'), may hold values from -400 to 400
- cache_values: bfloat16 [16, 32, 2048], P('req', None, 'exp'), may hold values from -24 to 24
- cache_block: int32 [32], replicated, may hold values from -1 to 15, as said below
- request_lengths: int32 [8, 4], P('req'), may hold values from 1 to 128, 256 in all within a row
- out_proj: bfloat16 [2048, 2048], P('exp'), may hold values from -0.125 to 0.125
- norm_gain: float32 [2048], replicated, may hold values from 0.25 to 1.75
- expert_ids: int32 [2048, 8], P(('req', 'exp')), may hold values from 0 to 15, all different within a row; in each aligned block of 64 rows (0 to 63, 64 to 127, ...) at most 40 rows name the same one
- gate_values: float32 [2048, 8], P(('req', 'exp')), may hold values from 0.4 to 1.6
- old_slots: int32 [16], replicated, may hold values from 0 to 15, each once
- new_replicas: int32 [8], replicated, may hold values from 0 to 15
- slot_weights: bfloat16 [16, 3, 2048, 1024], P('req', None, None, 'exp'), may hold values from -0.125 to 0.125
Outputs:
- layer_out: bfloat16 [2048, 2048], P(('req', 'exp'))
- replica_weights: bfloat16 [8, 3, 2048, 1024], P('req', None, None, 'exp')
Inputs may be any that keep to these rules, and one draw needn't show every extreme that they name: `cache_block`: each index of req has exactly 2 of its 4 requests with a block; every block serves exactly one request. `expert_ids`: in each aligned block of 64 rows (the rows of one device) no expert is named by more than 40 rows, a bound that some block reaches; the 8 experts of a row differ. `old_slots`: every expert is in exactly one slot. `request_lengths`: the lengths of each index of req sum to 256.
All inputs are finite; a program needn't handle non-finite values.
Results may differ from a plain program's by a relative error of at most 0.025.
Values may be sent and summed in bfloat16 or wider, within the bound.
No kernel may reach another device: no remote copies, remote signals or barrier semaphores. Data moves between devices by JAX's collectives and lax.ppermute only.
A program may use at most 128 MiB of HBM per device.

v0:
```python
import functools
import math

import jax
import jax.numpy as jnp
from jax import lax
from jax.experimental import pallas as pl
from jax.experimental.pallas import tpu as pltpu
from jax.sharding import PartitionSpec as P


def prepare(values, gain, position):
    vector = values.astype(jnp.float32)
    scaled = vector * lax.rsqrt(jnp.mean(vector * vector, axis=-1, keepdims=True) + 1e-06) * gain
    half_size = scaled.shape[-1] // 2
    frequency = 10000.0 ** (-(jnp.arange(half_size, dtype=jnp.float32) * 2.0 / scaled.shape[-1]))
    angles = position[:, None] * frequency[None, :]
    cosine = jnp.cos(angles)[:, None, :]
    sine_part = jnp.sin(angles)[:, None, :]
    lower_half = scaled[..., :half_size]
    upper_half = scaled[..., half_size:]
    rotated = jnp.concatenate(
        [
            lower_half * cosine - upper_half * sine_part,
            upper_half * cosine + lower_half * sine_part,
        ],
        axis=-1,
    )
    return rotated.astype(jnp.bfloat16)


def compact(block_rows, slots_wanted):
    live = block_rows >= 0
    ranks = jnp.cumsum(live.astype(jnp.int32), axis=1) - 1
    request_idx = jnp.arange(block_rows.shape[1], dtype=jnp.int32)[None, :]
    chosen_blocks = []
    chosen_requests = []
    for slot_num in range(slots_wanted):
        picked = live & (ranks == slot_num)
        chosen_blocks.append(jnp.sum(jnp.where(picked, block_rows, 0), axis=1))
        chosen_requests.append(jnp.sum(jnp.where(picked, request_idx, 0), axis=1))
    return (jnp.stack(chosen_blocks, axis=1), jnp.stack(chosen_requests, axis=1))


def experts_kernel(first_slot_ref, tok_ref, weights_ref, out_ref):
    slot_count, _, model_width, _ = weights_ref.shape
    rows = tok_ref[:, :model_width]
    codes = tok_ref[:, model_width:].astype(jnp.float32)
    half_codes = codes.shape[1] // 2
    lane = lax.broadcasted_iota(jnp.int32, codes.shape, 1)
    total = None
    for slot_num in range(slot_count):
        wanted = first_slot_ref[0] + slot_num
        picked = (lane == wanted) | (lane == wanted + half_codes)
        factor = jnp.sum(jnp.where(picked, codes, 0.0), axis=1, keepdims=True)
        gate_act = jnp.dot(rows, weights_ref[slot_num, 0], preferred_element_type=jnp.float32)
        up_act = jnp.dot(rows, weights_ref[slot_num, 1], preferred_element_type=jnp.float32)
        hidden = gate_act / (1.0 + jnp.exp(-gate_act)) * up_act
        hidden = (hidden * factor).astype(jnp.bfloat16)
        part = lax.dot_general(
            hidden,
            weights_ref[slot_num, 2],
            (((1,), (1,)), ((), ())),
            preferred_element_type=jnp.float32,
        )
        total = part if total is None else total + part
    out_ref[...] = total.astype(out_ref.dtype)


def run_experts(first_slot, tokens, slot_weights, block):
    count, ext_width = tokens.shape
    slots_here, mats, width, hidden_size = slot_weights.shape
    return pl.pallas_call(
        experts_kernel,
        out_shape=jax.ShapeDtypeStruct((count, width), jnp.bfloat16),
        grid=(count // block,),
        in_specs=[
            pl.BlockSpec(memory_space=pltpu.SMEM),
            pl.BlockSpec((block, ext_width), lambda i: (i, 0)),
            pl.BlockSpec((slots_here, mats, width, hidden_size), lambda i: (0, 0, 0, 0)),
        ],
        out_specs=pl.BlockSpec((block, width), lambda i: (i, 0)),
        compiler_params=pltpu.CompilerParams(vmem_limit_bytes=40 * 1024 * 1024),
        cost_estimate=pl.CostEstimate(
            flops=2 * count * width * hidden_size * mats * slots_here,
            bytes_accessed=4 * count * width + 2 * slot_weights.size,
            transcendentals=count * hidden_size * slots_here,
        ),
    )(first_slot, tokens, slot_weights)


def turn_pairs(value, step):
    count = lax.axis_size("req")
    return lax.ppermute(value, "req", [(i, (i + 2 * step) % count) for i in range(count)])


def swap(value, mask):
    count = lax.axis_size("req")
    return lax.ppermute(value, "req", [(i, i ^ mask) for i in range(count)])


def together(*values):
    return lax.optimization_barrier(values)


def after(value, *events):
    return lax.optimization_barrier((value,) + events)[0]


def flip_pair(value):
    count = lax.axis_size("req")
    return lax.ppermute(value, "req", [(i, i ^ 1) for i in range(count)])


def flip_chip(value):
    count = lax.axis_size("exp")
    return lax.ppermute(value, "exp", [(i, i ^ 2) for i in range(count)])


def flip_core(value):
    count = lax.axis_size("exp")
    return lax.ppermute(value, "exp", [(i, i ^ 1) for i in range(count)])


def pick(value, index, axis):
    return lax.dynamic_index_in_dim(value, index, axis, keepdims=False)


def add(first, second):
    return (first.astype(jnp.float32) + second.astype(jnp.float32)).astype(jnp.bfloat16)


def fetch_cache(cache_keys, cache_values, need_blocks):
    me = lax.axis_index("req")
    pair_count = lax.axis_size("req") // 2
    cache_dev = cache_keys.shape[0]
    mine = jnp.stack([cache_keys, cache_values], axis=1)
    column = jnp.stack([mine] + [turn_pairs(mine, step) for step in range(1, pair_count)])
    column = column.reshape((pair_count * cache_dev,) + mine.shape[1:])

    def rows_for(wanted):
        holder = wanted // cache_dev
        back = (me // 2 - holder // 2) % pair_count
        index = back * cache_dev + wanted % cache_dev
        return jnp.stack([pick(column, index[k], 0) for k in range(cache_dev)])

    mine_wanted = pick(need_blocks, me, 0)
    from_pair = flip_pair(rows_for(pick(need_blocks, me ^ 1, 0)))
    here = ((mine_wanted // cache_dev) ^ me) & 1
    wanted = jnp.where((here == 0)[:, None, None, None], rows_for(mine_wanted), from_pair)
    return wanted


def sum_heads(partial_value):
    me = lax.axis_index("exp")
    rows, width = partial_value.shape
    grid = partial_value.reshape(2, 2, rows // 4, width)
    core, chip = me % 2, me // 2
    got = flip_core(pick(grid, 1 - core, 1).astype(jnp.bfloat16))
    level = pick(grid, core, 1) + got.astype(jnp.float32)
    got = flip_chip(pick(level, 1 - chip, 0).astype(jnp.bfloat16))
    return pick(level, chip, 0) + got.astype(jnp.float32)


def spread_tokens(pieces):
    width = pieces[0].shape[1]
    stacked = jnp.stack(pieces)
    cut = stacked.shape[1] // 2
    first, second = stacked[:, :cut], stacked[:, cut:]
    first = jnp.stack([first, flip_pair(first)])
    second = jnp.stack([second, flip_chip(second)])
    first_far, second_far = flip_chip(first), flip_pair(second)
    parts = [first, first_far, second, second_far]
    return jnp.concatenate([part.reshape(-1, width) for part in parts])


def gather_sums(total, piece_count):
    rows, width = total.shape
    cut = rows // (8 * piece_count)
    first, second = total.reshape(2, 2, 2, piece_count, cut, width)
    first = add(first[0], flip_chip(first[1]))
    second = add(second[0], flip_pair(second[1]))
    first = add(first[0], flip_pair(first[1]))
    second = add(second[0], flip_chip(second[1]))
    return jnp.concatenate([first, second], axis=1)


def mix(normed, codes, slot_weights, held, pick_first):
    pair_count = lax.axis_size("req") // 2
    first_slot = (lax.axis_index("req") * slot_weights.shape[0]).astype(jnp.int32).reshape(1)
    ext = jnp.concatenate([normed, codes], axis=1)
    pieces = [ext]
    for step in range(1, pair_count):
        source = ext
        if step == 2:
            source, *held[3:] = together(ext, *held[3:])
        pieces.append(turn_pairs(source, step))
    outgoing = pick_first(held)
    outgoing = after(outgoing, *pieces[1:])
    *pieces[2:], outgoing = together(*pieces[2:], outgoing)
    arrived = trade_columns(outgoing)
    total = None
    for begin in range(0, pair_count, 2):
        here = spread_tokens(pieces[begin : begin + 2])
        there = flip_core(here)
        back = flip_core(run_experts(first_slot, there, slot_weights, 256))
        if begin + 2 >= pair_count:
            here, arrived = together(here, arrived)
        mixed = run_experts(first_slot, here, slot_weights, 256)
        sums = gather_sums(add(mixed, back), 2)
        for offset in range(2):
            step = begin + offset
            part = sums[offset] if step == 0 else turn_pairs(sums[offset], -step)
            part = part.astype(jnp.float32)
            total = part if total is None else total + part
    return total, arrived


def spread_weights(slot_weights):
    me = lax.axis_index("req")
    half = lax.axis_size("req") // 2
    spot = me % half
    slots_here = slot_weights.shape[0]
    chunks = slot_weights.reshape(slots_here, half, -1, slot_weights.shape[-1])
    held = [pick(chunks, spot, 1)]
    for mask in range(1, half):
        held.append(swap(pick(chunks, spot ^ mask, 1), mask))
    return held


def pick_kernel(slots_here, index_ref, *refs):
    sources, out_ref = refs[:-1], refs[-1]
    holder = index_ref[pl.program_id(0)] // slots_here
    for k, source in enumerate(sources):

        @pl.when(holder == k)
        def _():
            out_ref[...] = source[...]


def take_chunks(held, index, begin, size):
    slots_here, _, width = held[0].shape
    count = index.shape[0]
    place = begin // size

    def block_of(k):
        def index_map(i, index):
            mine = index[i] // slots_here == k
            return (jnp.where(mine, index[i] % slots_here, 0), place, 0)

        return pl.BlockSpec((1, size, width), index_map)

    return pl.pallas_call(
        functools.partial(pick_kernel, slots_here),
        out_shape=jax.ShapeDtypeStruct((count, size, width), held[0].dtype),
        grid_spec=pltpu.PrefetchScalarGridSpec(
            num_scalar_prefetch=1,
            grid=(count,),
            in_specs=[block_of(k) for k in range(len(held))],
            out_specs=pl.BlockSpec((1, size, width), lambda i, index: (i, 0, 0)),
        ),
        compiler_params=pltpu.CompilerParams(vmem_limit_bytes=24 * 1024 * 1024),
        cost_estimate=pl.CostEstimate(
            flops=0, bytes_accessed=4 * count * size * width, transcendentals=0
        ),
    )(index, *held)


def trade_columns(outgoing):
    pair_count = lax.axis_size("req") // 2
    columns = [[2 * i + k for i in range(pair_count)] for k in range(2)]
    outgoing = outgoing.reshape((pair_count, 2) + outgoing.shape[1:])
    return lax.all_to_all(outgoing, "req", 0, 0, axis_index_groups=columns, tiled=True)


def chunk_index(source_slot, slots_here):
    half = lax.axis_size("req") // 2
    spots = source_slot // slots_here % half
    return ((lax.axis_index("req") % half) ^ spots) * slots_here + source_slot % slots_here


def collect_replicas(arrivals, source_slot, slots_here):
    me = lax.axis_index("req")
    half = lax.axis_size("req") // 2
    side = me % 2
    halves = source_slot // slots_here // half
    width = arrivals[0].shape[3]
    rows_all = sum(arrived.shape[2] for arrived in arrivals)
    result = jnp.zeros((half // 2, 2, rows_all, width), arrivals[0].dtype)
    first_row = 0
    for arrived in arrivals:
        size = arrived.shape[2]

        def wanted_by(receiver):
            begin = pick(halves, receiver, 0) * (half // 2)
            where = (begin, receiver % 2, 0, 0)
            return lax.dynamic_slice(arrived, where, (half // 2, 1, size, width))

        swapped = swap(wanted_by(me ^ 1), 1)
        for rows, column in ((wanted_by(me), side), (swapped, 1 - side)):
            result = lax.dynamic_update_slice(result, rows, (0, column, first_row, 0))
        first_row += size
    return result


def body(
    hidden_in,
    query_in,
    key_in,
    value_in,
    query_gain,
    key_gain,
    cache_keys,
    cache_values,
    cache_block,
    request_lengths,
    out_proj,
    norm_gain,
    expert_ids,
    gate_values,
    old_slots,
    new_replicas,
    slot_weights,
):
    req_count = lax.axis_size("req")
    exp_count = lax.axis_size("exp")
    group_idx = lax.axis_index("req")
    tok_grp, width_q = query_in.shape
    tok_dev, model_width = hidden_in.shape
    head_size = query_gain.shape[0]
    head_count = width_q // head_size
    cache_dev = cache_keys.shape[0]
    pre_len = cache_keys.shape[1]
    req_grp = request_lengths.shape[1]
    lengths = request_lengths[0]
    req_ends = jnp.cumsum(lengths)
    starts = req_ends - lengths
    places = jnp.arange(tok_grp, dtype=jnp.int32)
    member = (places[:, None] >= starts[None, :]) & (places[:, None] < req_ends[None, :])
    request_idx = jnp.arange(req_grp, dtype=jnp.int32)
    segment = jnp.sum(jnp.where(member, request_idx[None, :], 0), axis=1)
    offset = places - jnp.sum(jnp.where(member, starts[None, :], 0), axis=1)
    block_rows = cache_block.reshape(req_count, req_grp)
    my_blocks = lax.dynamic_index_in_dim(block_rows, group_idx, 0, keepdims=False)
    has_cache = my_blocks >= 0
    token_cached = jnp.sum(jnp.where(member & has_cache[None, :], 1, 0), axis=1) > 0
    position = (offset + jnp.where(token_cached, pre_len, 0)).astype(jnp.float32)
    need_blocks, need_requests = compact(block_rows, cache_dev)
    my_requests = lax.dynamic_index_in_dim(need_requests, group_idx, 0, keepdims=False)
    far_cache = fetch_cache(cache_keys, cache_values, need_blocks)
    far_keys, far_values = far_cache[:, 0], far_cache[:, 1]
    held = spread_weights(slot_weights)
    query_n = prepare(query_in.reshape(tok_grp, head_count, head_size), query_gain, position)
    key_n = prepare(key_in.reshape(tok_grp, head_count, head_size), key_gain, position)
    keyset = jnp.concatenate(
        [key_n, far_keys.reshape(cache_dev * pre_len, head_count, head_size)], axis=0
    )
    valueset = jnp.concatenate(
        [
            value_in.reshape(tok_grp, head_count, head_size),
            far_values.reshape(cache_dev * pre_len, head_count, head_size),
        ],
        axis=0,
    )
    key_request = jnp.concatenate([segment, jnp.repeat(my_requests, pre_len)])
    allowed = segment[:, None] == key_request[None, :]
    scores = jnp.einsum("qhd,khd->hqk", query_n, keyset, preferred_element_type=jnp.float32) * (
        1.0 / math.sqrt(head_size)
    )
    scores = jnp.where(allowed[None], scores, -1e30)
    peak = jnp.max(scores, axis=-1, keepdims=True)
    expos = jnp.exp(scores - peak)
    weights = (expos / jnp.sum(expos, axis=-1, keepdims=True)).astype(jnp.bfloat16)
    attended = jnp.einsum("hqk,khd->qhd", weights, valueset, preferred_element_type=jnp.float32)
    attended = attended.astype(jnp.bfloat16).reshape(tok_grp, width_q)
    attended, *held[1:3] = together(attended, *held[1:3])
    attn_out = sum_heads(jnp.dot(attended, out_proj, preferred_element_type=jnp.float32))
    residual = hidden_in.astype(jnp.float32) + attn_out
    normed = (
        residual
        * lax.rsqrt(jnp.mean(residual * residual, axis=-1, keepdims=True) + 1e-06)
        * norm_gain
    ).astype(jnp.bfloat16)
    slot_total = old_slots.shape[0]
    slot_range = jnp.arange(slot_total, dtype=jnp.int32)
    slot_of = jnp.sum(
        jnp.where(old_slots[None, :] == slot_range[:, None], slot_range[None, :], 0), axis=1
    )
    dense_gates = jnp.sum(
        jnp.where(expert_ids[:, :, None] == old_slots[None, None, :], gate_values[:, :, None], 0.0),
        axis=1,
    )
    high_part = dense_gates.astype(jnp.bfloat16)
    low_part = (dense_gates - high_part.astype(jnp.float32)).astype(jnp.bfloat16)
    lanes = max(64, slot_total)
    gap = ((0, 0), (0, lanes - slot_total))
    codes = jnp.concatenate([jnp.pad(high_part, gap), jnp.pad(low_part, gap)], axis=1)
    replica_onehot = new_replicas[:, None] == slot_range[None, :]
    source_slot = jnp.sum(jnp.where(replica_onehot, slot_of[None, :], 0), axis=1)
    slots_here = slot_weights.shape[0]
    index = chunk_index(source_slot, slots_here)
    size = held[0].shape[1] // 2
    mixture, first = mix(
        normed, codes, slot_weights, held, lambda held: take_chunks(held, index, 0, size)
    )
    layer_out = (residual + mixture).astype(jnp.bfloat16)
    second = trade_columns(after(take_chunks(held, index, size, size), first))
    replica_weights = collect_replicas((first, second), source_slot, slots_here)
    return (layer_out, replica_weights.reshape((1,) + slot_weights.shape[1:]))


def solution(mesh):
    in_specs = (
        P(("req", "exp"), None),
        P("req", "exp"),
        P("req", "exp"),
        P("req", "exp"),
        P(),
        P(),
        P("req", None, "exp"),
        P("req", None, "exp"),
        P(),
        P("req", None),
        P("exp", None),
        P(),
        P(("req", "exp"), None),
        P(("req", "exp"), None),
        P(),
        P(),
        P("req", None, None, "exp"),
    )
    out_specs = (P(("req", "exp"), None), P("req", None, None, "exp"))
    return jax.shard_map(body, mesh=mesh, in_specs=in_specs, out_specs=out_specs, check_vma=False)
```

profile of v0, /device:TPU:0, one launch (start us, length us, event | category | flops | bytes accessed | tf_op | source)
XLA Modules:
  0.0 296.6 jit_solution(8800471800587648210)
XLA Ops:
  0.6 1.7 fusion.69
  2.4 4.0 %collective-permute-start.1 = (bf16[2,2,32,512]{3,2,1,0:T(8,128)(2,1)}, bf16[2,2,32,512]{3,2,1,0:T(8,128)(2,1)}, u32[]{:S(2)}, u32[]{:S(2)}) collective-permute-start(bf16[2,2,32,512]{3,2,1,0:T(8,128)(2,1)} %get-tuple-element.80), channel_id=1, source_target_pairs={{0,16},{4,20},{8,24},{12,28},{16,0},{20,4},{24,8},{28,12},{1,17},{... | collective-permute-start | bytes 393224 | tf_op jit(solution)/shard_map/ppermute | solution.py:94
  8.0 2.2 collective-permute-start.2
  10.2 5.7 %dynamic-slice_bitcast_fusion = (bf16[2,1536,256]{2,1,0:T(8,128)(2,1)}, bf16[2,1536,256]{2,1,0:T(8,128)(2,1)}, bf16[2,1536,256]{2,1,0:T(8,128)(2,1)}, bf16[2,1536,256]{2,1,0:T(8,128)(2,1)}) fusion(bf16[2,4,1536,256]{3,2,1,0:T(8,128)(2,1)} %bitcast.154, s32[]{:T(128)S(6)} %select_n.262, s32[]{:T(128)S(6)} %select_n.256, s32[]{:T(128)S(6)} %select_n.248, ...), kind=kLoop, calls=%fused_computation.6 | loop fusion | bytes 12582928 | tf_op jit(solution)/shard_map/jit(dynamic_index_in_dim)/squeeze | solution.py:126
  16.0 1.6 collective-permute-start.4
  34.6 19.7 %collective-permute-done.3 = bf16[2,2,32,512]{3,2,1,0:T(8,128)(2,1)S(1)} collective-permute-done((bf16[2,2,32,512]{3,2,1,0:T(8,128)(2,1)S(1)}, bf16[2,2,32,512]{3,2,1,0:T(8,128)(2,1)S(1)}, u32[]{:S(2)}, u32[]{:S(2)}) %collective-permute-start.3) | collective-permute-done | bytes 131104 | tf_op jit(solution)/shard_map/ppermute | solution.py:112
  54.5 2.8 fusion.78
  57.3 1.7 convolution_convert_fusion
  61.3 2.7 collective-permute-start.20
  68.5 6.3 %collective-permute-done.7 = bf16[64,2048]{1,0:T(8,128)(2,1)S(1)} collective-permute-done((bf16[64,2048]{1,0:T(8,128)(2,1)S(1)}, bf16[64,2048]{1,0:T(8,128)(2,1)S(1)}, u32[]{:S(2)}, u32[]{:S(2)}) %collective-permute-start.7) | collective-permute-done | bytes 262176 | tf_op jit(solution)/shard_map/ppermute | solution.py:117
  77.2 3.2 %collective-permute-start.22 = (bf16[64,2176]{1,0:T(8,128)(2,1)S(1)}, bf16[64,2176]{1,0:T(8,128)(2,1)S(1)}, u32[]{:S(2)}, u32[]{:S(2)}) collective-permute-start(bf16[64,2176]{1,0:T(8,128)(2,1)S(1)} %concatenate.37), channel_id=1, source_target_pairs={{0,24},{4,28},{8,0},{12,4},{16,8},{20,12},{24,16},{28,20},{1,25},{... | collective-permute-start | bytes 835592 | tf_op jit(solution)/shard_map/ppermute | solution.py:94
  80.3 28.4 %collective-permute-done.20.refs_3_ = bf16[2,1536,256]{2,1,0:T(8,128)(2,1)} collective-permute-done((bf16[2,1536,256]{2,1,0:T(8,128)(2,1)}, bf16[2,1536,256]{2,1,0:T(8,128)(2,1)}, u32[]{:S(2)}, u32[]{:S(2)}) %collective-permute-start.20) | collective-permute-done | bytes 1572896 | tf_op jit(solution)/shard_map/ppermute | solution.py:99
  108.7 4.7 %shard_map.178 = bf16[8,768,256]{2,1,0:T(8,128)(2,1)S(1)} custom-call(s32[8]{0:T(128)S(1)} %fusion.50.index_ref, bf16[2,1536,256]{2,1,0:T(8,128)(2,1)S(1)} %copy-done.2, bf16[2,1536,256]{2,1,0:T(8,128)(2,1)} %collective-permute-done.4.refs_1_, bf16[2,1536,256]{2,1,0:T(8,128)(2,1)} %collective-permute-done.5.refs_2_, ...), custom_call_target="tpu_custom_call" | custom-call | bytes 6291456 | tf_op jit(solution)/shard_map/pallas_call | solution.py:253
  113.5 2.4 collective-permute-start.9
  117.3 2.8 collective-permute-done.21
  121.8 3.6 %collective-permute-done.11 = bf16[2,32,2176]{2,1,0:T(8,128)(2,1)S(1)} collective-permute-done((bf16[2,32,2176]{2,1,0:T(8,128)(2,1)S(1)}, bf16[2,32,2176]{2,1,0:T(8,128)(2,1)S(1)}, u32[]{:S(2)}, u32[]{:S(2)}) %collective-permute-start.11) | collective-permute-done | bytes 278560 | tf_op jit(solution)/shard_map/ppermute | solution.py:117
  127.9 4.9 %all-to-all-start = ((bf16[4,2,768,256]{3,2,1,0:T(8,128)(2,1)}), bf16[4,2,768,256]{3,2,1,0:T(8,128)(2,1)}, u32[]{:S(2)}, u32[]{:S(2)}) async-start(bf16[4,2,768,256]{3,2,1,0:T(8,128)(2,1)} %bitcast.152), calls=%async_computation | async-start | bytes 6291456 | tf_op jit(solution)/shard_map/all_to_all | solution.py:273
  132.8 2.0 collective-permute-start.23
  136.0 5.2 %collective-permute-done.12 = bf16[2,2,32,2176]{3,2,1,0:T(8,128)(2,1)} collective-permute-done((bf16[2,2,32,2176]{3,2,1,0:T(8,128)(2,1)S(1)}, bf16[2,2,32,2176]{3,2,1,0:T(8,128)(2,1)}, u32[]{:S(2)}, u32[]{:S(2)}) %collective-permute-start.12) | collective-permute-done | bytes 557088 | tf_op jit(solution)/shard_map/ppermute | solution.py:112
  141.1 3.0 pad_maximum_fusion.tok_ref
  145.9 4.3 %collective-permute-done.26 = bf16[2,2,32,2176]{3,2,1,0:T(8,128)(2,1)S(1)} collective-permute-done((bf16[2,2,32,2176]{3,2,1,0:T(8,128)(2,1)S(1)}, bf16[2,2,32,2176]{3,2,1,0:T(8,128)(2,1)S(1)}, u32[]{:S(2)}, u32[]{:S(2)}) %collective-permute-start.26) | collective-permute-done | bytes 557088 | tf_op jit(solution)/shard_map/ppermute | solution.py:112
  150.2 9.0 %collective-permute-done.24 = bf16[2,2,32,2176]{3,2,1,0:T(8,128)(2,1)S(1)} collective-permute-done((bf16[2,2,32,2176]{3,2,1,0:T(8,128)(2,1)S(1)}, bf16[2,2,32,2176]{3,2,1,0:T(8,128)(2,1)S(1)}, u32[]{:S(2)}, u32[]{:S(2)}) %collective-permute-start.24) | collective-permute-done | bytes 557088 | tf_op jit(solution)/shard_map/ppermute | solution.py:117
  160.8 2.8 copy-done.5
  163.6 6.1 %shard_map.177 = bf16[512,2048]{1,0:T(8,128)(2,1)} custom-call(s32[1]{0:T(128)} %bitcast.35.first_slot_ref, bf16[512,2176]{1,0:T(8,128)(2,1)} %collective-permute-done.13.tok_ref, bf16[2,3,2048,256]{3,2,1,0:T(8,128)(2,1)S(1)} %copy-done.5), custom_call_target="tpu_custom_call" | custom-call | flops 3221225472 | bytes 10485760 | tf_op jit(solution)/shard_map/pallas_call | solution.py:73
  170.1 6.0 %shard_map.180 = bf16[512,2048]{1,0:T(8,128)(2,1)} custom-call(s32[1]{0:T(128)} %bitcast.35.first_slot_ref, bf16[512,2176]{1,0:T(8,128)(2,1)} %collective-permute-done.27.tok_ref, bf16[2,3,2048,256]{3,2,1,0:T(8,128)(2,1)S(1)} %copy-done.5), custom_call_target="tpu_custom_call" | custom-call | flops 3221225472 | bytes 10485760 | tf_op jit(solution)/shard_map/pallas_call | solution.py:73
  178.1 4.7 %shard_map.181 = bf16[8,768,256]{2,1,0:T(8,128)(2,1)S(1)} custom-call(s32[8]{0:T(128)S(1)} %fusion.50.index_ref, bf16[2,1536,256]{2,1,0:T(8,128)(2,1)S(1)} %copy-done.2, bf16[2,1536,256]{2,1,0:T(8,128)(2,1)} %collective-permute-done.4.refs_1_, bf16[2,1536,256]{2,1,0:T(8,128)(2,1)} %collective-permute-done.5.refs_2_, ...), custom_call_target="tpu_custom_call" | custom-call | bytes 6291456 | tf_op jit(solution)/shard_map/pallas_call | solution.py:253
  182.8 1.6 copy-done.4
  184.4 2.8 copy-done.6
  187.2 5.1 %shard_map.176 = bf16[512,2048]{1,0:T(8,128)(2,1)S(1)} custom-call(s32[1]{0:T(128)} %bitcast.35.first_slot_ref, bf16[512,2176]{1,0:T(8,128)(2,1)} %pad_maximum_fusion.tok_ref, bf16[2,3,2048,256]{3,2,1,0:T(8,128)(2,1)S(1)} %copy-done.6), custom_call_target="tpu_custom_call" | custom-call | flops 3221225472 | bytes 10485760 | tf_op jit(solution)/shard_map/pallas_call | solution.py:73
  192.3 3.3 %all-to-all-done = bf16[4,2,768,256]{3,2,1,0:T(8,128)(2,1)} async-done(((bf16[4,2,768,256]{3,2,1,0:T(8,128)(2,1)}), bf16[4,2,768,256]{3,2,1,0:T(8,128)(2,1)}, u32[]{:S(2)}, u32[]{:S(2)}) %all-to-all-start) | async-done | bytes 3145760 | tf_op jit(solution)/shard_map/all_to_all | solution.py:273
  195.6 4.7 %all-to-all-start.1 = ((bf16[4,2,768,256]{3,2,1,0:T(8,128)(2,1)}), bf16[4,2,768,256]{3,2,1,0:T(8,128)(2,1)}, u32[]{:S(2)}, u32[]{:S(2)}) async-start(bf16[4,2,768,256]{3,2,1,0:T(8,128)(2,1)} %bitcast.153), calls=%async_computation.1 | async-start | bytes 6291456 | tf_op jit(solution)/shard_map/all_to_all | solution.py:273
  200.3 1.9 broadcast_in_dim.162
  202.1 2.4 constant_dynamic-slice_fusion.1
  206.1 2.8 copy-done.7
  208.9 5.2 %shard_map.179 = bf16[512,2048]{1,0:T(8,128)(2,1)S(1)} custom-call(s32[1]{0:T(128)} %bitcast.35.first_slot_ref, bf16[512,2176]{1,0:T(8,128)(2,1)} %pad_maximum_fusion.1.tok_ref, bf16[2,3,2048,256]{3,2,1,0:T(8,128)(2,1)S(1)} %copy-done.7), custom_call_target="tpu_custom_call" | custom-call | flops 3221225472 | bytes 10485760 | tf_op jit(solution)/shard_map/pallas_call | solution.py:73
  214.1 2.4 add_convert_fusion.1
  218.7 2.4 add_convert_fusion
  221.3 1.6 collective-permute-start.31
  225.9 10.3 %collective-permute-done.17 = bf16[2,2,32,2048]{3,2,1,0:T(8,128)(2,1)S(1)} collective-permute-done((bf16[2,2,32,2048]{3,2,1,0:T(8,128)(2,1)S(1)}, bf16[2,2,32,2048]{3,2,1,0:T(8,128)(2,1)S(1)}, u32[]{:S(2)}, u32[]{:S(2)}) %collective-permute-start.17) | collective-permute-done | bytes 524320 | tf_op jit(solution)/shard_map/ppermute | solution.py:112
  238.0 1.7 collective-permute-start.16
  239.7 7.8 %collective-permute-done.31 = bf16[2,2,32,2048]{3,2,1,0:T(8,128)(2,1)S(1)} collective-permute-done((bf16[2,2,32,2048]{3,2,1,0:T(8,128)(2,1)S(1)}, bf16[2,2,32,2048]{3,2,1,0:T(8,128)(2,1)S(1)}, u32[]{:S(2)}, u32[]{:S(2)}) %collective-permute-start.31) | collective-permute-done | bytes 524320 | tf_op jit(solution)/shard_map/ppermute | solution.py:112
  249.2 1.7 collective-permute-start.30
  253.3 3.9 %collective-permute-start.19 = (bf16[64,2048]{1,0:T(8,128)(2,1)}, bf16[64,2048]{1,0:T(8,128)(2,1)}, u32[]{:S(2)}, u32[]{:S(2)}) collective-permute-start(bf16[64,2048]{1,0:T(8,128)(2,1)} %fusion.34), channel_id=1, source_target_pairs={{0,24},{4,28},{8,0},{12,4},{16,8},{20,12},{24,16},{28,20},{1,25},{... | collective-permute-start | bytes 786440 | tf_op jit(solution)/shard_map/ppermute | solution.py:94
  258.0 13.7 %all-to-all-done.1 = bf16[4,2,768,256]{3,2,1,0:T(8,128)(2,1)} async-done(((bf16[4,2,768,256]{3,2,1,0:T(8,128)(2,1)}), bf16[4,2,768,256]{3,2,1,0:T(8,128)(2,1)}, u32[]{:S(2)}, u32[]{:S(2)}) %all-to-all-start.1) | async-done | bytes 3145760 | tf_op jit(solution)/shard_map/all_to_all | solution.py:273
  271.8 2.4 constant_dynamic-slice_fusion
  275.4 6.5 %collective-permute-start.34 = (bf16[64,2048]{1,0:T(8,128)(2,1)S(1)}, bf16[64,2048]{1,0:T(8,128)(2,1)S(1)}, u32[]{:S(2)}, u32[]{:S(2)}) collective-permute-start(bf16[64,2048]{1,0:T(8,128)(2,1)S(1)} %get-tuple-element.70), channel_id=1, source_target_pairs={{0,8},{4,12},{8,16},{12,20},{16,24},{20,28},{24,0},{28,4},{1,9},{5... | collective-permute-start | bytes 786440 | tf_op jit(solution)/shard_map/ppermute | solution.py:94
  282.0 11.9 %collective-permute-done.33 = bf16[64,2048]{1,0:T(8,128)(2,1)S(1)} collective-permute-done((bf16[64,2048]{1,0:T(8,128)(2,1)S(1)}, bf16[64,2048]{1,0:T(8,128)(2,1)S(1)}, u32[]{:S(2)}, u32[]{:S(2)}) %collective-permute-start.33) | collective-permute-done | bytes 262176 | tf_op jit(solution)/shard_map/ppermute | solution.py:94
  293.9 1.8 fusion.14
  (188 shorter events, 47.7 us)
Async XLA Ops:
  0.6 58.4 %copy-start = (bf16[512,2048]{1,0:T(8,128)(2,1)S(1)}, bf16[512,2048]{1,0:T(8,128)(2,1)}, u32[]{:S(2)}) copy-start(bf16[512,2048]{1,0:T(8,128)(2,1)} %param.27) | copy-start | bytes 6291460
  2.4 29.7 %collective-permute-start.1 = (bf16[2,2,32,512]{3,2,1,0:T(8,128)(2,1)}, bf16[2,2,32,512]{3,2,1,0:T(8,128)(2,1)}, u32[]{:S(2)}, u32[]{:S(2)}) collective-permute-start(bf16[2,2,32,512]{3,2,1,0:T(8,128)(2,1)} %get-tuple-element.80), channel_id=1, source_target_pairs={{0,16},{4,20},{8,24},{12,28},{16,0},{20,4},{24,8},{28,12},{1,17},{... | collective-permute-start | bytes 393224 | tf_op jit(solution)/shard_map/ppermute | solution.py:94
  6.4 25.7 %collective-permute-start = (bf16[2,2,32,512]{3,2,1,0:T(8,128)(2,1)}, bf16[2,2,32,512]{3,2,1,0:T(8,128)(2,1)}, u32[]{:S(2)}, u32[]{:S(2)}) collective-permute-start(bf16[2,2,32,512]{3,2,1,0:T(8,128)(2,1)} %get-tuple-element.80), channel_id=1, source_target_pairs={{0,8},{4,12},{8,16},{12,20},{16,24},{20,28},{24,0},{28,4},{1,9},{5... | collective-permute-start | bytes 393224 | tf_op jit(solution)/shard_map/ppermute | solution.py:94
  8.0 24.2 %collective-permute-start.2 = (bf16[2,2,32,512]{3,2,1,0:T(8,128)(2,1)}, bf16[2,2,32,512]{3,2,1,0:T(8,128)(2,1)}, u32[]{:S(2)}, u32[]{:S(2)}) collective-permute-start(bf16[2,2,32,512]{3,2,1,0:T(8,128)(2,1)} %get-tuple-element.80), channel_id=1, source_target_pairs={{0,24},{4,28},{8,0},{12,4},{16,8},{20,12},{24,16},{28,20},{1,25},{... | collective-permute-start | bytes 393224 | tf_op jit(solution)/shard_map/ppermute | solution.py:94
  10.2 8.9 %copy-start.13 = (bf16[256,512]{1,0:T(8,128)(2,1)S(1)}, bf16[256,512]{1,0:T(8,128)(2,1)}, u32[]{:S(2)}) copy-start(bf16[256,512]{1,0:T(8,128)(2,1)} %param.18) | copy-start | bytes 786436
  10.2 9.1 %copy-start.14 = (bf16[256,512]{1,0:T(8,128)(2,1)S(1)}, bf16[256,512]{1,0:T(8,128)(2,1)}, u32[]{:S(2)}) copy-start(bf16[256,512]{1,0:T(8,128)(2,1)} %param.19) | copy-start | bytes 786436
  15.9 43.1 %collective-permute-start.5 = (bf16[2,1536,256]{2,1,0:T(8,128)(2,1)}, bf16[2,1536,256]{2,1,0:T(8,128)(2,1)}, u32[]{:S(2)}, u32[]{:S(2)}) collective-permute-start(bf16[2,1536,256]{2,1,0:T(8,128)(2,1)} %get-tuple-element.47), channel_id=1, source_target_pairs={{0,8},{4,12},{8,0},{12,4},{16,24},{20,28},{24,16},{28,20},{1,9},{5... | collective-permute-start | bytes 4718600 | tf_op jit(solution)/shard_map/ppermute | solution.py:99
  16.0 43.1 %collective-permute-start.4 = (bf16[2,1536,256]{2,1,0:T(8,128)(2,1)}, bf16[2,1536,256]{2,1,0:T(8,128)(2,1)}, u32[]{:S(2)}, u32[]{:S(2)}) collective-permute-start(bf16[2,1536,256]{2,1,0:T(8,128)(2,1)} %get-tuple-element.48), channel_id=1, source_target_pairs={{0,4},{4,0},{8,12},{12,8},{16,20},{20,16},{24,28},{28,24},{1,5},{5... | collective-permute-start | bytes 4718600 | tf_op jit(solution)/shard_map/ppermute | solution.py:99
  33.3 21.0 %collective-permute-start.3 = (bf16[2,2,32,512]{3,2,1,0:T(8,128)(2,1)S(1)}, bf16[2,2,32,512]{3,2,1,0:T(8,128)(2,1)S(1)}, u32[]{:S(2)}, u32[]{:S(2)}) collective-permute-start(bf16[2,2,32,512]{3,2,1,0:T(8,128)(2,1)S(1)} %pad_maximum_fusion.12), channel_id=1, source_target_pairs={{0,4},{4,0},{8,12},{12,8},{16,20},{20,16},{24,28},{28,24},{1,5},{5... | collective-permute-start | bytes 393224 | tf_op jit(solution)/shard_map/ppermute | solution.py:112
  59.8 8.5 %copy-start.25 = (s32[8]{0:T(128)S(1)}, s32[8]{0:T(128)}, u32[]{:S(2)}) copy-start(s32[8]{0:T(128)} %param.32) | copy-start | bytes 100
  59.8 15.1 %copy-start.16 = (bf16[64,2048]{1,0:T(8,128)(2,1)S(1)}, bf16[64,2048]{1,0:T(8,128)(2,1)}, u32[]{:S(2)}) copy-start(bf16[64,2048]{1,0:T(8,128)(2,1)} %param.17) | copy-start | bytes 786436
  61.2 2.9 collective-permute-start.6
  61.3 47.4 %collective-permute-start.20 = (bf16[2,1536,256]{2,1,0:T(8,128)(2,1)}, bf16[2,1536,256]{2,1,0:T(8,128)(2,1)}, u32[]{:S(2)}, u32[]{:S(2)}) collective-permute-start(bf16[2,1536,256]{2,1,0:T(8,128)(2,1)} %get-tuple-element.46), channel_id=1, source_target_pairs={{0,12},{4,8},{8,4},{12,0},{16,28},{20,24},{24,20},{28,16},{1,13},{... | collective-permute-start | bytes 4718600 | tf_op jit(solution)/shard_map/ppermute | solution.py:99
  64.0 12.1 %copy-start.17 = (f32[2048]{0:T(1024)S(1)}, f32[2048]{0:T(1024)}, u32[]{:S(2)}) copy-start(f32[2048]{0:T(1024)} %param.28) | copy-start | bytes 24580
  66.4 42.3 %copy-start.2 = (bf16[2,1536,256]{2,1,0:T(8,128)(2,1)S(1)}, bf16[2,1536,256]{2,1,0:T(8,128)(2,1)}, u32[]{:S(2)}) copy-start(bf16[2,1536,256]{2,1,0:T(8,128)(2,1)} %get-tuple-element.45.refs_0_) | copy-start | bytes 4718596
  66.4 8.4 %collective-permute-start.7 = (bf16[64,2048]{1,0:T(8,128)(2,1)S(1)}, bf16[64,2048]{1,0:T(8,128)(2,1)S(1)}, u32[]{:S(2)}, u32[]{:S(2)}) collective-permute-start(bf16[64,2048]{1,0:T(8,128)(2,1)S(1)} %fusion.28), channel_id=1, source_target_pairs={{0,2},{1,3},{2,0},{3,1},{4,6},{5,7},{6,4},{7,5},{8,10},{9,11},{10,... | collective-permute-start | bytes 786440 | tf_op jit(solution)/shard_map/ppermute | solution.py:117
  76.4 37.0 %collective-permute-start.8 = (bf16[64,2176]{1,0:T(8,128)(2,1)S(1)}, bf16[64,2176]{1,0:T(8,128)(2,1)S(1)}, u32[]{:S(2)}, u32[]{:S(2)}) collective-permute-start(bf16[64,2176]{1,0:T(8,128)(2,1)S(1)} %concatenate.37), channel_id=1, source_target_pairs={{0,8},{4,12},{8,16},{12,20},{16,24},{20,28},{24,0},{28,4},{1,9},{5... | collective-permute-start | bytes 835592 | tf_op jit(solution)/shard_map/ppermute | solution.py:94
  77.2 43.0 %collective-permute-start.22 = (bf16[64,2176]{1,0:T(8,128)(2,1)S(1)}, bf16[64,2176]{1,0:T(8,128)(2,1)S(1)}, u32[]{:S(2)}, u32[]{:S(2)}) collective-permute-start(bf16[64,2176]{1,0:T(8,128)(2,1)S(1)} %concatenate.37), channel_id=1, source_target_pairs={{0,24},{4,28},{8,0},{12,4},{16,8},{20,12},{24,16},{28,20},{1,25},{... | collective-permute-start | bytes 835592 | tf_op jit(solution)/shard_map/ppermute | solution.py:94
  108.7 11.5 %collective-permute-start.21 = (bf16[64,2176]{1,0:T(8,128)(2,1)S(1)}, bf16[64,2176]{1,0:T(8,128)(2,1)S(1)}, u32[]{:S(2)}, u32[]{:S(2)}) collective-permute-start(bf16[64,2176]{1,0:T(8,128)(2,1)S(1)} %concatenate.37), channel_id=1, source_target_pairs={{0,16},{4,20},{8,24},{12,28},{16,0},{20,4},{24,8},{28,12},{1,17},{... | collective-permute-start | bytes 835592 | tf_op jit(solution)/shard_map/ppermute | solution.py:94
  113.4 13.0 %copy-start.3 = (bf16[8,768,256]{2,1,0:T(8,128)(2,1)}, bf16[8,768,256]{2,1,0:T(8,128)(2,1)S(1)}, u32[]{:S(2)}) copy-start(bf16[8,768,256]{2,1,0:T(8,128)(2,1)S(1)} %shard_map.178) | copy-start | bytes 9437188
  113.5 12.1 %collective-permute-start.9 = (bf16[2,32,2176]{2,1,0:T(8,128)(2,1)S(1)}, bf16[2,32,2176]{2,1,0:T(8,128)(2,1)S(1)}, u32[]{:S(2)}, u32[]{:S(2)}) collective-permute-start(bf16[2,32,2176]{2,1,0:T(8,128)(2,1)S(1)} %get-tuple-element.65), channel_id=1, source_target_pairs={{0,4},{4,0},{8,12},{12,8},{16,20},{20,16},{24,28},{28,24},{1,5},{5... | collective-permute-start | bytes 835592 | tf_op jit(solution)/shard_map/ppermute | solution.py:112
  115.8 9.5 %collective-permute-start.11 = (bf16[2,32,2176]{2,1,0:T(8,128)(2,1)S(1)}, bf16[2,32,2176]{2,1,0:T(8,128)(2,1)S(1)}, u32[]{:S(2)}, u32[]{:S(2)}) collective-permute-start(bf16[2,32,2176]{2,1,0:T(8,128)(2,1)S(1)} %get-tuple-element.66), channel_id=1, source_target_pairs={{0,2},{1,3},{2,0},{3,1},{4,6},{5,7},{6,4},{7,5},{8,10},{9,11},{10,... | collective-permute-start | bytes 835592 | tf_op jit(solution)/shard_map/ppermute | solution.py:117
  120.2 14.6 %collective-permute-start.25 = (bf16[2,32,2176]{2,1,0:T(8,128)(2,1)S(1)}, bf16[2,32,2176]{2,1,0:T(8,128)(2,1)}, u32[]{:S(2)}, u32[]{:S(2)}) collective-permute-start(bf16[2,32,2176]{2,1,0:T(8,128)(2,1)S(1)} %get-tuple-element.68), channel_id=1, source_target_pairs={{0,2},{1,3},{2,0},{3,1},{4,6},{5,7},{6,4},{7,5},{8,10},{9,11},{10,... | collective-permute-start | bytes 835592 | tf_op jit(solution)/shard_map/ppermute | solution.py:117
  125.4 15.7 %collective-permute-start.12 = (bf16[2,2,32,2176]{3,2,1,0:T(8,128)(2,1)S(1)}, bf16[2,2,32,2176]{3,2,1,0:T(8,128)(2,1)}, u32[]{:S(2)}, u32[]{:S(2)}) collective-permute-start(bf16[2,2,32,2176]{3,2,1,0:T(8,128)(2,1)S(1)} %pad_maximum_fusion.3), channel_id=1, source_target_pairs={{0,4},{4,0},{8,12},{12,8},{16,20},{20,16},{24,28},{28,24},{1,5},{5... | collective-permute-start | bytes 1671176 | tf_op jit(solution)/shard_map/ppermute | solution.py:112
  126.4 14.7 %collective-permute-start.10 = (bf16[2,2,32,2176]{3,2,1,0:T(8,128)(2,1)}, bf16[2,2,32,2176]{3,2,1,0:T(8,128)(2,1)}, u32[]{:S(2)}, u32[]{:S(2)}) collective-permute-start(bf16[2,2,32,2176]{3,2,1,0:T(8,128)(2,1)} %pad_maximum_fusion.2), channel_id=1, source_target_pairs={{0,2},{1,3},{2,0},{3,1},{4,6},{5,7},{6,4},{7,5},{8,10},{9,11},{10,... | collective-permute-start | bytes 1671176 | tf_op jit(solution)/shard_map/ppermute | solution.py:117
  127.9 67.7 %all-to-all-start = ((bf16[4,2,768,256]{3,2,1,0:T(8,128)(2,1)}), bf16[4,2,768,256]{3,2,1,0:T(8,128)(2,1)}, u32[]{:S(2)}, u32[]{:S(2)}) async-start(bf16[4,2,768,256]{3,2,1,0:T(8,128)(2,1)} %bitcast.152), calls=%async_computation | async-start | bytes 6291456 | tf_op jit(solution)/shard_map/all_to_all | solution.py:273
  132.8 11.5 %collective-permute-start.23 = (bf16[2,32,2176]{2,1,0:T(8,128)(2,1)S(1)}, bf16[2,32,2176]{2,1,0:T(8,128)(2,1)S(1)}, u32[]{:S(2)}, u32[]{:S(2)}) collective-permute-start(bf16[2,32,2176]{2,1,0:T(8,128)(2,1)S(1)} %get-tuple-element.67), channel_id=1, source_target_pairs={{0,4},{4,0},{8,12},{12,8},{16,20},{20,16},{24,28},{28,24},{1,5},{5... | collective-permute-start | bytes 835592 | tf_op jit(solution)/shard_map/ppermute | solution.py:112
  135.8 14.5 %collective-permute-start.26 = (bf16[2,2,32,2176]{3,2,1,0:T(8,128)(2,1)S(1)}, bf16[2,2,32,2176]{3,2,1,0:T(8,128)(2,1)S(1)}, u32[]{:S(2)}, u32[]{:S(2)}) collective-permute-start(bf16[2,2,32,2176]{3,2,1,0:T(8,128)(2,1)S(1)} %pad_maximum_fusion.5), channel_id=1, source_target_pairs={{0,4},{4,0},{8,12},{12,8},{16,20},{20,16},{24,28},{28,24},{1,5},{5... | collective-permute-start | bytes 1671176 | tf_op jit(solution)/shard_map/ppermute | solution.py:112
  144.1 16.7 %collective-permute-start.13 = (bf16[512,2176]{1,0:T(8,128)(2,1)}, bf16[512,2176]{1,0:T(8,128)(2,1)}, u32[]{:S(2)}, u32[]{:S(2)}) collective-permute-start(bf16[512,2176]{1,0:T(8,128)(2,1)} %pad_maximum_fusion.tok_ref), channel_id=1, source_target_pairs={{0,1},{1,0},{2,3},{3,2},{4,5},{5,4},{6,7},{7,6},{8,9},{9,8},{10,11... | collective-permute-start | bytes 6684680 | tf_op jit(solution)/shard_map/ppermute | solution.py:122
  144.3 14.9 %collective-permute-start.24 = (bf16[2,2,32,2176]{3,2,1,0:T(8,128)(2,1)S(1)}, bf16[2,2,32,2176]{3,2,1,0:T(8,128)(2,1)S(1)}, u32[]{:S(2)}, u32[]{:S(2)}) collective-permute-start(bf16[2,2,32,2176]{3,2,1,0:T(8,128)(2,1)S(1)} %pad_maximum_fusion.4), channel_id=1, source_target_pairs={{0,2},{1,3},{2,0},{3,1},{4,6},{5,7},{6,4},{7,5},{8,10},{9,11},{10,... | collective-permute-start | bytes 1671176 | tf_op jit(solution)/shard_map/ppermute | solution.py:117
  160.8 9.4 %collective-permute-start.27 = (bf16[512,2176]{1,0:T(8,128)(2,1)}, bf16[512,2176]{1,0:T(8,128)(2,1)}, u32[]{:S(2)}, u32[]{:S(2)}) collective-permute-start(bf16[512,2176]{1,0:T(8,128)(2,1)} %pad_maximum_fusion.1.tok_ref), channel_id=1, source_target_pairs={{0,1},{1,0},{2,3},{3,2},{4,5},{5,4},{6,7},{7,6},{8,9},{9,8},{10,11... | collective-permute-start | bytes 6684680 | tf_op jit(solution)/shard_map/ppermute | solution.py:122
  169.6 44.5 %collective-permute-start.14 = (bf16[512,2048]{1,0:T(8,128)(2,1)}, bf16[512,2048]{1,0:T(8,128)(2,1)}, u32[]{:S(2)}, u32[]{:S(2)}) collective-permute-start(bf16[512,2048]{1,0:T(8,128)(2,1)} %shard_map.177), channel_id=1, source_target_pairs={{0,1},{1,0},{2,3},{3,2},{4,5},{5,4},{6,7},{7,6},{8,9},{9,8},{10,11... | collective-permute-start | bytes 6291464 | tf_op jit(solution)/shard_map/ppermute | solution.py:122
  176.2 42.5 %collective-permute-start.28 = (bf16[512,2048]{1,0:T(8,128)(2,1)}, bf16[512,2048]{1,0:T(8,128)(2,1)}, u32[]{:S(2)}, u32[]{:S(2)}) collective-permute-start(bf16[512,2048]{1,0:T(8,128)(2,1)} %shard_map.180), channel_id=1, source_target_pairs={{0,1},{1,0},{2,3},{3,2},{4,5},{5,4},{6,7},{7,6},{8,9},{9,8},{10,11... | collective-permute-start | bytes 6291464 | tf_op jit(solution)/shard_map/ppermute | solution.py:122
  195.6 76.2 %all-to-all-start.1 = ((bf16[4,2,768,256]{3,2,1,0:T(8,128)(2,1)}), bf16[4,2,768,256]{3,2,1,0:T(8,128)(2,1)}, u32[]{:S(2)}, u32[]{:S(2)}) async-start(bf16[4,2,768,256]{3,2,1,0:T(8,128)(2,1)} %bitcast.153), calls=%async_computation.1 | async-start | bytes 6291456 | tf_op jit(solution)/shard_map/all_to_all | solution.py:273
  204.5 20.5 %collective-permute-start.35 = (bf16[2,1,768,256]{3,2,1,0:T(8,128)(2,1)S(1)}, bf16[2,1,768,256]{3,2,1,0:T(8,128)(2,1)S(1)}, u32[]{:S(2)}, u32[]{:S(2)}) collective-permute-start(bf16[2,1,768,256]{3,2,1,0:T(8,128)(2,1)S(1)} %get-tuple-element.51), channel_id=1, source_target_pairs={{0,4},{4,0},{8,12},{12,8},{16,20},{20,16},{24,28},{28,24},{1,5},{5... | collective-permute-start | bytes 2359304 | tf_op jit(solution)/shard_map/ppermute | solution.py:99
  216.7 19.5 %collective-permute-start.17 = (bf16[2,2,32,2048]{3,2,1,0:T(8,128)(2,1)S(1)}, bf16[2,2,32,2048]{3,2,1,0:T(8,128)(2,1)S(1)}, u32[]{:S(2)}, u32[]{:S(2)}) collective-permute-start(bf16[2,2,32,2048]{3,2,1,0:T(8,128)(2,1)S(1)} %bitcast.178), channel_id=1, source_target_pairs={{0,4},{4,0},{8,12},{12,8},{16,20},{20,16},{24,28},{28,24},{1,5},{5... | collective-permute-start | bytes 1572872 | tf_op jit(solution)/shard_map/ppermute | solution.py:112
  217.2 20.6 %collective-permute-start.15 = (bf16[2,2,32,2048]{3,2,1,0:T(8,128)(2,1)S(1)}, bf16[2,2,32,2048]{3,2,1,0:T(8,128)(2,1)S(1)}, u32[]{:S(2)}, u32[]{:S(2)}) collective-permute-start(bf16[2,2,32,2048]{3,2,1,0:T(8,128)(2,1)S(1)} %bitcast.176), channel_id=1, source_target_pairs={{0,2},{1,3},{2,0},{3,1},{4,6},{5,7},{6,4},{7,5},{8,10},{9,11},{10,... | collective-permute-start | bytes 1572872 | tf_op jit(solution)/shard_map/ppermute | solution.py:117
  221.3 26.2 %collective-permute-start.31 = (bf16[2,2,32,2048]{3,2,1,0:T(8,128)(2,1)S(1)}, bf16[2,2,32,2048]{3,2,1,0:T(8,128)(2,1)S(1)}, u32[]{:S(2)}, u32[]{:S(2)}) collective-permute-start(bf16[2,2,32,2048]{3,2,1,0:T(8,128)(2,1)S(1)} %bitcast.177), channel_id=1, source_target_pairs={{0,4},{4,0},{8,12},{12,8},{16,20},{20,16},{24,28},{28,24},{1,5},{5... | collective-permute-start | bytes 1572872 | tf_op jit(solution)/shard_map/ppermute | solution.py:112
  222.9 26.2 %collective-permute-start.29 = (bf16[2,2,32,2048]{3,2,1,0:T(8,128)(2,1)S(1)}, bf16[2,2,32,2048]{3,2,1,0:T(8,128)(2,1)S(1)}, u32[]{:S(2)}, u32[]{:S(2)}) collective-permute-start(bf16[2,2,32,2048]{3,2,1,0:T(8,128)(2,1)S(1)} %bitcast.175), channel_id=1, source_target_pairs={{0,2},{1,3},{2,0},{3,1},{4,6},{5,7},{6,4},{7,5},{8,10},{9,11},{10,... | collective-permute-start | bytes 1572872 | tf_op jit(solution)/shard_map/ppermute | solution.py:117
  236.4 14.5 %collective-permute-start.18 = (bf16[2,32,2048]{2,1,0:T(8,128)(2,1)S(1)}, bf16[2,32,2048]{2,1,0:T(8,128)(2,1)S(1)}, u32[]{:S(2)}, u32[]{:S(2)}) collective-permute-start(bf16[2,32,2048]{2,1,0:T(8,128)(2,1)S(1)} %slice_bitcast_fusion.4), channel_id=1, source_target_pairs={{0,2},{1,3},{2,0},{3,1},{4,6},{5,7},{6,4},{7,5},{8,10},{9,11},{10,... | collective-permute-start | bytes 786440 | tf_op jit(solution)/shard_map/ppermute | solution.py:117
  238.0 14.5 %collective-permute-start.16 = (bf16[2,32,2048]{2,1,0:T(8,128)(2,1)S(1)}, bf16[2,32,2048]{2,1,0:T(8,128)(2,1)S(1)}, u32[]{:S(2)}, u32[]{:S(2)}) collective-permute-start(bf16[2,32,2048]{2,1,0:T(8,128)(2,1)S(1)} %slice_bitcast_fusion.6), channel_id=1, source_target_pairs={{0,4},{4,0},{8,12},{12,8},{16,20},{20,16},{24,28},{28,24},{1,5},{5... | collective-permute-start | bytes 786440 | tf_op jit(solution)/shard_map/ppermute | solution.py:112
  247.6 9.6 %collective-permute-start.32 = (bf16[2,32,2048]{2,1,0:T(8,128)(2,1)S(1)}, bf16[2,32,2048]{2,1,0:T(8,128)(2,1)S(1)}, u32[]{:S(2)}, u32[]{:S(2)}) collective-permute-start(bf16[2,32,2048]{2,1,0:T(8,128)(2,1)S(1)} %slice_bitcast_fusion), channel_id=1, source_target_pairs={{0,2},{1,3},{2,0},{3,1},{4,6},{5,7},{6,4},{7,5},{8,10},{9,11},{10,... | collective-permute-start | bytes 786440 | tf_op jit(solution)/shard_map/ppermute | solution.py:117
  249.2 8.0 %collective-permute-start.30 = (bf16[2,32,2048]{2,1,0:T(8,128)(2,1)S(1)}, bf16[2,32,2048]{2,1,0:T(8,128)(2,1)S(1)}, u32[]{:S(2)}, u32[]{:S(2)}) collective-permute-start(bf16[2,32,2048]{2,1,0:T(8,128)(2,1)S(1)} %slice_bitcast_fusion.2), channel_id=1, source_target_pairs={{0,4},{4,0},{8,12},{12,8},{16,20},{20,16},{24,28},{28,24},{1,5},{5... | collective-permute-start | bytes 786440 | tf_op jit(solution)/shard_map/ppermute | solution.py:112
  253.3 28.7 %collective-permute-start.19 = (bf16[64,2048]{1,0:T(8,128)(2,1)}, bf16[64,2048]{1,0:T(8,128)(2,1)}, u32[]{:S(2)}, u32[]{:S(2)}) collective-permute-start(bf16[64,2048]{1,0:T(8,128)(2,1)} %fusion.34), channel_id=1, source_target_pairs={{0,24},{4,28},{8,0},{12,4},{16,8},{20,12},{24,16},{28,20},{1,25},{... | collective-permute-start | bytes 786440 | tf_op jit(solution)/shard_map/ppermute | solution.py:94
  274.2 22.4 %copy-start.1 = (bf16[512,2048]{1,0:T(8,128)(2,1)S(1)}, bf16[512,2048]{1,0:T(8,128)(2,1)}, u32[]{:S(2)}) copy-start(bf16[512,2048]{1,0:T(8,128)(2,1)} %param.27) | copy-start | bytes 6291460
  274.2 21.5 %collective-permute-start.36 = (bf16[2,1,768,256]{3,2,1,0:T(8,128)(2,1)S(1)}, bf16[2,1,768,256]{3,2,1,0:T(8,128)(2,1)S(1)}, u32[]{:S(2)}, u32[]{:S(2)}) collective-permute-start(bf16[2,1,768,256]{3,2,1,0:T(8,128)(2,1)S(1)} %get-tuple-element.49), channel_id=1, source_target_pairs={{0,4},{4,0},{8,12},{12,8},{16,20},{20,16},{24,28},{28,24},{1,5},{5... | collective-permute-start | bytes 2359304 | tf_op jit(solution)/shard_map/ppermute | solution.py:99
  275.4 18.5 %collective-permute-start.33 = (bf16[64,2048]{1,0:T(8,128)(2,1)S(1)}, bf16[64,2048]{1,0:T(8,128)(2,1)S(1)}, u32[]{:S(2)}, u32[]{:S(2)}) collective-permute-start(bf16[64,2048]{1,0:T(8,128)(2,1)S(1)} %get-tuple-element.69), channel_id=1, source_target_pairs={{0,16},{4,20},{8,24},{12,28},{16,0},{20,4},{24,8},{28,12},{1,17},{... | collective-permute-start | bytes 786440 | tf_op jit(solution)/shard_map/ppermute | solution.py:94
  275.4 18.4 %collective-permute-start.34 = (bf16[64,2048]{1,0:T(8,128)(2,1)S(1)}, bf16[64,2048]{1,0:T(8,128)(2,1)S(1)}, u32[]{:S(2)}, u32[]{:S(2)}) collective-permute-start(bf16[64,2048]{1,0:T(8,128)(2,1)S(1)} %get-tuple-element.70), channel_id=1, source_target_pairs={{0,8},{4,12},{8,16},{12,20},{16,24},{20,28},{24,0},{28,4},{1,9},{5... | collective-permute-start | bytes 786440 | tf_op jit(solution)/shard_map/ppermute | solution.py:94
  (17 other events, 71.4 us)
where the time goes:
time: 298 us; the launch traced here: 297 us
  waiting for transfers between devices  130 us (44%)
  starting transfers between devices  62.8 us (21%)
  Pallas kernels  31.8 us (11%)
  local copies, waits for them, and re-layouts  31.4 us (11%)
  other arithmetic  26 us (9%)
  between operations  9.81 us (3%)
  matrix products  5.19 us (2%)
    ppermute x9, waiting for transfers between devices, flip_pair(): return lax.ppermute(value, 'req', [(i, i ^ 1) for i in range(count)])  49 us
    ppermute x5, waiting for transfers between devices, swap(): return lax.ppermute(value, 'req', [(i, i ^ mask) for i in range(count)])  29.9 us
    pallas_call x4, Pallas kernels, run_experts(): pl.pallas_call(experts_kernel, out_shape=jax.ShapeDtypeStruct((count, wid...  22.4 us
    ppermute x9, starting transfers between devices, turn_pairs(): lax.ppermute(value, 'req', [(i, (i + 2 * step) % count) for i in range(co...  22.3 us
    ppermute x9, waiting for transfers between devices, flip_chip(): return lax.ppermute(value, 'exp', [(i, i ^ 2) for i in range(count)])  18.9 us
    all_to_all x2, waiting for transfers between devices, trade_columns(): lax.all_to_all(outgoing, 'req', 0, 0, axis_index_groups=columns, tiled=True)  17 us
    ppermute x9, waiting for transfers between devices, turn_pairs(): lax.ppermute(value, 'req', [(i, (i + 2 * step) % count) for i in range(co...  14.7 us
    unnamed x57, local copies, waits for them, and re-layouts  12.9 us
  transfers between devices with their start and end apart: 39, of which 16 were waited for; matrix products, arithmetic and copies ran while one was open for 16% of the time, Pallas kernels for 11%

commit v1 on v0

--- a/solution.py
+++ b/solution.py
@@ -199,21 +199,22 @@
     outgoing = after(outgoing, *pieces[1:])
     *pieces[2:], outgoing = together(*pieces[2:], outgoing)
     arrived = trade_columns(outgoing)
-    total = None
+    total, ready = None, []
     for begin in range(0, pair_count, 2):
         here = spread_tokens(pieces[begin : begin + 2])
         there = flip_core(here)
+        if begin + 2 >= pair_count:
+            there, arrived = together(there, arrived)
         back = flip_core(run_experts(first_slot, there, slot_weights, 256))
-        if begin + 2 >= pair_count:
-            here, arrived = together(here, arrived)
         mixed = run_experts(first_slot, here, slot_weights, 256)
         sums = gather_sums(add(mixed, back), 2)
+        ready.append(sums)
         for offset in range(2):
             step = begin + offset
             part = sums[offset] if step == 0 else turn_pairs(sums[offset], -step)
             part = part.astype(jnp.float32)
             total = part if total is None else total + part
-    return total, arrived
+    return total, arrived, ready
 
 
 def spread_weights(slot_weights):
@@ -400,11 +401,12 @@
     slots_here = slot_weights.shape[0]
     index = chunk_index(source_slot, slots_here)
     size = held[0].shape[1] // 2
-    mixture, first = mix(
+    mixture, first, ready = mix(
         normed, codes, slot_weights, held, lambda held: take_chunks(held, index, 0, size)
     )
     layer_out = (residual + mixture).astype(jnp.bfloat16)
     second = trade_columns(after(take_chunks(held, index, size, size), first))
+    second = after(second, *ready)
     replica_weights = collect_replicas((first, second), source_slot, slots_here)
     return (layer_out, replica_weights.reshape((1,) + slot_weights.shape[1:]))
 

time: 298 us -> 350 us (1.17)
  waiting for transfers between devices: 130 us -> 174 us
  local copies, waits for them, and re-layouts: 31.4 us -> 35.4 us
  other arithmetic: 26 us -> 29.5 us
    ppermute x5, waiting for transfers between devices: 29.9 us -> 0.01 us  [swap(): return lax.ppermute(value, 'req', [(i, i ^ mask) for i in range(count)])]
    ppermute x9, waiting for transfers between devices: 49 us -> 77.3 us  [flip_pair(): return lax.ppermute(value, 'req', [(i, i ^ 1) for i in range(count)])]
    ppermute x9, waiting for transfers between devices: 14.7 us -> 34 us  [turn_pairs(): lax.ppermute(value, 'req', [(i, (i + 2 * step) % count) for i in range(co...]
    all_to_all x2, waiting for transfers between devices: 17 us -> 30.9 us  [trade_columns(): lax.all_to_all(outgoing, 'req', 0, 0, axis_index_groups=columns, tiled=True)]
    ppermute x9, waiting for transfers between devices: 18.9 us -> 30 us  [flip_chip(): return lax.ppermute(value, 'exp', [(i, i ^ 2) for i in range(count)])]
    unnamed x57 -> x69, local copies, waits for them, and re-layouts: 12.9 us -> 15.7 us
  transfers between devices with their start and end apart: 39 -> 39, of which waited for: 16 -> 20; matrix products, arithmetic and copies ran while one was open for 16% -> 14% of each run, Pallas kernels for 11% -> 9%
where the time goes in v1:
time: 350 us; the launch traced here: 349 us
  waiting for transfers between devices  174 us (50%)
  starting transfers between devices  60.8 us (17%)
  local copies, waits for them, and re-layouts  35.4 us (10%)
  Pallas kernels  32.9 us (9%)
  other arithmetic  29.5 us (8%)
  between operations  10.8 us (3%)
  matrix products  5.08 us (1%)
    ppermute x9, waiting for transfers between devices, flip_pair(): return lax.ppermute(value, 'req', [(i, i ^ 1) for i in range(count)])  77.3 us
    ppermute x9, waiting for transfers between devices, turn_pairs(): lax.ppermute(value, 'req', [(i, (i + 2 * step) % count) for i in range(co...  34 us
    all_to_all x2, waiting for transfers between devices, trade_columns(): lax.all_to_all(outgoing, 'req', 0, 0, axis_index_groups=columns, tiled=True)  30.9 us
    ppermute x9, waiting for transfers between devices, flip_chip(): return lax.ppermute(value, 'exp', [(i, i ^ 2) for i in range(count)])  30 us
    pallas_call x4, Pallas kernels, run_experts(): pl.pallas_call(experts_kernel, out_shape=jax.ShapeDtypeStruct((count, wid...  22.2 us
    ppermute x9, starting transfers between devices, turn_pairs(): lax.ppermute(value, 'req', [(i, (i + 2 * step) % count) for i in range(co...  21.5 us
    unnamed x69, local copies, waits for them, and re-layouts  15.7 us
    ppermute x9, starting transfers between devices, flip_chip(): return lax.ppermute(value, 'exp', [(i, i ^ 2) for i in range(count)])  11.2 us
  transfers between devices with their start and end apart: 39, of which 20 were waited for; matrix products, arithmetic and copies ran while one was open for 14% of the time, Pallas kernels for 9%

profile of v1, /device:TPU:0, one launch (start us, length us, event | category | flops | bytes accessed | tf_op | source)
XLA Modules:
  0.0 348.6 jit_solution(2978765774855784976)
XLA Ops:
  0.6 1.7 fusion.71
  2.3 5.0 %collective-permute-start.2 = (bf16[2,2,32,512]{3,2,1,0:T(8,128)(2,1)}, bf16[2,2,32,512]{3,2,1,0:T(8,128)(2,1)}, u32[]{:S(2)}, u32[]{:S(2)}) collective-permute-start(bf16[2,2,32,512]{3,2,1,0:T(8,128)(2,1)} %get-tuple-element.82), channel_id=1, source_target_pairs={{0,24},{4,28},{8,0},{12,4},{16,8},{20,12},{24,16},{28,20},{1,25},{... | collective-permute-start | bytes 393224 | tf_op jit(solution)/shard_map/ppermute | solution.py:94
  8.4 5.7 %dynamic-slice_bitcast_fusion = (bf16[2,1536,256]{2,1,0:T(8,128)(2,1)}, bf16[2,1536,256]{2,1,0:T(8,128)(2,1)}, bf16[2,1536,256]{2,1,0:T(8,128)(2,1)}, bf16[2,1536,256]{2,1,0:T(8,128)(2,1)}) fusion(bf16[2,4,1536,256]{3,2,1,0:T(8,128)(2,1)} %bitcast.154, s32[]{:T(128)S(6)} %select_n.262, s32[]{:T(128)S(6)} %select_n.256, s32[]{:T(128)S(6)} %select_n.248, ...), kind=kLoop, calls=%fused_computation.6 | loop fusion | bytes 12582928 | tf_op jit(solution)/shard_map/jit(dynamic_index_in_dim)/squeeze | solution.py:126
  15.7 2.5 collective-permute-start.5
  38.6 13.9 %collective-permute-done.3 = bf16[2,2,32,512]{3,2,1,0:T(8,128)(2,1)S(1)} collective-permute-done((bf16[2,2,32,512]{3,2,1,0:T(8,128)(2,1)S(1)}, bf16[2,2,32,512]{3,2,1,0:T(8,128)(2,1)S(1)}, u32[]{:S(2)}, u32[]{:S(2)}) %collective-permute-start.3) | collective-permute-done | bytes 131104 | tf_op jit(solution)/shard_map/ppermute | solution.py:112
  52.7 2.7 fusion.80
  59.3 1.9 collective-permute-done.6
  64.5 6.5 %collective-permute-done.7 = bf16[64,2048]{1,0:T(8,128)(2,1)S(1)} collective-permute-done((bf16[64,2048]{1,0:T(8,128)(2,1)S(1)}, bf16[64,2048]{1,0:T(8,128)(2,1)S(1)}, u32[]{:S(2)}, u32[]{:S(2)}) %collective-permute-start.7) | collective-permute-done | bytes 262176 | tf_op jit(solution)/shard_map/ppermute | solution.py:117
  71.4 2.5 collective-permute-start.8
  75.2 7.7 %collective-permute-done.8 = bf16[64,2176]{1,0:T(8,128)(2,1)S(1)} collective-permute-done((bf16[64,2176]{1,0:T(8,128)(2,1)S(1)}, bf16[64,2176]{1,0:T(8,128)(2,1)S(1)}, u32[]{:S(2)}, u32[]{:S(2)}) %collective-permute-start.8) | collective-permute-done | bytes 278560 | tf_op jit(solution)/shard_map/ppermute | solution.py:94
  86.2 3.4 collective-permute-done.11
  91.2 30.7 %collective-permute-done.9 = bf16[2,32,2176]{2,1,0:T(8,128)(2,1)S(1)} collective-permute-done((bf16[2,32,2176]{2,1,0:T(8,128)(2,1)S(1)}, bf16[2,32,2176]{2,1,0:T(8,128)(2,1)S(1)}, u32[]{:S(2)}, u32[]{:S(2)}) %collective-permute-start.9) | collective-permute-done | bytes 278560 | tf_op jit(solution)/shard_map/ppermute | solution.py:112
  126.7 5.4 %shard_map.178 = bf16[8,768,256]{2,1,0:T(8,128)(2,1)S(1)} custom-call(s32[8]{0:T(128)S(1)} %fusion.52.index_ref, bf16[2,1536,256]{2,1,0:T(8,128)(2,1)S(1)} %copy-done.2, bf16[2,1536,256]{2,1,0:T(8,128)(2,1)} %collective-permute-done.4.refs_1_, bf16[2,1536,256]{2,1,0:T(8,128)(2,1)} %collective-permute-done.5.refs_2_, ...), custom_call_target="tpu_custom_call" | custom-call | bytes 6291456 | tf_op jit(solution)/shard_map/pallas_call | solution.py:254
  133.8 9.7 %collective-permute-done.21 = bf16[64,2176]{1,0:T(8,128)(2,1)S(1)} collective-permute-done((bf16[64,2176]{1,0:T(8,128)(2,1)S(1)}, bf16[64,2176]{1,0:T(8,128)(2,1)S(1)}, u32[]{:S(2)}, u32[]{:S(2)}) %collective-permute-start.21) | collective-permute-done | bytes 278560 | tf_op jit(solution)/shard_map/ppermute | solution.py:94
  144.2 4.8 %all-to-all-start = ((bf16[4,2,768,256]{3,2,1,0:T(8,128)(2,1)}), bf16[4,2,768,256]{3,2,1,0:T(8,128)(2,1)}, u32[]{:S(2)}, u32[]{:S(2)}) async-start(bf16[4,2,768,256]{3,2,1,0:T(8,128)(2,1)} %bitcast.152), calls=%async_computation | async-start | bytes 6291456 | tf_op jit(solution)/shard_map/all_to_all | solution.py:274
  149.1 3.0 pad_maximum_fusion.tok_ref
  154.5 6.8 %collective-permute-done.25 = bf16[2,32,2176]{2,1,0:T(8,128)(2,1)S(1)} collective-permute-done((bf16[2,32,2176]{2,1,0:T(8,128)(2,1)S(1)}, bf16[2,32,2176]{2,1,0:T(8,128)(2,1)S(1)}, u32[]{:S(2)}, u32[]{:S(2)}) %collective-permute-start.25) | collective-permute-done | bytes 278560 | tf_op jit(solution)/shard_map/ppermute | solution.py:117
  164.5 11.3 %collective-permute-done.26 = bf16[2,2,32,2176]{3,2,1,0:T(8,128)(2,1)} collective-permute-done((bf16[2,2,32,2176]{3,2,1,0:T(8,128)(2,1)S(1)}, bf16[2,2,32,2176]{3,2,1,0:T(8,128)(2,1)}, u32[]{:S(2)}, u32[]{:S(2)}) %collective-permute-start.26) | collective-permute-done | bytes 557088 | tf_op jit(solution)/shard_map/ppermute | solution.py:112
  175.9 2.4 collective-permute-done.24
  178.2 2.9 pad_maximum_fusion.1.tok_ref
  181.2 2.8 copy-done.7
  184.0 6.0 %shard_map.177 = bf16[512,2048]{1,0:T(8,128)(2,1)} custom-call(s32[1]{0:T(128)} %bitcast.35.first_slot_ref, bf16[512,2176]{1,0:T(8,128)(2,1)} %collective-permute-done.13.tok_ref, bf16[2,3,2048,256]{3,2,1,0:T(8,128)(2,1)S(1)} %copy-done.7), custom_call_target="tpu_custom_call" | custom-call | flops 3221225472 | bytes 10485760 | tf_op jit(solution)/shard_map/pallas_call | solution.py:73
  193.9 5.4 %shard_map.181 = bf16[8,768,256]{2,1,0:T(8,128)(2,1)S(1)} custom-call(s32[8]{0:T(128)S(1)} %fusion.52.index_ref, bf16[2,1536,256]{2,1,0:T(8,128)(2,1)S(1)} %copy-done.2, bf16[2,1536,256]{2,1,0:T(8,128)(2,1)} %collective-permute-done.4.refs_1_, bf16[2,1536,256]{2,1,0:T(8,128)(2,1)} %collective-permute-done.5.refs_2_, bf16[2,1536,256]{2,1,0:T(8,128)(2,1)S(1)} %copy-done.6), custom_call_target="tpu_custom_call" | custom-call | bytes 6291456 | tf_op jit(solution)/shard_map/pallas_call | solution.py:254
  200.9 2.8 copy-done.8
  203.7 5.1 %shard_map.176 = bf16[512,2048]{1,0:T(8,128)(2,1)S(1)} custom-call(s32[1]{0:T(128)} %bitcast.35.first_slot_ref, bf16[512,2176]{1,0:T(8,128)(2,1)} %pad_maximum_fusion.tok_ref, bf16[2,3,2048,256]{3,2,1,0:T(8,128)(2,1)S(1)} %copy-done.8), custom_call_target="tpu_custom_call" | custom-call | flops 3221225472 | bytes 10485760 | tf_op jit(solution)/shard_map/pallas_call | solution.py:73
  208.8 9.4 %all-to-all-done = bf16[4,2,768,256]{3,2,1,0:T(8,128)(2,1)} async-done(((bf16[4,2,768,256]{3,2,1,0:T(8,128)(2,1)}), bf16[4,2,768,256]{3,2,1,0:T(8,128)(2,1)}, u32[]{:S(2)}, u32[]{:S(2)}) %all-to-all-start) | async-done | bytes 3145760 | tf_op jit(solution)/shard_map/all_to_all | solution.py:274
  218.1 1.9 broadcast_in_dim.162
  220.0 2.8 constant_dynamic-slice_fusion.1
  222.8 2.0 collective-permute-start.35
  224.8 2.4 add_convert_fusion.1
  229.2 5.1 %shard_map.179 = bf16[512,2048]{1,0:T(8,128)(2,1)S(1)} custom-call(s32[1]{0:T(128)} %bitcast.35.first_slot_ref, bf16[512,2176]{1,0:T(8,128)(2,1)} %pad_maximum_fusion.1.tok_ref, bf16[2,3,2048,256]{3,2,1,0:T(8,128)(2,1)S(1)} %bitcast.156), custom_call_target="tpu_custom_call" | custom-call | flops 3221225472 | bytes 10485760 | tf_op jit(solution)/shard_map/pallas_call | solution.py:73
  235.7 6.0 %shard_map.180 = bf16[512,2048]{1,0:T(8,128)(2,1)} custom-call(s32[1]{0:T(128)} %bitcast.35.first_slot_ref, bf16[512,2176]{1,0:T(8,128)(2,1)} %collective-permute-done.27.tok_ref, bf16[2,3,2048,256]{3,2,1,0:T(8,128)(2,1)S(1)} %bitcast.156), custom_call_target="tpu_custom_call" | custom-call | flops 3221225472 | bytes 10485760 | tf_op jit(solution)/shard_map/pallas_call | solution.py:73
  241.7 4.6 %all-to-all-start.1 = ((bf16[4,2,768,256]{3,2,1,0:T(8,128)(2,1)}), bf16[4,2,768,256]{3,2,1,0:T(8,128)(2,1)}, u32[]{:S(2)}, u32[]{:S(2)}) async-start(bf16[4,2,768,256]{3,2,1,0:T(8,128)(2,1)} %bitcast.153), calls=%async_computation.1 | async-start | bytes 6291456 | tf_op jit(solution)/shard_map/all_to_all | solution.py:274
  251.6 9.7 %collective-permute-done.17 = bf16[2,2,32,2048]{3,2,1,0:T(8,128)(2,1)S(1)} collective-permute-done((bf16[2,2,32,2048]{3,2,1,0:T(8,128)(2,1)}, bf16[2,2,32,2048]{3,2,1,0:T(8,128)(2,1)S(1)}, u32[]{:S(2)}, u32[]{:S(2)}) %collective-permute-start.17) | collective-permute-done | bytes 524320 | tf_op jit(solution)/shard_map/ppermute | solution.py:112
  262.8 3.8 %collective-permute-done.16 = bf16[2,32,2048]{2,1,0:T(8,128)(2,1)S(1)} collective-permute-done((bf16[2,32,2048]{2,1,0:T(8,128)(2,1)S(1)}, bf16[2,32,2048]{2,1,0:T(8,128)(2,1)S(1)}, u32[]{:S(2)}, u32[]{:S(2)}) %collective-permute-start.16) | collective-permute-done | bytes 262176 | tf_op jit(solution)/shard_map/ppermute | solution.py:112
  266.7 2.4 add_convert_fusion
  271.3 3.4 collective-permute-start.19
  275.0 8.0 %collective-permute-done.29 = bf16[2,2,32,2048]{3,2,1,0:T(8,128)(2,1)S(1)} collective-permute-done((bf16[2,2,32,2048]{3,2,1,0:T(8,128)(2,1)S(1)}, bf16[2,2,32,2048]{3,2,1,0:T(8,128)(2,1)S(1)}, u32[]{:S(2)}, u32[]{:S(2)}) %collective-permute-start.29) | collective-permute-done | bytes 524320 | tf_op jit(solution)/shard_map/ppermute | solution.py:117
  284.3 5.3 %collective-permute-done.31 = bf16[2,2,32,2048]{3,2,1,0:T(8,128)(2,1)S(1)} collective-permute-done((bf16[2,2,32,2048]{3,2,1,0:T(8,128)(2,1)S(1)}, bf16[2,2,32,2048]{3,2,1,0:T(8,128)(2,1)S(1)}, u32[]{:S(2)}, u32[]{:S(2)}) %collective-permute-start.31) | collective-permute-done | bytes 524320 | tf_op jit(solution)/shard_map/ppermute | solution.py:112
  290.6 2.5 collective-permute-done.30
  293.2 3.0 collective-permute-done.32
  296.9 21.5 %all-to-all-done.1 = bf16[4,2,768,256]{3,2,1,0:T(8,128)(2,1)} async-done(((bf16[4,2,768,256]{3,2,1,0:T(8,128)(2,1)}), bf16[4,2,768,256]{3,2,1,0:T(8,128)(2,1)}, u32[]{:S(2)}, u32[]{:S(2)}) %all-to-all-start.1) | async-done | bytes 3145760 | tf_op jit(solution)/shard_map/all_to_all | solution.py:274
  318.4 2.4 constant_dynamic-slice_fusion
  322.0 3.9 %collective-permute-start.34 = (bf16[64,2048]{1,0:T(8,128)(2,1)S(1)}, bf16[64,2048]{1,0:T(8,128)(2,1)S(1)}, u32[]{:S(2)}, u32[]{:S(2)}) collective-permute-start(bf16[64,2048]{1,0:T(8,128)(2,1)S(1)} %get-tuple-element.72), channel_id=1, source_target_pairs={{0,8},{4,12},{8,16},{12,20},{16,24},{20,28},{24,0},{28,4},{1,9},{5... | collective-permute-start | bytes 786440 | tf_op jit(solution)/shard_map/ppermute | solution.py:94
  325.9 3.4 collective-permute-start.33
  329.3 6.7 %collective-permute-done.34 = bf16[64,2048]{1,0:T(8,128)(2,1)S(1)} collective-permute-done((bf16[64,2048]{1,0:T(8,128)(2,1)S(1)}, bf16[64,2048]{1,0:T(8,128)(2,1)S(1)}, u32[]{:S(2)}, u32[]{:S(2)}) %collective-permute-start.34) | collective-permute-done | bytes 262176 | tf_op jit(solution)/shard_map/ppermute | solution.py:94
  336.0 9.9 %collective-permute-done.33 = bf16[64,2048]{1,0:T(8,128)(2,1)S(1)} collective-permute-done((bf16[64,2048]{1,0:T(8,128)(2,1)S(1)}, bf16[64,2048]{1,0:T(8,128)(2,1)S(1)}, u32[]{:S(2)}, u32[]{:S(2)}) %collective-permute-start.33) | collective-permute-done | bytes 262176 | tf_op jit(solution)/shard_map/ppermute | solution.py:94
  345.9 1.8 fusion.14
  (201 shorter events, 63.5 us)
Async XLA Ops:
  0.6 56.4 %copy-start = (bf16[512,2048]{1,0:T(8,128)(2,1)S(1)}, bf16[512,2048]{1,0:T(8,128)(2,1)}, u32[]{:S(2)}) copy-start(bf16[512,2048]{1,0:T(8,128)(2,1)} %param.27) | copy-start | bytes 6291460
  2.3 34.3 %collective-permute-start.2 = (bf16[2,2,32,512]{3,2,1,0:T(8,128)(2,1)}, bf16[2,2,32,512]{3,2,1,0:T(8,128)(2,1)}, u32[]{:S(2)}, u32[]{:S(2)}) collective-permute-start(bf16[2,2,32,512]{3,2,1,0:T(8,128)(2,1)} %get-tuple-element.82), channel_id=1, source_target_pairs={{0,24},{4,28},{8,0},{12,4},{16,8},{20,12},{24,16},{28,20},{1,25},{... | collective-permute-start | bytes 393224 | tf_op jit(solution)/shard_map/ppermute | solution.py:94
  7.4 29.3 %collective-permute-start.1 = (bf16[2,2,32,512]{3,2,1,0:T(8,128)(2,1)}, bf16[2,2,32,512]{3,2,1,0:T(8,128)(2,1)}, u32[]{:S(2)}, u32[]{:S(2)}) collective-permute-start(bf16[2,2,32,512]{3,2,1,0:T(8,128)(2,1)} %get-tuple-element.82), channel_id=1, source_target_pairs={{0,16},{4,20},{8,24},{12,28},{16,0},{20,4},{24,8},{28,12},{1,17},{... | collective-permute-start | bytes 393224 | tf_op jit(solution)/shard_map/ppermute | solution.py:94
  7.4 29.3 %collective-permute-start = (bf16[2,2,32,512]{3,2,1,0:T(8,128)(2,1)}, bf16[2,2,32,512]{3,2,1,0:T(8,128)(2,1)}, u32[]{:S(2)}, u32[]{:S(2)}) collective-permute-start(bf16[2,2,32,512]{3,2,1,0:T(8,128)(2,1)} %get-tuple-element.82), channel_id=1, source_target_pairs={{0,8},{4,12},{8,16},{12,20},{16,24},{20,28},{24,0},{28,4},{1,9},{5... | collective-permute-start | bytes 393224 | tf_op jit(solution)/shard_map/ppermute | solution.py:94
  8.4 14.1 %copy-start.16 = (bf16[256,512]{1,0:T(8,128)(2,1)S(1)}, bf16[256,512]{1,0:T(8,128)(2,1)}, u32[]{:S(2)}) copy-start(bf16[256,512]{1,0:T(8,128)(2,1)} %param.19) | copy-start | bytes 786436
  8.4 14.5 %copy-start.17 = (bf16[256,512]{1,0:T(8,128)(2,1)S(1)}, bf16[256,512]{1,0:T(8,128)(2,1)}, u32[]{:S(2)}) copy-start(bf16[256,512]{1,0:T(8,128)(2,1)} %param.18) | copy-start | bytes 786436
  14.2 42.9 %collective-permute-start.4 = (bf16[2,1536,256]{2,1,0:T(8,128)(2,1)}, bf16[2,1536,256]{2,1,0:T(8,128)(2,1)}, u32[]{:S(2)}, u32[]{:S(2)}) collective-permute-start(bf16[2,1536,256]{2,1,0:T(8,128)(2,1)} %get-tuple-element.50), channel_id=1, source_target_pairs={{0,4},{4,0},{8,12},{12,8},{16,20},{20,16},{24,28},{28,24},{1,5},{5... | collective-permute-start | bytes 4718600 | tf_op jit(solution)/shard_map/ppermute | solution.py:99
  15.7 41.4 %collective-permute-start.5 = (bf16[2,1536,256]{2,1,0:T(8,128)(2,1)}, bf16[2,1536,256]{2,1,0:T(8,128)(2,1)}, u32[]{:S(2)}, u32[]{:S(2)}) collective-permute-start(bf16[2,1536,256]{2,1,0:T(8,128)(2,1)} %get-tuple-element.49), channel_id=1, source_target_pairs={{0,8},{4,12},{8,0},{12,4},{16,24},{20,28},{24,16},{28,20},{1,9},{5... | collective-permute-start | bytes 4718600 | tf_op jit(solution)/shard_map/ppermute | solution.py:99
  27.5 25.1 %copy-start.20 = (bf16[256,4,64]{2,0,1:T(8,128)(2,1)S(1)}, bf16[256,4,64]{2,0,1:T(8,128)(2,1)}, u32[]{:S(2)}) copy-start(bf16[256,4,64]{2,0,1:T(8,128)(2,1)} %get-tuple-element.77) | copy-start | bytes 393220
  37.9 14.6 %collective-permute-start.3 = (bf16[2,2,32,512]{3,2,1,0:T(8,128)(2,1)S(1)}, bf16[2,2,32,512]{3,2,1,0:T(8,128)(2,1)S(1)}, u32[]{:S(2)}, u32[]{:S(2)}) collective-permute-start(bf16[2,2,32,512]{3,2,1,0:T(8,128)(2,1)S(1)} %pad_maximum_fusion.12), channel_id=1, source_target_pairs={{0,4},{4,0},{8,12},{12,8},{16,20},{20,16},{24,28},{28,24},{1,5},{5... | collective-permute-start | bytes 393224 | tf_op jit(solution)/shard_map/ppermute | solution.py:112
  57.8 13.1 %copy-start.19 = (bf16[64,2048]{1,0:T(8,128)(2,1)S(1)}, bf16[64,2048]{1,0:T(8,128)(2,1)}, u32[]{:S(2)}) copy-start(bf16[64,2048]{1,0:T(8,128)(2,1)} %param.17) | copy-start | bytes 786436
  59.2 2.0 collective-permute-start.6
  62.6 8.4 %collective-permute-start.7 = (bf16[64,2048]{1,0:T(8,128)(2,1)S(1)}, bf16[64,2048]{1,0:T(8,128)(2,1)S(1)}, u32[]{:S(2)}, u32[]{:S(2)}) collective-permute-start(bf16[64,2048]{1,0:T(8,128)(2,1)S(1)} %fusion.28), channel_id=1, source_target_pairs={{0,2},{1,3},{2,0},{3,1},{4,6},{5,7},{6,4},{7,5},{8,10},{9,11},{10,... | collective-permute-start | bytes 786440 | tf_op jit(solution)/shard_map/ppermute | solution.py:117
  71.2 53.1 %copy-start.29 = (s32[8]{0:T(128)S(1)}, s32[8]{0:T(128)}, u32[]{:S(2)}) copy-start(s32[8]{0:T(128)} %param.32) | copy-start | bytes 100
  71.2 55.5 %copy-start.2 = (bf16[2,1536,256]{2,1,0:T(8,128)(2,1)S(1)}, bf16[2,1536,256]{2,1,0:T(8,128)(2,1)}, u32[]{:S(2)}) copy-start(bf16[2,1536,256]{2,1,0:T(8,128)(2,1)} %get-tuple-element.47.refs_0_) | copy-start | bytes 4718596
  71.4 11.4 %collective-permute-start.8 = (bf16[64,2176]{1,0:T(8,128)(2,1)S(1)}, bf16[64,2176]{1,0:T(8,128)(2,1)S(1)}, u32[]{:S(2)}, u32[]{:S(2)}) collective-permute-start(bf16[64,2176]{1,0:T(8,128)(2,1)S(1)} %concatenate.37), channel_id=1, source_target_pairs={{0,8},{4,12},{8,16},{12,20},{16,24},{20,28},{24,0},{28,4},{1,9},{5... | collective-permute-start | bytes 835592 | tf_op jit(solution)/shard_map/ppermute | solution.py:94
  74.0 51.9 %collective-permute-start.20 = (bf16[2,1536,256]{2,1,0:T(8,128)(2,1)}, bf16[2,1536,256]{2,1,0:T(8,128)(2,1)S(1)}, u32[]{:S(2)}, u32[]{:S(2)}) collective-permute-start(bf16[2,1536,256]{2,1,0:T(8,128)(2,1)} %get-tuple-element.48), channel_id=1, source_target_pairs={{0,12},{4,8},{8,4},{12,0},{16,28},{20,24},{24,20},{28,16},{1,13},{... | collective-permute-start | bytes 4718600 | tf_op jit(solution)/shard_map/ppermute | solution.py:99
  82.9 6.6 %collective-permute-start.11 = (bf16[2,32,2176]{2,1,0:T(8,128)(2,1)S(1)}, bf16[2,32,2176]{2,1,0:T(8,128)(2,1)S(1)}, u32[]{:S(2)}, u32[]{:S(2)}) collective-permute-start(bf16[2,32,2176]{2,1,0:T(8,128)(2,1)S(1)} %get-tuple-element.68), channel_id=1, source_target_pairs={{0,2},{1,3},{2,0},{3,1},{4,6},{5,7},{6,4},{7,5},{8,10},{9,11},{10,... | collective-permute-start | bytes 835592 | tf_op jit(solution)/shard_map/ppermute | solution.py:117
  84.6 37.3 %collective-permute-start.9 = (bf16[2,32,2176]{2,1,0:T(8,128)(2,1)S(1)}, bf16[2,32,2176]{2,1,0:T(8,128)(2,1)S(1)}, u32[]{:S(2)}, u32[]{:S(2)}) collective-permute-start(bf16[2,32,2176]{2,1,0:T(8,128)(2,1)S(1)} %get-tuple-element.67), channel_id=1, source_target_pairs={{0,4},{4,0},{8,12},{12,8},{16,20},{20,16},{24,28},{28,24},{1,5},{5... | collective-permute-start | bytes 835592 | tf_op jit(solution)/shard_map/ppermute | solution.py:112
  89.6 59.4 %collective-permute-start.12 = (bf16[2,2,32,2176]{3,2,1,0:T(8,128)(2,1)S(1)}, bf16[2,2,32,2176]{3,2,1,0:T(8,128)(2,1)}, u32[]{:S(2)}, u32[]{:S(2)}) collective-permute-start(bf16[2,2,32,2176]{3,2,1,0:T(8,128)(2,1)S(1)} %pad_maximum_fusion.5), channel_id=1, source_target_pairs={{0,4},{4,0},{8,12},{12,8},{16,20},{20,16},{24,28},{28,24},{1,5},{5... | collective-permute-start | bytes 1671176 | tf_op jit(solution)/shard_map/ppermute | solution.py:112
  122.7 26.3 %collective-permute-start.10 = (bf16[2,2,32,2176]{3,2,1,0:T(8,128)(2,1)}, bf16[2,2,32,2176]{3,2,1,0:T(8,128)(2,1)}, u32[]{:S(2)}, u32[]{:S(2)}) collective-permute-start(bf16[2,2,32,2176]{3,2,1,0:T(8,128)(2,1)} %pad_maximum_fusion.4), channel_id=1, source_target_pairs={{0,2},{1,3},{2,0},{3,1},{4,6},{5,7},{6,4},{7,5},{8,10},{9,11},{10,... | collective-permute-start | bytes 1671176 | tf_op jit(solution)/shard_map/ppermute | solution.py:117
  124.5 19.0 %collective-permute-start.22 = (bf16[64,2176]{1,0:T(8,128)(2,1)S(1)}, bf16[64,2176]{1,0:T(8,128)(2,1)S(1)}, u32[]{:S(2)}, u32[]{:S(2)}) collective-permute-start(bf16[64,2176]{1,0:T(8,128)(2,1)S(1)} %concatenate.37), channel_id=1, source_target_pairs={{0,24},{4,28},{8,0},{12,4},{16,8},{20,12},{24,16},{28,20},{1,25},{... | collective-permute-start | bytes 835592 | tf_op jit(solution)/shard_map/ppermute | solution.py:94
  125.8 17.7 %collective-permute-start.21 = (bf16[64,2176]{1,0:T(8,128)(2,1)S(1)}, bf16[64,2176]{1,0:T(8,128)(2,1)S(1)}, u32[]{:S(2)}, u32[]{:S(2)}) collective-permute-start(bf16[64,2176]{1,0:T(8,128)(2,1)S(1)} %concatenate.37), channel_id=1, source_target_pairs={{0,16},{4,20},{8,24},{12,28},{16,0},{20,4},{24,8},{28,12},{1,17},{... | collective-permute-start | bytes 835592 | tf_op jit(solution)/shard_map/ppermute | solution.py:94
  144.2 73.9 %all-to-all-start = ((bf16[4,2,768,256]{3,2,1,0:T(8,128)(2,1)}), bf16[4,2,768,256]{3,2,1,0:T(8,128)(2,1)}, u32[]{:S(2)}, u32[]{:S(2)}) async-start(bf16[4,2,768,256]{3,2,1,0:T(8,128)(2,1)} %bitcast.152), calls=%async_computation | async-start | bytes 6291456 | tf_op jit(solution)/shard_map/all_to_all | solution.py:274
  152.1 29.1 %collective-permute-start.13 = (bf16[512,2176]{1,0:T(8,128)(2,1)}, bf16[512,2176]{1,0:T(8,128)(2,1)}, u32[]{:S(2)}, u32[]{:S(2)}) collective-permute-start(bf16[512,2176]{1,0:T(8,128)(2,1)} %pad_maximum_fusion.tok_ref), channel_id=1, source_target_pairs={{0,1},{1,0},{2,3},{3,2},{4,5},{5,4},{6,7},{7,6},{8,9},{9,8},{10,11... | collective-permute-start | bytes 6684680 | tf_op jit(solution)/shard_map/ppermute | solution.py:122
  152.1 9.1 %collective-permute-start.25 = (bf16[2,32,2176]{2,1,0:T(8,128)(2,1)S(1)}, bf16[2,32,2176]{2,1,0:T(8,128)(2,1)S(1)}, u32[]{:S(2)}, u32[]{:S(2)}) collective-permute-start(bf16[2,32,2176]{2,1,0:T(8,128)(2,1)S(1)} %get-tuple-element.70), channel_id=1, source_target_pairs={{0,2},{1,3},{2,0},{3,1},{4,6},{5,7},{6,4},{7,5},{8,10},{9,11},{10,... | collective-permute-start | bytes 835592 | tf_op jit(solution)/shard_map/ppermute | solution.py:117
  153.8 9.2 %collective-permute-start.23 = (bf16[2,32,2176]{2,1,0:T(8,128)(2,1)S(1)}, bf16[2,32,2176]{2,1,0:T(8,128)(2,1)S(1)}, u32[]{:S(2)}, u32[]{:S(2)}) collective-permute-start(bf16[2,32,2176]{2,1,0:T(8,128)(2,1)S(1)} %get-tuple-element.69), channel_id=1, source_target_pairs={{0,4},{4,0},{8,12},{12,8},{16,20},{20,16},{24,28},{28,24},{1,5},{5... | collective-permute-start | bytes 835592 | tf_op jit(solution)/shard_map/ppermute | solution.py:112
  161.3 14.5 %collective-permute-start.26 = (bf16[2,2,32,2176]{3,2,1,0:T(8,128)(2,1)S(1)}, bf16[2,2,32,2176]{3,2,1,0:T(8,128)(2,1)}, u32[]{:S(2)}, u32[]{:S(2)}) collective-permute-start(bf16[2,2,32,2176]{3,2,1,0:T(8,128)(2,1)S(1)} %pad_maximum_fusion.7), channel_id=1, source_target_pairs={{0,4},{4,0},{8,12},{12,8},{16,20},{20,16},{24,28},{28,24},{1,5},{5... | collective-permute-start | bytes 1671176 | tf_op jit(solution)/shard_map/ppermute | solution.py:112
  163.8 14.4 %collective-permute-start.24 = (bf16[2,2,32,2176]{3,2,1,0:T(8,128)(2,1)}, bf16[2,2,32,2176]{3,2,1,0:T(8,128)(2,1)}, u32[]{:S(2)}, u32[]{:S(2)}) collective-permute-start(bf16[2,2,32,2176]{3,2,1,0:T(8,128)(2,1)} %pad_maximum_fusion.6), channel_id=1, source_target_pairs={{0,2},{1,3},{2,0},{3,1},{4,6},{5,7},{6,4},{7,5},{8,10},{9,11},{10,... | collective-permute-start | bytes 1671176 | tf_op jit(solution)/shard_map/ppermute | solution.py:117
  181.2 27.6 %collective-permute-start.27 = (bf16[512,2176]{1,0:T(8,128)(2,1)}, bf16[512,2176]{1,0:T(8,128)(2,1)}, u32[]{:S(2)}, u32[]{:S(2)}) collective-permute-start(bf16[512,2176]{1,0:T(8,128)(2,1)} %pad_maximum_fusion.1.tok_ref), channel_id=1, source_target_pairs={{0,1},{1,0},{2,3},{3,2},{4,5},{5,4},{6,7},{7,6},{8,9},{9,8},{10,11... | collective-permute-start | bytes 6684680 | tf_op jit(solution)/shard_map/ppermute | solution.py:122
  190.0 34.8 %collective-permute-start.14 = (bf16[512,2048]{1,0:T(8,128)(2,1)}, bf16[512,2048]{1,0:T(8,128)(2,1)}, u32[]{:S(2)}, u32[]{:S(2)}) collective-permute-start(bf16[512,2048]{1,0:T(8,128)(2,1)} %shard_map.177), channel_id=1, source_target_pairs={{0,1},{1,0},{2,3},{3,2},{4,5},{5,4},{6,7},{7,6},{8,9},{9,8},{10,11... | collective-permute-start | bytes 6291464 | tf_op jit(solution)/shard_map/ppermute | solution.py:122
  222.8 24.8 %collective-permute-start.35 = (bf16[2,1,768,256]{3,2,1,0:T(8,128)(2,1)}, bf16[2,1,768,256]{3,2,1,0:T(8,128)(2,1)S(1)}, u32[]{:S(2)}, u32[]{:S(2)}) collective-permute-start(bf16[2,1,768,256]{3,2,1,0:T(8,128)(2,1)} %get-tuple-element.53), channel_id=1, source_target_pairs={{0,4},{4,0},{8,12},{12,8},{16,20},{20,16},{24,28},{28,24},{1,5},{5... | collective-permute-start | bytes 2359304 | tf_op jit(solution)/shard_map/ppermute | solution.py:99
  228.3 20.1 %collective-permute-start.15 = (bf16[2,2,32,2048]{3,2,1,0:T(8,128)(2,1)}, bf16[2,2,32,2048]{3,2,1,0:T(8,128)(2,1)S(1)}, u32[]{:S(2)}, u32[]{:S(2)}) collective-permute-start(bf16[2,2,32,2048]{3,2,1,0:T(8,128)(2,1)} %bitcast.47), channel_id=1, source_target_pairs={{0,2},{1,3},{2,0},{3,1},{4,6},{5,7},{6,4},{7,5},{8,10},{9,11},{10,... | collective-permute-start | bytes 1572872 | tf_op jit(solution)/shard_map/ppermute | solution.py:117
  241.7 24.9 %collective-permute-start.28 = (bf16[512,2048]{1,0:T(8,128)(2,1)}, bf16[512,2048]{1,0:T(8,128)(2,1)}, u32[]{:S(2)}, u32[]{:S(2)}) collective-permute-start(bf16[512,2048]{1,0:T(8,128)(2,1)} %shard_map.180), channel_id=1, source_target_pairs={{0,1},{1,0},{2,3},{3,2},{4,5},{5,4},{6,7},{7,6},{8,9},{9,8},{10,11... | collective-permute-start | bytes 6291464 | tf_op jit(solution)/shard_map/ppermute | solution.py:122
  241.7 76.7 %all-to-all-start.1 = ((bf16[4,2,768,256]{3,2,1,0:T(8,128)(2,1)}), bf16[4,2,768,256]{3,2,1,0:T(8,128)(2,1)}, u32[]{:S(2)}, u32[]{:S(2)}) async-start(bf16[4,2,768,256]{3,2,1,0:T(8,128)(2,1)} %bitcast.153), calls=%async_computation.1 | async-start | bytes 6291456 | tf_op jit(solution)/shard_map/all_to_all | solution.py:274
  246.4 15.0 %collective-permute-start.17 = (bf16[2,2,32,2048]{3,2,1,0:T(8,128)(2,1)}, bf16[2,2,32,2048]{3,2,1,0:T(8,128)(2,1)S(1)}, u32[]{:S(2)}, u32[]{:S(2)}) collective-permute-start(bf16[2,2,32,2048]{3,2,1,0:T(8,128)(2,1)} %bitcast.174), channel_id=1, source_target_pairs={{0,4},{4,0},{8,12},{12,8},{16,20},{20,16},{24,28},{28,24},{1,5},{5... | collective-permute-start | bytes 1572872 | tf_op jit(solution)/shard_map/ppermute | solution.py:112
  249.3 17.4 %copy-start.10 = (bf16[512,2048]{1,0:T(8,128)(2,1)S(1)}, bf16[512,2048]{1,0:T(8,128)(2,1)}, u32[]{:S(2)}) copy-start(bf16[512,2048]{1,0:T(8,128)(2,1)} %copy-done.9) | copy-start | bytes 6291460
  250.6 16.0 %collective-permute-start.16 = (bf16[2,32,2048]{2,1,0:T(8,128)(2,1)S(1)}, bf16[2,32,2048]{2,1,0:T(8,128)(2,1)S(1)}, u32[]{:S(2)}, u32[]{:S(2)}) collective-permute-start(bf16[2,32,2048]{2,1,0:T(8,128)(2,1)S(1)} %slice_bitcast_fusion.6), channel_id=1, source_target_pairs={{0,4},{4,0},{8,12},{12,8},{16,20},{20,16},{24,28},{28,24},{1,5},{5... | collective-permute-start | bytes 786440 | tf_op jit(solution)/shard_map/ppermute | solution.py:112
  261.5 8.9 %collective-permute-start.18 = (bf16[2,32,2048]{2,1,0:T(8,128)(2,1)S(1)}, bf16[2,32,2048]{2,1,0:T(8,128)(2,1)S(1)}, u32[]{:S(2)}, u32[]{:S(2)}) collective-permute-start(bf16[2,32,2048]{2,1,0:T(8,128)(2,1)S(1)} %slice_bitcast_fusion.4), channel_id=1, source_target_pairs={{0,2},{1,3},{2,0},{3,1},{4,6},{5,7},{6,4},{7,5},{8,10},{9,11},{10,... | collective-permute-start | bytes 786440 | tf_op jit(solution)/shard_map/ppermute | solution.py:117
  269.2 13.7 %collective-permute-start.29 = (bf16[2,2,32,2048]{3,2,1,0:T(8,128)(2,1)S(1)}, bf16[2,2,32,2048]{3,2,1,0:T(8,128)(2,1)S(1)}, u32[]{:S(2)}, u32[]{:S(2)}) collective-permute-start(bf16[2,2,32,2048]{3,2,1,0:T(8,128)(2,1)S(1)} %bitcast.176), channel_id=1, source_target_pairs={{0,2},{1,3},{2,0},{3,1},{4,6},{5,7},{6,4},{7,5},{8,10},{9,11},{10,... | collective-permute-start | bytes 1572872 | tf_op jit(solution)/shard_map/ppermute | solution.py:117
  271.3 58.0 %collective-permute-start.19 = (bf16[64,2048]{1,0:T(8,128)(2,1)}, bf16[64,2048]{1,0:T(8,128)(2,1)}, u32[]{:S(2)}, u32[]{:S(2)}) collective-permute-start(bf16[64,2048]{1,0:T(8,128)(2,1)} %fusion.36), channel_id=1, source_target_pairs={{0,24},{4,28},{8,0},{12,4},{16,8},{20,12},{24,16},{28,20},{1,25},{... | collective-permute-start | bytes 786440 | tf_op jit(solution)/shard_map/ppermute | solution.py:94
  274.7 14.9 %collective-permute-start.31 = (bf16[2,2,32,2048]{3,2,1,0:T(8,128)(2,1)S(1)}, bf16[2,2,32,2048]{3,2,1,0:T(8,128)(2,1)S(1)}, u32[]{:S(2)}, u32[]{:S(2)}) collective-permute-start(bf16[2,2,32,2048]{3,2,1,0:T(8,128)(2,1)S(1)} %bitcast.175), channel_id=1, source_target_pairs={{0,4},{4,0},{8,12},{12,8},{16,20},{20,16},{24,28},{28,24},{1,5},{5... | collective-permute-start | bytes 1572872 | tf_op jit(solution)/shard_map/ppermute | solution.py:112
  283.1 10.0 %collective-permute-start.30 = (bf16[2,32,2048]{2,1,0:T(8,128)(2,1)S(1)}, bf16[2,32,2048]{2,1,0:T(8,128)(2,1)S(1)}, u32[]{:S(2)}, u32[]{:S(2)}) collective-permute-start(bf16[2,32,2048]{2,1,0:T(8,128)(2,1)S(1)} %slice_bitcast_fusion.2), channel_id=1, source_target_pairs={{0,4},{4,0},{8,12},{12,8},{16,20},{20,16},{24,28},{28,24},{1,5},{5... | collective-permute-start | bytes 786440 | tf_op jit(solution)/shard_map/ppermute | solution.py:112
  289.7 6.4 %collective-permute-start.32 = (bf16[2,32,2048]{2,1,0:T(8,128)(2,1)S(1)}, bf16[2,32,2048]{2,1,0:T(8,128)(2,1)S(1)}, u32[]{:S(2)}, u32[]{:S(2)}) collective-permute-start(bf16[2,32,2048]{2,1,0:T(8,128)(2,1)S(1)} %slice_bitcast_fusion), channel_id=1, source_target_pairs={{0,2},{1,3},{2,0},{3,1},{4,6},{5,7},{6,4},{7,5},{8,10},{9,11},{10,... | collective-permute-start | bytes 786440 | tf_op jit(solution)/shard_map/ppermute | solution.py:117
  320.8 27.8 %copy-start.1 = (bf16[512,2048]{1,0:T(8,128)(2,1)S(1)}, bf16[512,2048]{1,0:T(8,128)(2,1)}, u32[]{:S(2)}) copy-start(bf16[512,2048]{1,0:T(8,128)(2,1)} %param.27) | copy-start | bytes 6291460
  320.8 26.8 %collective-permute-start.36 = (bf16[2,1,768,256]{3,2,1,0:T(8,128)(2,1)S(1)}, bf16[2,1,768,256]{3,2,1,0:T(8,128)(2,1)S(1)}, u32[]{:S(2)}, u32[]{:S(2)}) collective-permute-start(bf16[2,1,768,256]{3,2,1,0:T(8,128)(2,1)S(1)} %get-tuple-element.51), channel_id=1, source_target_pairs={{0,4},{4,0},{8,12},{12,8},{16,20},{20,16},{24,28},{28,24},{1,5},{5... | collective-permute-start | bytes 2359304 | tf_op jit(solution)/shard_map/ppermute | solution.py:99
  322.0 14.0 %collective-permute-start.34 = (bf16[64,2048]{1,0:T(8,128)(2,1)S(1)}, bf16[64,2048]{1,0:T(8,128)(2,1)S(1)}, u32[]{:S(2)}, u32[]{:S(2)}) collective-permute-start(bf16[64,2048]{1,0:T(8,128)(2,1)S(1)} %get-tuple-element.72), channel_id=1, source_target_pairs={{0,8},{4,12},{8,16},{12,20},{16,24},{20,28},{24,0},{28,4},{1,9},{5... | collective-permute-start | bytes 786440 | tf_op jit(solution)/shard_map/ppermute | solution.py:94
  325.9 20.0 %collective-permute-start.33 = (bf16[64,2048]{1,0:T(8,128)(2,1)S(1)}, bf16[64,2048]{1,0:T(8,128)(2,1)S(1)}, u32[]{:S(2)}, u32[]{:S(2)}) collective-permute-start(bf16[64,2048]{1,0:T(8,128)(2,1)S(1)} %get-tuple-element.71), channel_id=1, source_target_pairs={{0,16},{4,20},{8,24},{12,28},{16,0},{20,4},{24,8},{28,12},{1,17},{... | collective-permute-start | bytes 786440 | tf_op jit(solution)/shard_map/ppermute | solution.py:94
  (23 other events, 110.9 us)

commit v2 on v0

--- a/solution.py
+++ b/solution.py
@@ -197,7 +197,7 @@
         pieces.append(turn_pairs(source, step))
     outgoing = pick_first(held)
     outgoing = after(outgoing, *pieces[1:])
-    *pieces[2:], outgoing = together(*pieces[2:], outgoing)
+    *pieces, outgoing = together(*pieces, outgoing)
     arrived = trade_columns(outgoing)
     total = None
     for begin in range(0, pair_count, 2):
@@ -213,7 +213,7 @@
             part = sums[offset] if step == 0 else turn_pairs(sums[offset], -step)
             part = part.astype(jnp.float32)
             total = part if total is None else total + part
-    return total, arrived
+    return total, arrived, mixed
 
 
 def spread_weights(slot_weights):
@@ -399,12 +399,14 @@
     source_slot = jnp.sum(jnp.where(replica_onehot, slot_of[None, :], 0), axis=1)
     slots_here = slot_weights.shape[0]
     index = chunk_index(source_slot, slots_here)
-    size = held[0].shape[1] // 2
-    mixture, first = mix(
+    last = held[0].shape[1] // 3
+    size = held[0].shape[1] - last
+    mixture, first, mixed = mix(
         normed, codes, slot_weights, held, lambda held: take_chunks(held, index, 0, size)
     )
     layer_out = (residual + mixture).astype(jnp.bfloat16)
-    second = trade_columns(after(take_chunks(held, index, size, size), first))
+    second = trade_columns(after(take_chunks(held, index, size, last), first))
+    first = after(first, mixed)
     replica_weights = collect_replicas((first, second), source_slot, slots_here)
     return (layer_out, replica_weights.reshape((1,) + slot_weights.shape[1:]))
 

time: 298 us -> 335 us (1.12)
  waiting for transfers between devices: 130 us -> 173 us
  starting transfers between devices: 62.8 us -> 54.5 us
  local copies, waits for them, and re-layouts: 31.4 us -> 35.3 us
    all_to_all x2, waiting for transfers between devices: 17 us -> 40 us  [trade_columns(): lax.all_to_all(outgoing, 'req', 0, 0, axis_index_groups=columns, tiled=True)]
    ppermute x9, waiting for transfers between devices: 18.9 us -> 40.8 us  [flip_chip(): return lax.ppermute(value, 'exp', [(i, i ^ 2) for i in range(count)])]
    ppermute x9, starting transfers between devices: 22.3 us -> 15.3 us  [turn_pairs(): lax.ppermute(value, 'req', [(i, (i + 2 * step) % count) for i in range(co...]
    ppermute x9, waiting for transfers between devices: 49 us -> 55.2 us  [flip_pair(): return lax.ppermute(value, 'req', [(i, i ^ 1) for i in range(count)])]
    ppermute x9, waiting for transfers between devices: 14.7 us -> 10.7 us  [turn_pairs(): lax.ppermute(value, 'req', [(i, (i + 2 * step) % count) for i in range(co...]
    unnamed x57 -> x59, local copies, waits for them, and re-layouts: 12.9 us -> 15.3 us
  transfers between devices with their start and end apart: 39 -> 39, of which waited for: 16 -> 19; matrix products, arithmetic and copies ran while one was open for 16% -> 14% of each run, Pallas kernels for 11% -> 9%
where the time goes in v2:
time: 335 us; the launch traced here: 334 us
  waiting for transfers between devices  173 us (52%)
  starting transfers between devices  54.5 us (16%)
  local copies, waits for them, and re-layouts  35.3 us (11%)
  Pallas kernels  31.1 us (9%)
  other arithmetic  24.9 us (7%)
  between operations  9.84 us (3%)
  matrix products  5.11 us (2%)
    ppermute x9, waiting for transfers between devices, flip_pair(): return lax.ppermute(value, 'req', [(i, i ^ 1) for i in range(count)])  55.2 us
    ppermute x9, waiting for transfers between devices, flip_chip(): return lax.ppermute(value, 'exp', [(i, i ^ 2) for i in range(count)])  40.8 us
    all_to_all x2, waiting for transfers between devices, trade_columns(): lax.all_to_all(outgoing, 'req', 0, 0, axis_index_groups=columns, tiled=True)  40 us
    ppermute x5, waiting for transfers between devices, swap(): return lax.ppermute(value, 'req', [(i, i ^ mask) for i in range(count)])  26.6 us
    pallas_call x4, Pallas kernels, run_experts(): pl.pallas_call(experts_kernel, out_shape=jax.ShapeDtypeStruct((count, wid...  21.4 us
    ppermute x9, starting transfers between devices, turn_pairs(): lax.ppermute(value, 'req', [(i, (i + 2 * step) % count) for i in range(co...  15.3 us
    unnamed x59, local copies, waits for them, and re-layouts  15.3 us
    ppermute x9, starting transfers between devices, flip_chip(): return lax.ppermute(value, 'exp', [(i, i ^ 2) for i in range(count)])  11.2 us
  transfers between devices with their start and end apart: 39, of which 19 were waited for; matrix products, arithmetic and copies ran while one was open for 14% of the time, Pallas kernels for 9%

profile of v2, /device:TPU:0, one launch (start us, length us, event | category | flops | bytes accessed | tf_op | source)
XLA Modules:
  0.0 334.1 jit_solution(7497851569478697096)
XLA Ops:
  0.6 1.7 fusion.69
  2.3 5.0 %collective-permute-start.2 = (bf16[2,2,32,512]{3,2,1,0:T(8,128)(2,1)}, bf16[2,2,32,512]{3,2,1,0:T(8,128)(2,1)}, u32[]{:S(2)}, u32[]{:S(2)}) collective-permute-start(bf16[2,2,32,512]{3,2,1,0:T(8,128)(2,1)} %get-tuple-element.86), channel_id=1, source_target_pairs={{0,24},{4,28},{8,0},{12,4},{16,8},{20,12},{24,16},{28,20},{1,25},{... | collective-permute-start | bytes 393224 | tf_op jit(solution)/shard_map/ppermute | solution.py:94
  8.4 5.7 %dynamic-slice_bitcast_fusion = (bf16[2,1536,256]{2,1,0:T(8,128)(2,1)}, bf16[2,1536,256]{2,1,0:T(8,128)(2,1)}, bf16[2,1536,256]{2,1,0:T(8,128)(2,1)}, bf16[2,1536,256]{2,1,0:T(8,128)(2,1)}) fusion(bf16[2,4,1536,256]{3,2,1,0:T(8,128)(2,1)} %bitcast.153, s32[]{:T(128)S(6)} %select_n.262, s32[]{:T(128)S(6)} %select_n.256, s32[]{:T(128)S(6)} %select_n.248, ...), kind=kLoop, calls=%fused_computation.6 | loop fusion | bytes 12582928 | tf_op jit(solution)/shard_map/jit(dynamic_index_in_dim)/squeeze | solution.py:126
  15.6 2.5 collective-permute-start.5
  37.3 15.1 %collective-permute-done.3 = bf16[2,2,32,512]{3,2,1,0:T(8,128)(2,1)S(1)} collective-permute-done((bf16[2,2,32,512]{3,2,1,0:T(8,128)(2,1)S(1)}, bf16[2,2,32,512]{3,2,1,0:T(8,128)(2,1)S(1)}, u32[]{:S(2)}, u32[]{:S(2)}) %collective-permute-start.3) | collective-permute-done | bytes 131104 | tf_op jit(solution)/shard_map/ppermute | solution.py:112
  52.6 2.7 fusion.78
  55.4 1.7 convolution_convert_fusion
  59.3 3.5 %collective-permute-start.9 = (bf16[2,1536,256]{2,1,0:T(8,128)(2,1)}, bf16[2,1536,256]{2,1,0:T(8,128)(2,1)}, u32[]{:S(2)}, u32[]{:S(2)}) collective-permute-start(bf16[2,1536,256]{2,1,0:T(8,128)(2,1)} %get-tuple-element.52), channel_id=1, source_target_pairs={{0,12},{4,8},{8,4},{12,0},{16,28},{20,24},{24,20},{28,16},{1,13},{... | collective-permute-start | bytes 4718600 | tf_op jit(solution)/shard_map/ppermute | solution.py:99
  65.3 1.6 collective-permute-start.7
  67.4 6.3 %collective-permute-done.7 = bf16[64,2048]{1,0:T(8,128)(2,1)S(1)} collective-permute-done((bf16[64,2048]{1,0:T(8,128)(2,1)S(1)}, bf16[64,2048]{1,0:T(8,128)(2,1)S(1)}, u32[]{:S(2)}, u32[]{:S(2)}) %collective-permute-start.7) | collective-permute-done | bytes 262176 | tf_op jit(solution)/shard_map/ppermute | solution.py:117
  76.0 3.1 collective-permute-start.11
  79.1 19.3 %collective-permute-done.9.refs_3_ = bf16[2,1536,256]{2,1,0:T(8,128)(2,1)} collective-permute-done((bf16[2,1536,256]{2,1,0:T(8,128)(2,1)}, bf16[2,1536,256]{2,1,0:T(8,128)(2,1)}, u32[]{:S(2)}, u32[]{:S(2)}) %collective-permute-start.9) | collective-permute-done | bytes 1572896 | tf_op jit(solution)/shard_map/ppermute | solution.py:99
  98.4 1.6 collective-permute-start.10
  100.0 4.1 %shard_map.176 = bf16[8,1024,256]{2,1,0:T(8,128)(2,1)S(1)} custom-call(s32[8]{0:T(128)S(1)} %fusion.50.index_ref, bf16[2,1536,256]{2,1,0:T(8,128)(2,1)S(1)} %copy-done.3, bf16[2,1536,256]{2,1,0:T(8,128)(2,1)} %collective-permute-done.4.refs_1_, bf16[2,1536,256]{2,1,0:T(8,128)(2,1)} %collective-permute-done.5.refs_2_, ...), custom_call_target="tpu_custom_call" | custom-call | bytes 8388608 | tf_op jit(solution)/shard_map/pallas_call | solution.py:253
  104.2 2.0 copy-done.2
  106.2 9.0 %collective-permute-done.10 = bf16[64,2176]{1,0:T(8,128)(2,1)S(1)} collective-permute-done((bf16[64,2176]{1,0:T(8,128)(2,1)S(1)}, bf16[64,2176]{1,0:T(8,128)(2,1)S(1)}, u32[]{:S(2)}, u32[]{:S(2)}) %collective-permute-start.10) | collective-permute-done | bytes 278560 | tf_op jit(solution)/shard_map/ppermute | solution.py:94
  115.3 1.6 collective-permute-start.14
  118.1 5.5 %collective-permute-done.14 = bf16[2,32,2176]{2,1,0:T(8,128)(2,1)S(1)} collective-permute-done((bf16[2,32,2176]{2,1,0:T(8,128)(2,1)S(1)}, bf16[2,32,2176]{2,1,0:T(8,128)(2,1)S(1)}, u32[]{:S(2)}, u32[]{:S(2)}) %collective-permute-start.14) | collective-permute-done | bytes 278560 | tf_op jit(solution)/shard_map/ppermute | solution.py:117
  126.8 10.2 %collective-permute-done.15 = bf16[2,2,32,2176]{3,2,1,0:T(8,128)(2,1)S(1)} collective-permute-done((bf16[2,2,32,2176]{3,2,1,0:T(8,128)(2,1)S(1)}, bf16[2,2,32,2176]{3,2,1,0:T(8,128)(2,1)S(1)}, u32[]{:S(2)}, u32[]{:S(2)}) %collective-permute-start.15) | collective-permute-done | bytes 557088 | tf_op jit(solution)/shard_map/ppermute | solution.py:112
  138.5 1.6 pad_maximum_fusion.tok_ref
  140.2 1.6 collective-permute-start.25
  142.1 5.0 %all-to-all-start = ((bf16[4,2,1024,256]{3,2,1,0:T(8,128)(2,1)}), bf16[4,2,1024,256]{3,2,1,0:T(8,128)(2,1)}, u32[]{:S(2)}, u32[]{:S(2)}) async-start(bf16[4,2,1024,256]{3,2,1,0:T(8,128)(2,1)} %bitcast.152), calls=%async_computation | async-start | bytes 8388608 | tf_op jit(solution)/shard_map/all_to_all | solution.py:273
  147.1 2.2 collective-permute-done.25
  150.5 2.8 copy-done.5
  153.2 5.1 %shard_map.178 = bf16[512,2048]{1,0:T(8,128)(2,1)S(1)} custom-call(s32[1]{0:T(128)} %bitcast.35.first_slot_ref, bf16[512,2176]{1,0:T(8,128)(2,1)} %collective-permute-done.16.tok_ref, bf16[2,3,2048,256]{3,2,1,0:T(8,128)(2,1)S(1)} %copy-done.5), custom_call_target="tpu_custom_call" | custom-call | flops 3221225472 | bytes 10485760 | tf_op jit(solution)/shard_map/pallas_call | solution.py:73
  159.4 4.3 %collective-permute-done.26 = bf16[2,2,32,2176]{3,2,1,0:T(8,128)(2,1)S(1)} collective-permute-done((bf16[2,2,32,2176]{3,2,1,0:T(8,128)(2,1)S(1)}, bf16[2,2,32,2176]{3,2,1,0:T(8,128)(2,1)S(1)}, u32[]{:S(2)}, u32[]{:S(2)}) %collective-permute-start.26) | collective-permute-done | bytes 557088 | tf_op jit(solution)/shard_map/ppermute | solution.py:112
  163.7 9.9 %collective-permute-done.24 = bf16[2,2,32,2176]{3,2,1,0:T(8,128)(2,1)S(1)} collective-permute-done((bf16[2,2,32,2176]{3,2,1,0:T(8,128)(2,1)S(1)}, bf16[2,2,32,2176]{3,2,1,0:T(8,128)(2,1)S(1)}, u32[]{:S(2)}, u32[]{:S(2)}) %collective-permute-start.24) | collective-permute-done | bytes 557088 | tf_op jit(solution)/shard_map/ppermute | solution.py:117
  175.1 5.1 %shard_map.177 = bf16[512,2048]{1,0:T(8,128)(2,1)S(1)} custom-call(s32[1]{0:T(128)} %bitcast.35.first_slot_ref, bf16[512,2176]{1,0:T(8,128)(2,1)} %pad_maximum_fusion.tok_ref, bf16[2,3,2048,256]{3,2,1,0:T(8,128)(2,1)S(1)} %copy-done.5), custom_call_target="tpu_custom_call" | custom-call | flops 3221225472 | bytes 10485760 | tf_op jit(solution)/shard_map/pallas_call | solution.py:73
  186.5 5.6 %shard_map.181 = bf16[8,512,256]{2,1,0:T(8,128)(2,1)} custom-call(s32[8]{0:T(128)S(1)} %fusion.50.index_ref, bf16[2,1536,256]{2,1,0:T(8,128)(2,1)S(1)} %copy-done.4, bf16[2,1536,256]{2,1,0:T(8,128)(2,1)} %collective-permute-done.4.refs_1_, bf16[2,1536,256]{2,1,0:T(8,128)(2,1)} %collective-permute-done.5.refs_2_, ...), custom_call_target="tpu_custom_call" | custom-call | bytes 4194304 | tf_op jit(solution)/shard_map/pallas_call | solution.py:253
  192.2 2.8 copy-done.6
  194.9 6.1 %shard_map.180 = bf16[512,2048]{1,0:T(8,128)(2,1)} custom-call(s32[1]{0:T(128)} %bitcast.35.first_slot_ref, bf16[512,2176]{1,0:T(8,128)(2,1)} %collective-permute-done.27.tok_ref, bf16[2,3,2048,256]{3,2,1,0:T(8,128)(2,1)S(1)} %copy-done.6), custom_call_target="tpu_custom_call" | custom-call | flops 3221225472 | bytes 10485760 | tf_op jit(solution)/shard_map/pallas_call | solution.py:73
  204.6 11.5 %collective-permute-done.18 = bf16[2,2,32,2048]{3,2,1,0:T(8,128)(2,1)S(1)} collective-permute-done((bf16[2,2,32,2048]{3,2,1,0:T(8,128)(2,1)S(1)}, bf16[2,2,32,2048]{3,2,1,0:T(8,128)(2,1)S(1)}, u32[]{:S(2)}, u32[]{:S(2)}) %collective-permute-start.18) | collective-permute-done | bytes 524320 | tf_op jit(solution)/shard_map/ppermute | solution.py:117
  216.2 1.7 collective-permute-start.19
  217.9 3.1 collective-permute-done.21
  221.1 20.3 %all-to-all-done = bf16[4,2,1024,256]{3,2,1,0:T(8,128)(2,1)} async-done(((bf16[4,2,1024,256]{3,2,1,0:T(8,128)(2,1)}), bf16[4,2,1024,256]{3,2,1,0:T(8,128)(2,1)}, u32[]{:S(2)}, u32[]{:S(2)}) %all-to-all-start) | async-done | bytes 4194336 | tf_op jit(solution)/shard_map/all_to_all | solution.py:273
  241.4 2.8 copy-done.7
  244.2 5.1 %shard_map.179 = bf16[512,2048]{1,0:T(8,128)(2,1)S(1)} custom-call(s32[1]{0:T(128)} %bitcast.35.first_slot_ref, bf16[512,2176]{1,0:T(8,128)(2,1)} %pad_maximum_fusion.1.tok_ref, bf16[2,3,2048,256]{3,2,1,0:T(8,128)(2,1)S(1)} %copy-done.7), custom_call_target="tpu_custom_call" | custom-call | flops 3221225472 | bytes 10485760 | tf_op jit(solution)/shard_map/pallas_call | solution.py:73
  249.3 2.4 add_convert_fusion
  255.7 4.5 %all-to-all-start.1 = ((bf16[4,2,512,256]{3,2,1,0:T(8,128)(2,1)}), bf16[4,2,512,256]{3,2,1,0:T(8,128)(2,1)}, u32[]{:S(2)}, u32[]{:S(2)}) async-start(bf16[4,2,512,256]{3,2,1,0:T(8,128)(2,1)} %bitcast.81), calls=%async_computation.1 | async-start | bytes 4194304 | tf_op jit(solution)/shard_map/all_to_all | solution.py:273
  260.2 1.9 broadcast_in_dim.162
  262.1 2.6 constant_dynamic-slice_fusion.1
  267.0 1.8 collective-permute-done.31
  271.4 23.8 %collective-permute-done.30 = bf16[2,32,2048]{2,1,0:T(8,128)(2,1)S(1)} collective-permute-done((bf16[2,32,2048]{2,1,0:T(8,128)(2,1)S(1)}, bf16[2,32,2048]{2,1,0:T(8,128)(2,1)S(1)}, u32[]{:S(2)}, u32[]{:S(2)}) %collective-permute-start.30) | collective-permute-done | bytes 262176 | tf_op jit(solution)/shard_map/ppermute | solution.py:112
  299.7 19.7 %all-to-all-done.1 = bf16[4,2,512,256]{3,2,1,0:T(8,128)(2,1)} async-done(((bf16[4,2,512,256]{3,2,1,0:T(8,128)(2,1)}), bf16[4,2,512,256]{3,2,1,0:T(8,128)(2,1)}, u32[]{:S(2)}, u32[]{:S(2)}) %all-to-all-start.1) | async-done | bytes 2097184 | tf_op jit(solution)/shard_map/all_to_all | solution.py:273
  319.4 2.1 constant_dynamic-slice_fusion
  322.4 1.6 collective-permute-done.33
  324.0 2.0 fusion.14
  325.9 7.4 %collective-permute-done.36 = bf16[2,1,512,256]{3,2,1,0:T(8,128)(2,1)S(1)} collective-permute-done((bf16[2,1,512,256]{3,2,1,0:T(8,128)(2,1)S(1)}, bf16[2,1,512,256]{3,2,1,0:T(8,128)(2,1)S(1)}, u32[]{:S(2)}, u32[]{:S(2)}) %collective-permute-start.36) | collective-permute-done | bytes 524320 | tf_op jit(solution)/shard_map/ppermute | solution.py:99
  (190 shorter events, 55.9 us)
Async XLA Ops:
  0.6 56.4 %copy-start = (bf16[512,2048]{1,0:T(8,128)(2,1)S(1)}, bf16[512,2048]{1,0:T(8,128)(2,1)}, u32[]{:S(2)}) copy-start(bf16[512,2048]{1,0:T(8,128)(2,1)} %param.27) | copy-start | bytes 6291460
  2.3 33.1 %collective-permute-start.2 = (bf16[2,2,32,512]{3,2,1,0:T(8,128)(2,1)}, bf16[2,2,32,512]{3,2,1,0:T(8,128)(2,1)}, u32[]{:S(2)}, u32[]{:S(2)}) collective-permute-start(bf16[2,2,32,512]{3,2,1,0:T(8,128)(2,1)} %get-tuple-element.86), channel_id=1, source_target_pairs={{0,24},{4,28},{8,0},{12,4},{16,8},{20,12},{24,16},{28,20},{1,25},{... | collective-permute-start | bytes 393224 | tf_op jit(solution)/shard_map/ppermute | solution.py:94
  7.4 28.1 %collective-permute-start.1 = (bf16[2,2,32,512]{3,2,1,0:T(8,128)(2,1)}, bf16[2,2,32,512]{3,2,1,0:T(8,128)(2,1)}, u32[]{:S(2)}, u32[]{:S(2)}) collective-permute-start(bf16[2,2,32,512]{3,2,1,0:T(8,128)(2,1)} %get-tuple-element.86), channel_id=1, source_target_pairs={{0,16},{4,20},{8,24},{12,28},{16,0},{20,4},{24,8},{28,12},{1,17},{... | collective-permute-start | bytes 393224 | tf_op jit(solution)/shard_map/ppermute | solution.py:94
  7.4 28.1 %collective-permute-start = (bf16[2,2,32,512]{3,2,1,0:T(8,128)(2,1)}, bf16[2,2,32,512]{3,2,1,0:T(8,128)(2,1)}, u32[]{:S(2)}, u32[]{:S(2)}) collective-permute-start(bf16[2,2,32,512]{3,2,1,0:T(8,128)(2,1)} %get-tuple-element.86), channel_id=1, source_target_pairs={{0,8},{4,12},{8,16},{12,20},{16,24},{20,28},{24,0},{28,4},{1,9},{5... | collective-permute-start | bytes 393224 | tf_op jit(solution)/shard_map/ppermute | solution.py:94
  8.4 10.2 %copy-start.25 = (s32[1,4]{1,0:T(1,128)S(1)}, s32[1,4]{1,0:T(1,128)}, u32[]{:S(2)}) copy-start(s32[1,4]{1,0:T(1,128)} %param.26) | copy-start | bytes 52
  8.4 11.5 %copy-start.21 = (s32[32]{0:T(128)S(1)}, s32[32]{0:T(128)}, u32[]{:S(2)}) copy-start(s32[32]{0:T(128)} %param.25) | copy-start | bytes 388
  8.4 13.9 %copy-start.14 = (bf16[256,512]{1,0:T(8,128)(2,1)S(1)}, bf16[256,512]{1,0:T(8,128)(2,1)}, u32[]{:S(2)}) copy-start(bf16[256,512]{1,0:T(8,128)(2,1)} %param.19) | copy-start | bytes 786436
  8.4 14.3 %copy-start.15 = (bf16[256,512]{1,0:T(8,128)(2,1)S(1)}, bf16[256,512]{1,0:T(8,128)(2,1)}, u32[]{:S(2)}) copy-start(bf16[256,512]{1,0:T(8,128)(2,1)} %param.18) | copy-start | bytes 786436
  14.1 42.9 %collective-permute-start.4 = (bf16[2,1536,256]{2,1,0:T(8,128)(2,1)}, bf16[2,1536,256]{2,1,0:T(8,128)(2,1)}, u32[]{:S(2)}, u32[]{:S(2)}) collective-permute-start(bf16[2,1536,256]{2,1,0:T(8,128)(2,1)} %get-tuple-element.54), channel_id=1, source_target_pairs={{0,4},{4,0},{8,12},{12,8},{16,20},{20,16},{24,28},{28,24},{1,5},{5... | collective-permute-start | bytes 4718600 | tf_op jit(solution)/shard_map/ppermute | solution.py:99
  15.6 41.4 %collective-permute-start.5 = (bf16[2,1536,256]{2,1,0:T(8,128)(2,1)}, bf16[2,1536,256]{2,1,0:T(8,128)(2,1)}, u32[]{:S(2)}, u32[]{:S(2)}) collective-permute-start(bf16[2,1536,256]{2,1,0:T(8,128)(2,1)} %get-tuple-element.53), channel_id=1, source_target_pairs={{0,8},{4,12},{8,0},{12,4},{16,24},{20,28},{24,16},{28,20},{1,9},{5... | collective-permute-start | bytes 4718600 | tf_op jit(solution)/shard_map/ppermute | solution.py:99
  36.6 15.8 %collective-permute-start.3 = (bf16[2,2,32,512]{3,2,1,0:T(8,128)(2,1)S(1)}, bf16[2,2,32,512]{3,2,1,0:T(8,128)(2,1)S(1)}, u32[]{:S(2)}, u32[]{:S(2)}) collective-permute-start(bf16[2,2,32,512]{3,2,1,0:T(8,128)(2,1)S(1)} %pad_maximum_fusion.12), channel_id=1, source_target_pairs={{0,4},{4,0},{8,12},{12,8},{16,20},{20,16},{24,28},{28,24},{1,5},{5... | collective-permute-start | bytes 393224 | tf_op jit(solution)/shard_map/ppermute | solution.py:112
  57.9 15.9 %copy-start.17 = (bf16[64,2048]{1,0:T(8,128)(2,1)S(1)}, bf16[64,2048]{1,0:T(8,128)(2,1)}, u32[]{:S(2)}) copy-start(bf16[64,2048]{1,0:T(8,128)(2,1)} %param.17) | copy-start | bytes 786436
  59.2 3.7 %collective-permute-start.6 = (bf16[2,64,2048]{2,1,0:T(8,128)(2,1)S(1)}, bf16[2,64,2048]{2,1,0:T(8,128)(2,1)S(1)}, u32[]{:S(2)}, u32[]{:S(2)}) collective-permute-start(bf16[2,64,2048]{2,1,0:T(8,128)(2,1)S(1)} %fusion.8), channel_id=1, source_target_pairs={{0,1},{1,0},{2,3},{3,2},{4,5},{5,4},{6,7},{7,6},{8,9},{9,8},{10,11... | collective-permute-start | bytes 1572872 | tf_op jit(solution)/shard_map/ppermute | solution.py:122
  59.3 39.1 %collective-permute-start.9 = (bf16[2,1536,256]{2,1,0:T(8,128)(2,1)}, bf16[2,1536,256]{2,1,0:T(8,128)(2,1)}, u32[]{:S(2)}, u32[]{:S(2)}) collective-permute-start(bf16[2,1536,256]{2,1,0:T(8,128)(2,1)} %get-tuple-element.52), channel_id=1, source_target_pairs={{0,12},{4,8},{8,4},{12,0},{16,28},{20,24},{24,20},{28,16},{1,13},{... | collective-permute-start | bytes 4718600 | tf_op jit(solution)/shard_map/ppermute | solution.py:99
  62.9 12.1 %copy-start.18 = (f32[2048]{0:T(1024)S(1)}, f32[2048]{0:T(1024)}, u32[]{:S(2)}) copy-start(f32[2048]{0:T(1024)} %param.28) | copy-start | bytes 24580
  65.2 34.8 %copy-start.3 = (bf16[2,1536,256]{2,1,0:T(8,128)(2,1)S(1)}, bf16[2,1536,256]{2,1,0:T(8,128)(2,1)}, u32[]{:S(2)}) copy-start(bf16[2,1536,256]{2,1,0:T(8,128)(2,1)} %get-tuple-element.51.refs_0_) | copy-start | bytes 4718596
  65.3 8.4 %collective-permute-start.7 = (bf16[64,2048]{1,0:T(8,128)(2,1)S(1)}, bf16[64,2048]{1,0:T(8,128)(2,1)S(1)}, u32[]{:S(2)}, u32[]{:S(2)}) collective-permute-start(bf16[64,2048]{1,0:T(8,128)(2,1)S(1)} %fusion.28), channel_id=1, source_target_pairs={{0,2},{1,3},{2,0},{3,1},{4,6},{5,7},{6,4},{7,5},{8,10},{9,11},{10,... | collective-permute-start | bytes 786440 | tf_op jit(solution)/shard_map/ppermute | solution.py:117
  75.2 31.0 %collective-permute-start.8 = (bf16[64,2176]{1,0:T(8,128)(2,1)S(1)}, bf16[64,2176]{1,0:T(8,128)(2,1)S(1)}, u32[]{:S(2)}, u32[]{:S(2)}) collective-permute-start(bf16[64,2176]{1,0:T(8,128)(2,1)S(1)} %concatenate.37), channel_id=1, source_target_pairs={{0,8},{4,12},{8,16},{12,20},{16,24},{20,28},{24,0},{28,4},{1,9},{5... | collective-permute-start | bytes 835592 | tf_op jit(solution)/shard_map/ppermute | solution.py:94
  76.0 39.2 %collective-permute-start.11 = (bf16[64,2176]{1,0:T(8,128)(2,1)S(1)}, bf16[64,2176]{1,0:T(8,128)(2,1)S(1)}, u32[]{:S(2)}, u32[]{:S(2)}) collective-permute-start(bf16[64,2176]{1,0:T(8,128)(2,1)S(1)} %concatenate.37), channel_id=1, source_target_pairs={{0,24},{4,28},{8,0},{12,4},{16,8},{20,12},{24,16},{28,20},{1,25},{... | collective-permute-start | bytes 835592 | tf_op jit(solution)/shard_map/ppermute | solution.py:94
  98.4 16.9 %collective-permute-start.10 = (bf16[64,2176]{1,0:T(8,128)(2,1)S(1)}, bf16[64,2176]{1,0:T(8,128)(2,1)S(1)}, u32[]{:S(2)}, u32[]{:S(2)}) collective-permute-start(bf16[64,2176]{1,0:T(8,128)(2,1)S(1)} %concatenate.37), channel_id=1, source_target_pairs={{0,16},{4,20},{8,24},{12,28},{16,0},{20,4},{24,8},{28,12},{1,17},{... | collective-permute-start | bytes 835592 | tf_op jit(solution)/shard_map/ppermute | solution.py:94
  115.3 8.3 %collective-permute-start.14 = (bf16[2,32,2176]{2,1,0:T(8,128)(2,1)S(1)}, bf16[2,32,2176]{2,1,0:T(8,128)(2,1)S(1)}, u32[]{:S(2)}, u32[]{:S(2)}) collective-permute-start(bf16[2,32,2176]{2,1,0:T(8,128)(2,1)S(1)} %get-tuple-element.72), channel_id=1, source_target_pairs={{0,2},{1,3},{2,0},{3,1},{4,6},{5,7},{6,4},{7,5},{8,10},{9,11},{10,... | collective-permute-start | bytes 835592 | tf_op jit(solution)/shard_map/ppermute | solution.py:117
  116.8 8.3 %collective-permute-start.12 = (bf16[2,32,2176]{2,1,0:T(8,128)(2,1)S(1)}, bf16[2,32,2176]{2,1,0:T(8,128)(2,1)S(1)}, u32[]{:S(2)}, u32[]{:S(2)}) collective-permute-start(bf16[2,32,2176]{2,1,0:T(8,128)(2,1)S(1)} %get-tuple-element.71), channel_id=1, source_target_pairs={{0,4},{4,0},{8,12},{12,8},{16,20},{20,16},{24,28},{28,24},{1,5},{5... | collective-permute-start | bytes 835592 | tf_op jit(solution)/shard_map/ppermute | solution.py:112
  123.6 13.4 %collective-permute-start.15 = (bf16[2,2,32,2176]{3,2,1,0:T(8,128)(2,1)S(1)}, bf16[2,2,32,2176]{3,2,1,0:T(8,128)(2,1)S(1)}, u32[]{:S(2)}, u32[]{:S(2)}) collective-permute-start(bf16[2,2,32,2176]{3,2,1,0:T(8,128)(2,1)S(1)} %pad_maximum_fusion.3), channel_id=1, source_target_pairs={{0,4},{4,0},{8,12},{12,8},{16,20},{20,16},{24,28},{28,24},{1,5},{5... | collective-permute-start | bytes 1671176 | tf_op jit(solution)/shard_map/ppermute | solution.py:112
  125.2 13.3 %collective-permute-start.13 = (bf16[2,2,32,2176]{3,2,1,0:T(8,128)(2,1)S(1)}, bf16[2,2,32,2176]{3,2,1,0:T(8,128)(2,1)S(1)}, u32[]{:S(2)}, u32[]{:S(2)}) collective-permute-start(bf16[2,2,32,2176]{3,2,1,0:T(8,128)(2,1)S(1)} %pad_maximum_fusion.2), channel_id=1, source_target_pairs={{0,2},{1,3},{2,0},{3,1},{4,6},{5,7},{6,4},{7,5},{8,10},{9,11},{10,... | collective-permute-start | bytes 1671176 | tf_op jit(solution)/shard_map/ppermute | solution.py:117
  140.1 10.4 %collective-permute-start.16 = (bf16[512,2176]{1,0:T(8,128)(2,1)}, bf16[512,2176]{1,0:T(8,128)(2,1)}, u32[]{:S(2)}, u32[]{:S(2)}) collective-permute-start(bf16[512,2176]{1,0:T(8,128)(2,1)} %pad_maximum_fusion.tok_ref), channel_id=1, source_target_pairs={{0,1},{1,0},{2,3},{3,2},{4,5},{5,4},{6,7},{7,6},{8,9},{9,8},{10,11... | collective-permute-start | bytes 6684680 | tf_op jit(solution)/shard_map/ppermute | solution.py:122
  140.2 9.1 %collective-permute-start.25 = (bf16[2,32,2176]{2,1,0:T(8,128)(2,1)S(1)}, bf16[2,32,2176]{2,1,0:T(8,128)(2,1)S(1)}, u32[]{:S(2)}, u32[]{:S(2)}) collective-permute-start(bf16[2,32,2176]{2,1,0:T(8,128)(2,1)S(1)} %get-tuple-element.74), channel_id=1, source_target_pairs={{0,2},{1,3},{2,0},{3,1},{4,6},{5,7},{6,4},{7,5},{8,10},{9,11},{10,... | collective-permute-start | bytes 835592 | tf_op jit(solution)/shard_map/ppermute | solution.py:117
  141.7 16.7 %collective-permute-start.23 = (bf16[2,32,2176]{2,1,0:T(8,128)(2,1)S(1)}, bf16[2,32,2176]{2,1,0:T(8,128)(2,1)S(1)}, u32[]{:S(2)}, u32[]{:S(2)}) collective-permute-start(bf16[2,32,2176]{2,1,0:T(8,128)(2,1)S(1)} %get-tuple-element.73), channel_id=1, source_target_pairs={{0,4},{4,0},{8,12},{12,8},{16,20},{20,16},{24,28},{28,24},{1,5},{5... | collective-permute-start | bytes 835592 | tf_op jit(solution)/shard_map/ppermute | solution.py:112
  142.1 99.3 %all-to-all-start = ((bf16[4,2,1024,256]{3,2,1,0:T(8,128)(2,1)}), bf16[4,2,1024,256]{3,2,1,0:T(8,128)(2,1)}, u32[]{:S(2)}, u32[]{:S(2)}) async-start(bf16[4,2,1024,256]{3,2,1,0:T(8,128)(2,1)} %bitcast.152), calls=%async_computation | async-start | bytes 8388608 | tf_op jit(solution)/shard_map/all_to_all | solution.py:273
  149.4 14.3 %collective-permute-start.26 = (bf16[2,2,32,2176]{3,2,1,0:T(8,128)(2,1)S(1)}, bf16[2,2,32,2176]{3,2,1,0:T(8,128)(2,1)S(1)}, u32[]{:S(2)}, u32[]{:S(2)}) collective-permute-start(bf16[2,2,32,2176]{3,2,1,0:T(8,128)(2,1)S(1)} %pad_maximum_fusion.5), channel_id=1, source_target_pairs={{0,4},{4,0},{8,12},{12,8},{16,20},{20,16},{24,28},{28,24},{1,5},{5... | collective-permute-start | bytes 1671176 | tf_op jit(solution)/shard_map/ppermute | solution.py:112
  158.3 21.9 %collective-permute-start.17 = (bf16[512,2048]{1,0:T(8,128)(2,1)S(1)}, bf16[512,2048]{1,0:T(8,128)(2,1)S(1)}, u32[]{:S(2)}, u32[]{:S(2)}) collective-permute-start(bf16[512,2048]{1,0:T(8,128)(2,1)S(1)} %shard_map.178), channel_id=1, source_target_pairs={{0,1},{1,0},{2,3},{3,2},{4,5},{5,4},{6,7},{7,6},{8,9},{9,8},{10,11... | collective-permute-start | bytes 6291464 | tf_op jit(solution)/shard_map/ppermute | solution.py:122
  158.5 15.1 %collective-permute-start.24 = (bf16[2,2,32,2176]{3,2,1,0:T(8,128)(2,1)S(1)}, bf16[2,2,32,2176]{3,2,1,0:T(8,128)(2,1)S(1)}, u32[]{:S(2)}, u32[]{:S(2)}) collective-permute-start(bf16[2,2,32,2176]{3,2,1,0:T(8,128)(2,1)S(1)} %pad_maximum_fusion.4), channel_id=1, source_target_pairs={{0,2},{1,3},{2,0},{3,1},{4,6},{5,7},{6,4},{7,5},{8,10},{9,11},{10,... | collective-permute-start | bytes 1671176 | tf_op jit(solution)/shard_map/ppermute | solution.py:117
  175.1 17.1 %collective-permute-start.27 = (bf16[512,2176]{1,0:T(8,128)(2,1)}, bf16[512,2176]{1,0:T(8,128)(2,1)}, u32[]{:S(2)}, u32[]{:S(2)}) collective-permute-start(bf16[512,2176]{1,0:T(8,128)(2,1)} %pad_maximum_fusion.1.tok_ref), channel_id=1, source_target_pairs={{0,1},{1,0},{2,3},{3,2},{4,5},{5,4},{6,7},{7,6},{8,9},{9,8},{10,11... | collective-permute-start | bytes 6684680 | tf_op jit(solution)/shard_map/ppermute | solution.py:122
  182.3 20.5 %collective-permute-start.20 = (bf16[2,2,32,2048]{3,2,1,0:T(8,128)(2,1)}, bf16[2,2,32,2048]{3,2,1,0:T(8,128)(2,1)}, u32[]{:S(2)}, u32[]{:S(2)}) collective-permute-start(bf16[2,2,32,2048]{3,2,1,0:T(8,128)(2,1)} %bitcast.53), channel_id=1, source_target_pairs={{0,4},{4,0},{8,12},{12,8},{16,20},{20,16},{24,28},{28,24},{1,5},{5... | collective-permute-start | bytes 1572872 | tf_op jit(solution)/shard_map/ppermute | solution.py:112
  201.1 48.2 %collective-permute-start.28 = (bf16[512,2048]{1,0:T(8,128)(2,1)}, bf16[512,2048]{1,0:T(8,128)(2,1)}, u32[]{:S(2)}, u32[]{:S(2)}) collective-permute-start(bf16[512,2048]{1,0:T(8,128)(2,1)} %shard_map.180), channel_id=1, source_target_pairs={{0,1},{1,0},{2,3},{3,2},{4,5},{5,4},{6,7},{7,6},{8,9},{9,8},{10,11... | collective-permute-start | bytes 6291464 | tf_op jit(solution)/shard_map/ppermute | solution.py:122
  201.3 14.8 %collective-permute-start.18 = (bf16[2,2,32,2048]{3,2,1,0:T(8,128)(2,1)S(1)}, bf16[2,2,32,2048]{3,2,1,0:T(8,128)(2,1)S(1)}, u32[]{:S(2)}, u32[]{:S(2)}) collective-permute-start(bf16[2,2,32,2048]{3,2,1,0:T(8,128)(2,1)S(1)} %bitcast.177), channel_id=1, source_target_pairs={{0,2},{1,3},{2,0},{3,1},{4,6},{5,7},{6,4},{7,5},{8,10},{9,11},{10,... | collective-permute-start | bytes 1572872 | tf_op jit(solution)/shard_map/ppermute | solution.py:117
  204.0 17.0 %collective-permute-start.21 = (bf16[2,32,2048]{2,1,0:T(8,128)(2,1)S(1)}, bf16[2,32,2048]{2,1,0:T(8,128)(2,1)S(1)}, u32[]{:S(2)}, u32[]{:S(2)}) collective-permute-start(bf16[2,32,2048]{2,1,0:T(8,128)(2,1)S(1)} %slice_bitcast_fusion.4), channel_id=1, source_target_pairs={{0,2},{1,3},{2,0},{3,1},{4,6},{5,7},{6,4},{7,5},{8,10},{9,11},{10,... | collective-permute-start | bytes 786440 | tf_op jit(solution)/shard_map/ppermute | solution.py:117
  216.2 37.1 %collective-permute-start.19 = (bf16[2,32,2048]{2,1,0:T(8,128)(2,1)S(1)}, bf16[2,32,2048]{2,1,0:T(8,128)(2,1)S(1)}, u32[]{:S(2)}, u32[]{:S(2)}) collective-permute-start(bf16[2,32,2048]{2,1,0:T(8,128)(2,1)S(1)} %slice_bitcast_fusion.6), channel_id=1, source_target_pairs={{0,4},{4,0},{8,12},{12,8},{16,20},{20,16},{24,28},{28,24},{1,5},{5... | collective-permute-start | bytes 786440 | tf_op jit(solution)/shard_map/ppermute | solution.py:112
  252.8 13.8 %collective-permute-start.29 = (bf16[2,2,32,2048]{3,2,1,0:T(8,128)(2,1)}, bf16[2,2,32,2048]{3,2,1,0:T(8,128)(2,1)S(1)}, u32[]{:S(2)}, u32[]{:S(2)}) collective-permute-start(bf16[2,2,32,2048]{3,2,1,0:T(8,128)(2,1)} %bitcast.70), channel_id=1, source_target_pairs={{0,2},{1,3},{2,0},{3,1},{4,6},{5,7},{6,4},{7,5},{8,10},{9,11},{10,... | collective-permute-start | bytes 1572872 | tf_op jit(solution)/shard_map/ppermute | solution.py:117
  253.4 68.9 %collective-permute-start.22 = (bf16[64,2048]{1,0:T(8,128)(2,1)S(1)}, bf16[64,2048]{1,0:T(8,128)(2,1)}, u32[]{:S(2)}, u32[]{:S(2)}) collective-permute-start(bf16[64,2048]{1,0:T(8,128)(2,1)S(1)} %fusion.34), channel_id=1, source_target_pairs={{0,24},{4,28},{8,0},{12,4},{16,8},{20,12},{24,16},{28,20},{1,25},{... | collective-permute-start | bytes 786440 | tf_op jit(solution)/shard_map/ppermute | solution.py:94
  254.7 14.0 %collective-permute-start.31 = (bf16[2,2,32,2048]{3,2,1,0:T(8,128)(2,1)}, bf16[2,2,32,2048]{3,2,1,0:T(8,128)(2,1)}, u32[]{:S(2)}, u32[]{:S(2)}) collective-permute-start(bf16[2,2,32,2048]{3,2,1,0:T(8,128)(2,1)} %bitcast.74), channel_id=1, source_target_pairs={{0,4},{4,0},{8,12},{12,8},{16,20},{20,16},{24,28},{28,24},{1,5},{5... | collective-permute-start | bytes 1572872 | tf_op jit(solution)/shard_map/ppermute | solution.py:112
  255.7 63.7 %all-to-all-start.1 = ((bf16[4,2,512,256]{3,2,1,0:T(8,128)(2,1)}), bf16[4,2,512,256]{3,2,1,0:T(8,128)(2,1)}, u32[]{:S(2)}, u32[]{:S(2)}) async-start(bf16[4,2,512,256]{3,2,1,0:T(8,128)(2,1)} %bitcast.81), calls=%async_computation.1 | async-start | bytes 4194304 | tf_op jit(solution)/shard_map/all_to_all | solution.py:273
  264.7 34.0 %collective-permute-start.35 = (bf16[2,1,1024,256]{3,2,1,0:T(8,128)(2,1)S(1)}, bf16[2,1,1024,256]{3,2,1,0:T(8,128)(2,1)S(1)}, u32[]{:S(2)}, u32[]{:S(2)}) collective-permute-start(bf16[2,1,1024,256]{3,2,1,0:T(8,128)(2,1)S(1)} %get-tuple-element.55), channel_id=1, source_target_pairs={{0,4},{4,0},{8,12},{12,8},{16,20},{20,16},{24,28},{28,24},{1,5},{5... | collective-permute-start | bytes 3145736 | tf_op jit(solution)/shard_map/ppermute | solution.py:99
  266.8 28.4 %collective-permute-start.30 = (bf16[2,32,2048]{2,1,0:T(8,128)(2,1)S(1)}, bf16[2,32,2048]{2,1,0:T(8,128)(2,1)S(1)}, u32[]{:S(2)}, u32[]{:S(2)}) collective-permute-start(bf16[2,32,2048]{2,1,0:T(8,128)(2,1)S(1)} %slice_bitcast_fusion.2), channel_id=1, source_target_pairs={{0,4},{4,0},{8,12},{12,8},{16,20},{20,16},{24,28},{28,24},{1,5},{5... | collective-permute-start | bytes 786440 | tf_op jit(solution)/shard_map/ppermute | solution.py:112
  269.9 25.3 %collective-permute-start.32 = (bf16[2,32,2048]{2,1,0:T(8,128)(2,1)S(1)}, bf16[2,32,2048]{2,1,0:T(8,128)(2,1)S(1)}, u32[]{:S(2)}, u32[]{:S(2)}) collective-permute-start(bf16[2,32,2048]{2,1,0:T(8,128)(2,1)S(1)} %slice_bitcast_fusion), channel_id=1, source_target_pairs={{0,2},{1,3},{2,0},{3,1},{4,6},{5,7},{6,4},{7,5},{8,10},{9,11},{10,... | collective-permute-start | bytes 786440 | tf_op jit(solution)/shard_map/ppermute | solution.py:117
  296.2 26.2 %collective-permute-start.34 = (bf16[64,2048]{1,0:T(8,128)(2,1)}, bf16[64,2048]{1,0:T(8,128)(2,1)}, u32[]{:S(2)}, u32[]{:S(2)}) collective-permute-start(bf16[64,2048]{1,0:T(8,128)(2,1)} %get-tuple-element.76), channel_id=1, source_target_pairs={{0,8},{4,12},{8,16},{12,20},{16,24},{20,28},{24,0},{28,4},{1,9},{5... | collective-permute-start | bytes 786440 | tf_op jit(solution)/shard_map/ppermute | solution.py:94
  297.6 26.4 %collective-permute-start.33 = (bf16[64,2048]{1,0:T(8,128)(2,1)}, bf16[64,2048]{1,0:T(8,128)(2,1)}, u32[]{:S(2)}, u32[]{:S(2)}) collective-permute-start(bf16[64,2048]{1,0:T(8,128)(2,1)} %get-tuple-element.75), channel_id=1, source_target_pairs={{0,16},{4,20},{8,24},{12,28},{16,0},{20,4},{24,8},{28,12},{1,17},{... | collective-permute-start | bytes 786440 | tf_op jit(solution)/shard_map/ppermute | solution.py:94
  298.7 35.5 %copy-start.1 = (bf16[512,2048]{1,0:T(8,128)(2,1)S(1)}, bf16[512,2048]{1,0:T(8,128)(2,1)}, u32[]{:S(2)}) copy-start(bf16[512,2048]{1,0:T(8,128)(2,1)} %param.27) | copy-start | bytes 6291460
  321.5 11.8 %collective-permute-start.36 = (bf16[2,1,512,256]{3,2,1,0:T(8,128)(2,1)S(1)}, bf16[2,1,512,256]{3,2,1,0:T(8,128)(2,1)S(1)}, u32[]{:S(2)}, u32[]{:S(2)}) collective-permute-start(bf16[2,1,512,256]{3,2,1,0:T(8,128)(2,1)S(1)} %get-tuple-element.57), channel_id=1, source_target_pairs={{0,4},{4,0},{8,12},{12,8},{16,20},{20,16},{24,28},{28,24},{1,5},{5... | collective-permute-start | bytes 1572872 | tf_op jit(solution)/shard_map/ppermute | solution.py:99
  (18 other events, 75.2 us)

commit v3 on v0

--- a/solution.py
+++ b/solution.py
@@ -213,7 +213,7 @@
             part = sums[offset] if step == 0 else turn_pairs(sums[offset], -step)
             part = part.astype(jnp.float32)
             total = part if total is None else total + part
-    return total, arrived
+    return total, arrived, mixed
 
 
 def spread_weights(slot_weights):
@@ -400,11 +400,12 @@
     slots_here = slot_weights.shape[0]
     index = chunk_index(source_slot, slots_here)
     size = held[0].shape[1] // 2
-    mixture, first = mix(
+    mixture, first, mixed = mix(
         normed, codes, slot_weights, held, lambda held: take_chunks(held, index, 0, size)
     )
     layer_out = (residual + mixture).astype(jnp.bfloat16)
     second = trade_columns(after(take_chunks(held, index, size, size), first))
+    first = after(first, mixed)
     replica_weights = collect_replicas((first, second), source_slot, slots_here)
     return (layer_out, replica_weights.reshape((1,) + slot_weights.shape[1:]))
 

time: 298 us -> 299 us (level)
  starting transfers between devices: 62.8 us -> 69 us
  waiting for transfers between devices: 130 us -> 127 us
    ppermute x5, waiting for transfers between devices: 29.9 us -> 37.8 us  [swap(): return lax.ppermute(value, 'req', [(i, i ^ mask) for i in range(count)])]
    all_to_all x2, waiting for transfers between devices: 17 us -> 11.2 us  [trade_columns(): lax.all_to_all(outgoing, 'req', 0, 0, axis_index_groups=columns, tiled=True)]
    ppermute x9, starting transfers between devices: 22.3 us -> 28.1 us  [turn_pairs(): lax.ppermute(value, 'req', [(i, (i + 2 * step) % count) for i in range(co...]
    ppermute x9, waiting for transfers between devices: 14.7 us -> 10.3 us  [turn_pairs(): lax.ppermute(value, 'req', [(i, (i + 2 * step) % count) for i in range(co...]
  transfers between devices with their start and end apart: 39 -> 39, of which waited for: 16 -> 17; matrix products, arithmetic and copies ran while one was open for 16% -> 16% of each run, Pallas kernels for 11% -> 10%
where the time goes in v3:
time: 299 us; the launch traced here: 298 us
  waiting for transfers between devices  127 us (42%)
  starting transfers between devices  69 us (23%)
  local copies, waits for them, and re-layouts  31.6 us (11%)
  Pallas kernels  30 us (10%)
  other arithmetic  26 us (9%)
  between operations  9.82 us (3%)
  matrix products  5.19 us (2%)
    ppermute x9, waiting for transfers between devices, flip_pair(): return lax.ppermute(value, 'req', [(i, i ^ 1) for i in range(count)])  50.7 us
    ppermute x5, waiting for transfers between devices, swap(): return lax.ppermute(value, 'req', [(i, i ^ mask) for i in range(count)])  37.8 us
    ppermute x9, starting transfers between devices, turn_pairs(): lax.ppermute(value, 'req', [(i, (i + 2 * step) % count) for i in range(co...  28.1 us
    pallas_call x4, Pallas kernels, run_experts(): pl.pallas_call(experts_kernel, out_shape=jax.ShapeDtypeStruct((count, wid...  22.2 us
    ppermute x9, waiting for transfers between devices, flip_chip(): return lax.ppermute(value, 'exp', [(i, i ^ 2) for i in range(count)])  16.7 us
    unnamed x57, local copies, waits for them, and re-layouts  12.9 us
    ppermute x9, starting transfers between devices, flip_chip(): return lax.ppermute(value, 'exp', [(i, i ^ 2) for i in range(count)])  12.8 us
    all_to_all x2, waiting for transfers between devices, trade_columns(): lax.all_to_all(outgoing, 'req', 0, 0, axis_index_groups=columns, tiled=True)  11.2 us
  transfers between devices with their start and end apart: 39, of which 17 were waited for; matrix products, arithmetic and copies ran while one was open for 16% of the time, Pallas kernels for 10%

profile of v3, /device:TPU:0, one launch (start us, length us, event | category | flops | bytes accessed | tf_op | source)
XLA Modules:
  0.0 298.3 jit_solution(2239366346402348342)
XLA Ops:
  0.6 1.7 fusion.69
  2.4 4.0 %collective-permute-start.1 = (bf16[2,2,32,512]{3,2,1,0:T(8,128)(2,1)}, bf16[2,2,32,512]{3,2,1,0:T(8,128)(2,1)}, u32[]{:S(2)}, u32[]{:S(2)}) collective-permute-start(bf16[2,2,32,512]{3,2,1,0:T(8,128)(2,1)} %get-tuple-element.82), channel_id=1, source_target_pairs={{0,16},{4,20},{8,24},{12,28},{16,0},{20,4},{24,8},{28,12},{1,17},{... | collective-permute-start | bytes 393224 | tf_op jit(solution)/shard_map/ppermute | solution.py:94
  8.0 2.2 collective-permute-start.2
  10.2 5.7 %dynamic-slice_bitcast_fusion = (bf16[2,1536,256]{2,1,0:T(8,128)(2,1)}, bf16[2,1536,256]{2,1,0:T(8,128)(2,1)}, bf16[2,1536,256]{2,1,0:T(8,128)(2,1)}, bf16[2,1536,256]{2,1,0:T(8,128)(2,1)}) fusion(bf16[2,4,1536,256]{3,2,1,0:T(8,128)(2,1)} %bitcast.154, s32[]{:T(128)S(6)} %select_n.262, s32[]{:T(128)S(6)} %select_n.256, s32[]{:T(128)S(6)} %select_n.248, ...), kind=kLoop, calls=%fused_computation.6 | loop fusion | bytes 12582928 | tf_op jit(solution)/shard_map/jit(dynamic_index_in_dim)/squeeze | solution.py:126
  34.6 19.7 %collective-permute-done.3 = bf16[2,2,32,512]{3,2,1,0:T(8,128)(2,1)S(1)} collective-permute-done((bf16[2,2,32,512]{3,2,1,0:T(8,128)(2,1)S(1)}, bf16[2,2,32,512]{3,2,1,0:T(8,128)(2,1)S(1)}, u32[]{:S(2)}, u32[]{:S(2)}) %collective-permute-start.3) | collective-permute-done | bytes 131104 | tf_op jit(solution)/shard_map/ppermute | solution.py:112
  54.5 2.8 fusion.78
  57.3 1.7 convolution_convert_fusion
  61.3 2.7 collective-permute-start.20
  68.5 6.3 %collective-permute-done.7 = bf16[64,2048]{1,0:T(8,128)(2,1)S(1)} collective-permute-done((bf16[64,2048]{1,0:T(8,128)(2,1)S(1)}, bf16[64,2048]{1,0:T(8,128)(2,1)S(1)}, u32[]{:S(2)}, u32[]{:S(2)}) %collective-permute-start.7) | collective-permute-done | bytes 262176 | tf_op jit(solution)/shard_map/ppermute | solution.py:117
  77.2 3.2 %collective-permute-start.22 = (bf16[64,2176]{1,0:T(8,128)(2,1)S(1)}, bf16[64,2176]{1,0:T(8,128)(2,1)S(1)}, u32[]{:S(2)}, u32[]{:S(2)}) collective-permute-start(bf16[64,2176]{1,0:T(8,128)(2,1)S(1)} %concatenate.37), channel_id=1, source_target_pairs={{0,24},{4,28},{8,0},{12,4},{16,8},{20,12},{24,16},{28,20},{1,25},{... | collective-permute-start | bytes 835592 | tf_op jit(solution)/shard_map/ppermute | solution.py:94
  80.3 28.4 %collective-permute-done.20.refs_3_ = bf16[2,1536,256]{2,1,0:T(8,128)(2,1)} collective-permute-done((bf16[2,1536,256]{2,1,0:T(8,128)(2,1)}, bf16[2,1536,256]{2,1,0:T(8,128)(2,1)}, u32[]{:S(2)}, u32[]{:S(2)}) %collective-permute-start.20) | collective-permute-done | bytes 1572896 | tf_op jit(solution)/shard_map/ppermute | solution.py:99
  108.7 3.9 %shard_map.178 = bf16[8,768,256]{2,1,0:T(8,128)(2,1)S(1)} custom-call(s32[8]{0:T(128)S(1)} %fusion.50.index_ref, bf16[2,1536,256]{2,1,0:T(8,128)(2,1)S(1)} %copy-done.2, bf16[2,1536,256]{2,1,0:T(8,128)(2,1)} %collective-permute-done.4.refs_1_, bf16[2,1536,256]{2,1,0:T(8,128)(2,1)} %collective-permute-done.5.refs_2_, ...), custom_call_target="tpu_custom_call" | custom-call | bytes 6291456 | tf_op jit(solution)/shard_map/pallas_call | solution.py:253
  112.6 2.3 collective-permute-start.9
  116.5 3.7 %collective-permute-done.21 = bf16[64,2176]{1,0:T(8,128)(2,1)S(1)} collective-permute-done((bf16[64,2176]{1,0:T(8,128)(2,1)S(1)}, bf16[64,2176]{1,0:T(8,128)(2,1)S(1)}, u32[]{:S(2)}, u32[]{:S(2)}) %collective-permute-start.21) | collective-permute-done | bytes 278560 | tf_op jit(solution)/shard_map/ppermute | solution.py:94
  121.8 2.5 collective-permute-done.11
  126.7 4.9 %all-to-all-start = ((bf16[4,2,768,256]{3,2,1,0:T(8,128)(2,1)}), bf16[4,2,768,256]{3,2,1,0:T(8,128)(2,1)}, u32[]{:S(2)}, u32[]{:S(2)}) async-start(bf16[4,2,768,256]{3,2,1,0:T(8,128)(2,1)} %bitcast.152), calls=%async_computation | async-start | bytes 6291456 | tf_op jit(solution)/shard_map/all_to_all | solution.py:273
  131.6 2.1 collective-permute-start.23
  134.8 5.2 %collective-permute-done.12 = bf16[2,2,32,2176]{3,2,1,0:T(8,128)(2,1)} collective-permute-done((bf16[2,2,32,2176]{3,2,1,0:T(8,128)(2,1)S(1)}, bf16[2,2,32,2176]{3,2,1,0:T(8,128)(2,1)}, u32[]{:S(2)}, u32[]{:S(2)}) %collective-permute-start.12) | collective-permute-done | bytes 557088 | tf_op jit(solution)/shard_map/ppermute | solution.py:112
  140.0 3.0 pad_maximum_fusion.tok_ref
  145.9 4.3 %collective-permute-done.26 = bf16[2,2,32,2176]{3,2,1,0:T(8,128)(2,1)S(1)} collective-permute-done((bf16[2,2,32,2176]{3,2,1,0:T(8,128)(2,1)S(1)}, bf16[2,2,32,2176]{3,2,1,0:T(8,128)(2,1)S(1)}, u32[]{:S(2)}, u32[]{:S(2)}) %collective-permute-start.26) | collective-permute-done | bytes 557088 | tf_op jit(solution)/shard_map/ppermute | solution.py:112
  150.2 7.9 %collective-permute-done.24 = bf16[2,2,32,2176]{3,2,1,0:T(8,128)(2,1)S(1)} collective-permute-done((bf16[2,2,32,2176]{3,2,1,0:T(8,128)(2,1)S(1)}, bf16[2,2,32,2176]{3,2,1,0:T(8,128)(2,1)S(1)}, u32[]{:S(2)}, u32[]{:S(2)}) %collective-permute-start.24) | collective-permute-done | bytes 557088 | tf_op jit(solution)/shard_map/ppermute | solution.py:117
  159.7 2.8 copy-done.5
  162.5 6.1 %shard_map.177 = bf16[512,2048]{1,0:T(8,128)(2,1)} custom-call(s32[1]{0:T(128)} %bitcast.35.first_slot_ref, bf16[512,2176]{1,0:T(8,128)(2,1)} %collective-permute-done.13.tok_ref, bf16[2,3,2048,256]{3,2,1,0:T(8,128)(2,1)S(1)} %copy-done.5), custom_call_target="tpu_custom_call" | custom-call | flops 3221225472 | bytes 10485760 | tf_op jit(solution)/shard_map/pallas_call | solution.py:73
  169.0 6.0 %shard_map.180 = bf16[512,2048]{1,0:T(8,128)(2,1)} custom-call(s32[1]{0:T(128)} %bitcast.35.first_slot_ref, bf16[512,2176]{1,0:T(8,128)(2,1)} %collective-permute-done.27.tok_ref, bf16[2,3,2048,256]{3,2,1,0:T(8,128)(2,1)S(1)} %copy-done.5), custom_call_target="tpu_custom_call" | custom-call | flops 3221225472 | bytes 10485760 | tf_op jit(solution)/shard_map/pallas_call | solution.py:73
  177.0 3.9 %shard_map.181 = bf16[8,768,256]{2,1,0:T(8,128)(2,1)S(1)} custom-call(s32[8]{0:T(128)S(1)} %fusion.50.index_ref, bf16[2,1536,256]{2,1,0:T(8,128)(2,1)S(1)} %copy-done.2, bf16[2,1536,256]{2,1,0:T(8,128)(2,1)} %collective-permute-done.4.refs_1_, bf16[2,1536,256]{2,1,0:T(8,128)(2,1)} %collective-permute-done.5.refs_2_, ...), custom_call_target="tpu_custom_call" | custom-call | bytes 6291456 | tf_op jit(solution)/shard_map/pallas_call | solution.py:253
  182.5 2.8 copy-done.6
  185.3 5.1 %shard_map.176 = bf16[512,2048]{1,0:T(8,128)(2,1)S(1)} custom-call(s32[1]{0:T(128)} %bitcast.35.first_slot_ref, bf16[512,2176]{1,0:T(8,128)(2,1)} %pad_maximum_fusion.tok_ref, bf16[2,3,2048,256]{3,2,1,0:T(8,128)(2,1)S(1)} %copy-done.6), custom_call_target="tpu_custom_call" | custom-call | flops 3221225472 | bytes 10485760 | tf_op jit(solution)/shard_map/pallas_call | solution.py:73
  190.4 5.2 %all-to-all-done = bf16[4,2,768,256]{3,2,1,0:T(8,128)(2,1)} async-done(((bf16[4,2,768,256]{3,2,1,0:T(8,128)(2,1)}), bf16[4,2,768,256]{3,2,1,0:T(8,128)(2,1)}, u32[]{:S(2)}, u32[]{:S(2)}) %all-to-all-start) | async-done | bytes 3145760 | tf_op jit(solution)/shard_map/all_to_all | solution.py:273
  195.6 4.7 %all-to-all-start.1 = ((bf16[4,2,768,256]{3,2,1,0:T(8,128)(2,1)}), bf16[4,2,768,256]{3,2,1,0:T(8,128)(2,1)}, u32[]{:S(2)}, u32[]{:S(2)}) async-start(bf16[4,2,768,256]{3,2,1,0:T(8,128)(2,1)} %bitcast.153), calls=%async_computation.1 | async-start | bytes 6291456 | tf_op jit(solution)/shard_map/all_to_all | solution.py:273
  200.3 2.8 copy-done.7
  203.1 5.1 %shard_map.179 = bf16[512,2048]{1,0:T(8,128)(2,1)S(1)} custom-call(s32[1]{0:T(128)} %bitcast.35.first_slot_ref, bf16[512,2176]{1,0:T(8,128)(2,1)} %pad_maximum_fusion.1.tok_ref, bf16[2,3,2048,256]{3,2,1,0:T(8,128)(2,1)S(1)} %copy-done.7), custom_call_target="tpu_custom_call" | custom-call | flops 3221225472 | bytes 10485760 | tf_op jit(solution)/shard_map/pallas_call | solution.py:73
  208.2 1.9 broadcast_in_dim.162
  210.0 2.5 constant_dynamic-slice_fusion.1
  214.1 2.4 add_convert_fusion.1
  218.7 2.4 add_convert_fusion
  221.3 1.6 collective-permute-start.31
  223.5 9.4 %collective-permute-done.35 = bf16[2,1,768,256]{3,2,1,0:T(8,128)(2,1)S(1)} collective-permute-done((bf16[2,1,768,256]{3,2,1,0:T(8,128)(2,1)S(1)}, bf16[2,1,768,256]{3,2,1,0:T(8,128)(2,1)S(1)}, u32[]{:S(2)}, u32[]{:S(2)}) %collective-permute-start.35) | collective-permute-done | bytes 786464 | tf_op jit(solution)/shard_map/ppermute | solution.py:99
  233.9 10.3 %collective-permute-done.17 = bf16[2,2,32,2048]{3,2,1,0:T(8,128)(2,1)S(1)} collective-permute-done((bf16[2,2,32,2048]{3,2,1,0:T(8,128)(2,1)S(1)}, bf16[2,2,32,2048]{3,2,1,0:T(8,128)(2,1)S(1)}, u32[]{:S(2)}, u32[]{:S(2)}) %collective-permute-start.17) | collective-permute-done | bytes 524320 | tf_op jit(solution)/shard_map/ppermute | solution.py:112
  246.0 1.6 collective-permute-start.16
  247.7 7.7 %collective-permute-done.31 = bf16[2,2,32,2048]{3,2,1,0:T(8,128)(2,1)S(1)} collective-permute-done((bf16[2,2,32,2048]{3,2,1,0:T(8,128)(2,1)S(1)}, bf16[2,2,32,2048]{3,2,1,0:T(8,128)(2,1)S(1)}, u32[]{:S(2)}, u32[]{:S(2)}) %collective-permute-start.31) | collective-permute-done | bytes 524320 | tf_op jit(solution)/shard_map/ppermute | solution.py:112
  257.3 1.6 collective-permute-start.30
  259.0 2.0 collective-permute-done.16
  261.8 3.8 %collective-permute-start.19 = (bf16[64,2048]{1,0:T(8,128)(2,1)}, bf16[64,2048]{1,0:T(8,128)(2,1)}, u32[]{:S(2)}, u32[]{:S(2)}) collective-permute-start(bf16[64,2048]{1,0:T(8,128)(2,1)} %fusion.34), channel_id=1, source_target_pairs={{0,24},{4,28},{8,0},{12,4},{16,8},{20,12},{24,16},{28,20},{1,25},{... | collective-permute-start | bytes 786440 | tf_op jit(solution)/shard_map/ppermute | solution.py:94
  266.5 6.0 %all-to-all-done.1 = bf16[4,2,768,256]{3,2,1,0:T(8,128)(2,1)} async-done(((bf16[4,2,768,256]{3,2,1,0:T(8,128)(2,1)}), bf16[4,2,768,256]{3,2,1,0:T(8,128)(2,1)}, u32[]{:S(2)}, u32[]{:S(2)}) %all-to-all-start.1) | async-done | bytes 3145760 | tf_op jit(solution)/shard_map/all_to_all | solution.py:273
  272.4 2.4 constant_dynamic-slice_fusion
  276.5 12.5 %collective-permute-start.34 = (bf16[64,2048]{1,0:T(8,128)(2,1)S(1)}, bf16[64,2048]{1,0:T(8,128)(2,1)S(1)}, u32[]{:S(2)}, u32[]{:S(2)}) collective-permute-start(bf16[64,2048]{1,0:T(8,128)(2,1)S(1)} %get-tuple-element.72), channel_id=1, source_target_pairs={{0,8},{4,12},{8,16},{12,20},{16,24},{20,28},{24,0},{28,4},{1,9},{5... | collective-permute-start | bytes 786440 | tf_op jit(solution)/shard_map/ppermute | solution.py:94
  289.4 6.2 %collective-permute-done.34 = bf16[64,2048]{1,0:T(8,128)(2,1)S(1)} collective-permute-done((bf16[64,2048]{1,0:T(8,128)(2,1)S(1)}, bf16[64,2048]{1,0:T(8,128)(2,1)S(1)}, u32[]{:S(2)}, u32[]{:S(2)}) %collective-permute-start.34) | collective-permute-done | bytes 262176 | tf_op jit(solution)/shard_map/ppermute | solution.py:94
  295.6 1.8 fusion.14
  (188 shorter events, 49.9 us)
Async XLA Ops:
  0.6 58.4 %copy-start = (bf16[512,2048]{1,0:T(8,128)(2,1)S(1)}, bf16[512,2048]{1,0:T(8,128)(2,1)}, u32[]{:S(2)}) copy-start(bf16[512,2048]{1,0:T(8,128)(2,1)} %param.27) | copy-start | bytes 6291460
  2.4 29.7 %collective-permute-start.1 = (bf16[2,2,32,512]{3,2,1,0:T(8,128)(2,1)}, bf16[2,2,32,512]{3,2,1,0:T(8,128)(2,1)}, u32[]{:S(2)}, u32[]{:S(2)}) collective-permute-start(bf16[2,2,32,512]{3,2,1,0:T(8,128)(2,1)} %get-tuple-element.82), channel_id=1, source_target_pairs={{0,16},{4,20},{8,24},{12,28},{16,0},{20,4},{24,8},{28,12},{1,17},{... | collective-permute-start | bytes 393224 | tf_op jit(solution)/shard_map/ppermute | solution.py:94
  6.4 25.7 %collective-permute-start = (bf16[2,2,32,512]{3,2,1,0:T(8,128)(2,1)}, bf16[2,2,32,512]{3,2,1,0:T(8,128)(2,1)}, u32[]{:S(2)}, u32[]{:S(2)}) collective-permute-start(bf16[2,2,32,512]{3,2,1,0:T(8,128)(2,1)} %get-tuple-element.82), channel_id=1, source_target_pairs={{0,8},{4,12},{8,16},{12,20},{16,24},{20,28},{24,0},{28,4},{1,9},{5... | collective-permute-start | bytes 393224 | tf_op jit(solution)/shard_map/ppermute | solution.py:94
  8.0 24.2 %collective-permute-start.2 = (bf16[2,2,32,512]{3,2,1,0:T(8,128)(2,1)}, bf16[2,2,32,512]{3,2,1,0:T(8,128)(2,1)}, u32[]{:S(2)}, u32[]{:S(2)}) collective-permute-start(bf16[2,2,32,512]{3,2,1,0:T(8,128)(2,1)} %get-tuple-element.82), channel_id=1, source_target_pairs={{0,24},{4,28},{8,0},{12,4},{16,8},{20,12},{24,16},{28,20},{1,25},{... | collective-permute-start | bytes 393224 | tf_op jit(solution)/shard_map/ppermute | solution.py:94
  10.2 8.9 %copy-start.13 = (bf16[256,512]{1,0:T(8,128)(2,1)S(1)}, bf16[256,512]{1,0:T(8,128)(2,1)}, u32[]{:S(2)}) copy-start(bf16[256,512]{1,0:T(8,128)(2,1)} %param.18) | copy-start | bytes 786436
  10.2 9.1 %copy-start.14 = (bf16[256,512]{1,0:T(8,128)(2,1)S(1)}, bf16[256,512]{1,0:T(8,128)(2,1)}, u32[]{:S(2)}) copy-start(bf16[256,512]{1,0:T(8,128)(2,1)} %param.19) | copy-start | bytes 786436
  15.9 43.1 %collective-permute-start.5 = (bf16[2,1536,256]{2,1,0:T(8,128)(2,1)}, bf16[2,1536,256]{2,1,0:T(8,128)(2,1)}, u32[]{:S(2)}, u32[]{:S(2)}) collective-permute-start(bf16[2,1536,256]{2,1,0:T(8,128)(2,1)} %get-tuple-element.49), channel_id=1, source_target_pairs={{0,8},{4,12},{8,0},{12,4},{16,24},{20,28},{24,16},{28,20},{1,9},{5... | collective-permute-start | bytes 4718600 | tf_op jit(solution)/shard_map/ppermute | solution.py:99
  16.0 43.1 %collective-permute-start.4 = (bf16[2,1536,256]{2,1,0:T(8,128)(2,1)}, bf16[2,1536,256]{2,1,0:T(8,128)(2,1)}, u32[]{:S(2)}, u32[]{:S(2)}) collective-permute-start(bf16[2,1536,256]{2,1,0:T(8,128)(2,1)} %get-tuple-element.50), channel_id=1, source_target_pairs={{0,4},{4,0},{8,12},{12,8},{16,20},{20,16},{24,28},{28,24},{1,5},{5... | collective-permute-start | bytes 4718600 | tf_op jit(solution)/shard_map/ppermute | solution.py:99
  33.3 21.0 %collective-permute-start.3 = (bf16[2,2,32,512]{3,2,1,0:T(8,128)(2,1)S(1)}, bf16[2,2,32,512]{3,2,1,0:T(8,128)(2,1)S(1)}, u32[]{:S(2)}, u32[]{:S(2)}) collective-permute-start(bf16[2,2,32,512]{3,2,1,0:T(8,128)(2,1)S(1)} %pad_maximum_fusion.12), channel_id=1, source_target_pairs={{0,4},{4,0},{8,12},{12,8},{16,20},{20,16},{24,28},{28,24},{1,5},{5... | collective-permute-start | bytes 393224 | tf_op jit(solution)/shard_map/ppermute | solution.py:112
  59.8 8.5 %copy-start.25 = (s32[8]{0:T(128)S(1)}, s32[8]{0:T(128)}, u32[]{:S(2)}) copy-start(s32[8]{0:T(128)} %param.32) | copy-start | bytes 100
  59.8 15.1 %copy-start.16 = (bf16[64,2048]{1,0:T(8,128)(2,1)S(1)}, bf16[64,2048]{1,0:T(8,128)(2,1)}, u32[]{:S(2)}) copy-start(bf16[64,2048]{1,0:T(8,128)(2,1)} %param.17) | copy-start | bytes 786436
  61.2 2.9 collective-permute-start.6
  61.3 47.4 %collective-permute-start.20 = (bf16[2,1536,256]{2,1,0:T(8,128)(2,1)}, bf16[2,1536,256]{2,1,0:T(8,128)(2,1)}, u32[]{:S(2)}, u32[]{:S(2)}) collective-permute-start(bf16[2,1536,256]{2,1,0:T(8,128)(2,1)} %get-tuple-element.48), channel_id=1, source_target_pairs={{0,12},{4,8},{8,4},{12,0},{16,28},{20,24},{24,20},{28,16},{1,13},{... | collective-permute-start | bytes 4718600 | tf_op jit(solution)/shard_map/ppermute | solution.py:99
  64.0 12.1 %copy-start.17 = (f32[2048]{0:T(1024)S(1)}, f32[2048]{0:T(1024)}, u32[]{:S(2)}) copy-start(f32[2048]{0:T(1024)} %param.28) | copy-start | bytes 24580
  66.4 42.3 %copy-start.2 = (bf16[2,1536,256]{2,1,0:T(8,128)(2,1)S(1)}, bf16[2,1536,256]{2,1,0:T(8,128)(2,1)}, u32[]{:S(2)}) copy-start(bf16[2,1536,256]{2,1,0:T(8,128)(2,1)} %get-tuple-element.47.refs_0_) | copy-start | bytes 4718596
  66.4 8.4 %collective-permute-start.7 = (bf16[64,2048]{1,0:T(8,128)(2,1)S(1)}, bf16[64,2048]{1,0:T(8,128)(2,1)S(1)}, u32[]{:S(2)}, u32[]{:S(2)}) collective-permute-start(bf16[64,2048]{1,0:T(8,128)(2,1)S(1)} %fusion.28), channel_id=1, source_target_pairs={{0,2},{1,3},{2,0},{3,1},{4,6},{5,7},{6,4},{7,5},{8,10},{9,11},{10,... | collective-permute-start | bytes 786440 | tf_op jit(solution)/shard_map/ppermute | solution.py:117
  76.4 36.2 %collective-permute-start.8 = (bf16[64,2176]{1,0:T(8,128)(2,1)S(1)}, bf16[64,2176]{1,0:T(8,128)(2,1)S(1)}, u32[]{:S(2)}, u32[]{:S(2)}) collective-permute-start(bf16[64,2176]{1,0:T(8,128)(2,1)S(1)} %concatenate.37), channel_id=1, source_target_pairs={{0,8},{4,12},{8,16},{12,20},{16,24},{20,28},{24,0},{28,4},{1,9},{5... | collective-permute-start | bytes 835592 | tf_op jit(solution)/shard_map/ppermute | solution.py:94
  77.2 43.0 %collective-permute-start.22 = (bf16[64,2176]{1,0:T(8,128)(2,1)S(1)}, bf16[64,2176]{1,0:T(8,128)(2,1)S(1)}, u32[]{:S(2)}, u32[]{:S(2)}) collective-permute-start(bf16[64,2176]{1,0:T(8,128)(2,1)S(1)} %concatenate.37), channel_id=1, source_target_pairs={{0,24},{4,28},{8,0},{12,4},{16,8},{20,12},{24,16},{28,20},{1,25},{... | collective-permute-start | bytes 835592 | tf_op jit(solution)/shard_map/ppermute | solution.py:94
  108.7 11.5 %collective-permute-start.21 = (bf16[64,2176]{1,0:T(8,128)(2,1)S(1)}, bf16[64,2176]{1,0:T(8,128)(2,1)S(1)}, u32[]{:S(2)}, u32[]{:S(2)}) collective-permute-start(bf16[64,2176]{1,0:T(8,128)(2,1)S(1)} %concatenate.37), channel_id=1, source_target_pairs={{0,16},{4,20},{8,24},{12,28},{16,0},{20,4},{24,8},{28,12},{1,17},{... | collective-permute-start | bytes 835592 | tf_op jit(solution)/shard_map/ppermute | solution.py:94
  112.6 12.7 %copy-start.3 = (bf16[8,768,256]{2,1,0:T(8,128)(2,1)}, bf16[8,768,256]{2,1,0:T(8,128)(2,1)S(1)}, u32[]{:S(2)}) copy-start(bf16[8,768,256]{2,1,0:T(8,128)(2,1)S(1)} %shard_map.178) | copy-start | bytes 9437188
  112.6 11.7 %collective-permute-start.9 = (bf16[2,32,2176]{2,1,0:T(8,128)(2,1)S(1)}, bf16[2,32,2176]{2,1,0:T(8,128)(2,1)S(1)}, u32[]{:S(2)}, u32[]{:S(2)}) collective-permute-start(bf16[2,32,2176]{2,1,0:T(8,128)(2,1)S(1)} %get-tuple-element.67), channel_id=1, source_target_pairs={{0,4},{4,0},{8,12},{12,8},{16,20},{20,16},{24,28},{28,24},{1,5},{5... | collective-permute-start | bytes 835592 | tf_op jit(solution)/shard_map/ppermute | solution.py:112
  115.0 9.3 %collective-permute-start.11 = (bf16[2,32,2176]{2,1,0:T(8,128)(2,1)S(1)}, bf16[2,32,2176]{2,1,0:T(8,128)(2,1)S(1)}, u32[]{:S(2)}, u32[]{:S(2)}) collective-permute-start(bf16[2,32,2176]{2,1,0:T(8,128)(2,1)S(1)} %get-tuple-element.68), channel_id=1, source_target_pairs={{0,2},{1,3},{2,0},{3,1},{4,6},{5,7},{6,4},{7,5},{8,10},{9,11},{10,... | collective-permute-start | bytes 835592 | tf_op jit(solution)/shard_map/ppermute | solution.py:117
  120.2 13.5 %collective-permute-start.25 = (bf16[2,32,2176]{2,1,0:T(8,128)(2,1)S(1)}, bf16[2,32,2176]{2,1,0:T(8,128)(2,1)}, u32[]{:S(2)}, u32[]{:S(2)}) collective-permute-start(bf16[2,32,2176]{2,1,0:T(8,128)(2,1)S(1)} %get-tuple-element.70), channel_id=1, source_target_pairs={{0,2},{1,3},{2,0},{3,1},{4,6},{5,7},{6,4},{7,5},{8,10},{9,11},{10,... | collective-permute-start | bytes 835592 | tf_op jit(solution)/shard_map/ppermute | solution.py:117
  124.3 15.7 %collective-permute-start.12 = (bf16[2,2,32,2176]{3,2,1,0:T(8,128)(2,1)S(1)}, bf16[2,2,32,2176]{3,2,1,0:T(8,128)(2,1)}, u32[]{:S(2)}, u32[]{:S(2)}) collective-permute-start(bf16[2,2,32,2176]{3,2,1,0:T(8,128)(2,1)S(1)} %pad_maximum_fusion.3), channel_id=1, source_target_pairs={{0,4},{4,0},{8,12},{12,8},{16,20},{20,16},{24,28},{28,24},{1,5},{5... | collective-permute-start | bytes 1671176 | tf_op jit(solution)/shard_map/ppermute | solution.py:112
  125.2 14.8 %collective-permute-start.10 = (bf16[2,2,32,2176]{3,2,1,0:T(8,128)(2,1)}, bf16[2,2,32,2176]{3,2,1,0:T(8,128)(2,1)}, u32[]{:S(2)}, u32[]{:S(2)}) collective-permute-start(bf16[2,2,32,2176]{3,2,1,0:T(8,128)(2,1)} %pad_maximum_fusion.2), channel_id=1, source_target_pairs={{0,2},{1,3},{2,0},{3,1},{4,6},{5,7},{6,4},{7,5},{8,10},{9,11},{10,... | collective-permute-start | bytes 1671176 | tf_op jit(solution)/shard_map/ppermute | solution.py:117
  126.7 68.9 %all-to-all-start = ((bf16[4,2,768,256]{3,2,1,0:T(8,128)(2,1)}), bf16[4,2,768,256]{3,2,1,0:T(8,128)(2,1)}, u32[]{:S(2)}, u32[]{:S(2)}) async-start(bf16[4,2,768,256]{3,2,1,0:T(8,128)(2,1)} %bitcast.152), calls=%async_computation | async-start | bytes 6291456 | tf_op jit(solution)/shard_map/all_to_all | solution.py:273
  131.6 12.7 %collective-permute-start.23 = (bf16[2,32,2176]{2,1,0:T(8,128)(2,1)S(1)}, bf16[2,32,2176]{2,1,0:T(8,128)(2,1)S(1)}, u32[]{:S(2)}, u32[]{:S(2)}) collective-permute-start(bf16[2,32,2176]{2,1,0:T(8,128)(2,1)S(1)} %get-tuple-element.69), channel_id=1, source_target_pairs={{0,4},{4,0},{8,12},{12,8},{16,20},{20,16},{24,28},{28,24},{1,5},{5... | collective-permute-start | bytes 835592 | tf_op jit(solution)/shard_map/ppermute | solution.py:112
  134.7 15.6 %collective-permute-start.26 = (bf16[2,2,32,2176]{3,2,1,0:T(8,128)(2,1)S(1)}, bf16[2,2,32,2176]{3,2,1,0:T(8,128)(2,1)S(1)}, u32[]{:S(2)}, u32[]{:S(2)}) collective-permute-start(bf16[2,2,32,2176]{3,2,1,0:T(8,128)(2,1)S(1)} %pad_maximum_fusion.5), channel_id=1, source_target_pairs={{0,4},{4,0},{8,12},{12,8},{16,20},{20,16},{24,28},{28,24},{1,5},{5... | collective-permute-start | bytes 1671176 | tf_op jit(solution)/shard_map/ppermute | solution.py:112
  143.0 16.7 %collective-permute-start.13 = (bf16[512,2176]{1,0:T(8,128)(2,1)}, bf16[512,2176]{1,0:T(8,128)(2,1)}, u32[]{:S(2)}, u32[]{:S(2)}) collective-permute-start(bf16[512,2176]{1,0:T(8,128)(2,1)} %pad_maximum_fusion.tok_ref), channel_id=1, source_target_pairs={{0,1},{1,0},{2,3},{3,2},{4,5},{5,4},{6,7},{7,6},{8,9},{9,8},{10,11... | collective-permute-start | bytes 6684680 | tf_op jit(solution)/shard_map/ppermute | solution.py:122
  144.3 13.8 %collective-permute-start.24 = (bf16[2,2,32,2176]{3,2,1,0:T(8,128)(2,1)S(1)}, bf16[2,2,32,2176]{3,2,1,0:T(8,128)(2,1)S(1)}, u32[]{:S(2)}, u32[]{:S(2)}) collective-permute-start(bf16[2,2,32,2176]{3,2,1,0:T(8,128)(2,1)S(1)} %pad_maximum_fusion.4), channel_id=1, source_target_pairs={{0,2},{1,3},{2,0},{3,1},{4,6},{5,7},{6,4},{7,5},{8,10},{9,11},{10,... | collective-permute-start | bytes 1671176 | tf_op jit(solution)/shard_map/ppermute | solution.py:117
  159.7 9.4 %collective-permute-start.27 = (bf16[512,2176]{1,0:T(8,128)(2,1)}, bf16[512,2176]{1,0:T(8,128)(2,1)}, u32[]{:S(2)}, u32[]{:S(2)}) collective-permute-start(bf16[512,2176]{1,0:T(8,128)(2,1)} %pad_maximum_fusion.1.tok_ref), channel_id=1, source_target_pairs={{0,1},{1,0},{2,3},{3,2},{4,5},{5,4},{6,7},{7,6},{8,9},{9,8},{10,11... | collective-permute-start | bytes 6684680 | tf_op jit(solution)/shard_map/ppermute | solution.py:122
  168.5 45.6 %collective-permute-start.14 = (bf16[512,2048]{1,0:T(8,128)(2,1)}, bf16[512,2048]{1,0:T(8,128)(2,1)}, u32[]{:S(2)}, u32[]{:S(2)}) collective-permute-start(bf16[512,2048]{1,0:T(8,128)(2,1)} %shard_map.177), channel_id=1, source_target_pairs={{0,1},{1,0},{2,3},{3,2},{4,5},{5,4},{6,7},{7,6},{8,9},{9,8},{10,11... | collective-permute-start | bytes 6291464 | tf_op jit(solution)/shard_map/ppermute | solution.py:122
  175.1 43.7 %collective-permute-start.28 = (bf16[512,2048]{1,0:T(8,128)(2,1)}, bf16[512,2048]{1,0:T(8,128)(2,1)}, u32[]{:S(2)}, u32[]{:S(2)}) collective-permute-start(bf16[512,2048]{1,0:T(8,128)(2,1)} %shard_map.180), channel_id=1, source_target_pairs={{0,1},{1,0},{2,3},{3,2},{4,5},{5,4},{6,7},{7,6},{8,9},{9,8},{10,11... | collective-permute-start | bytes 6291464 | tf_op jit(solution)/shard_map/ppermute | solution.py:122
  195.6 76.8 %all-to-all-start.1 = ((bf16[4,2,768,256]{3,2,1,0:T(8,128)(2,1)}), bf16[4,2,768,256]{3,2,1,0:T(8,128)(2,1)}, u32[]{:S(2)}, u32[]{:S(2)}) async-start(bf16[4,2,768,256]{3,2,1,0:T(8,128)(2,1)} %bitcast.153), calls=%async_computation.1 | async-start | bytes 6291456 | tf_op jit(solution)/shard_map/all_to_all | solution.py:273
  212.5 20.4 %collective-permute-start.35 = (bf16[2,1,768,256]{3,2,1,0:T(8,128)(2,1)S(1)}, bf16[2,1,768,256]{3,2,1,0:T(8,128)(2,1)S(1)}, u32[]{:S(2)}, u32[]{:S(2)}) collective-permute-start(bf16[2,1,768,256]{3,2,1,0:T(8,128)(2,1)S(1)} %get-tuple-element.53), channel_id=1, source_target_pairs={{0,4},{4,0},{8,12},{12,8},{16,20},{20,16},{24,28},{28,24},{1,5},{5... | collective-permute-start | bytes 2359304 | tf_op jit(solution)/shard_map/ppermute | solution.py:99
  216.7 27.4 %collective-permute-start.17 = (bf16[2,2,32,2048]{3,2,1,0:T(8,128)(2,1)S(1)}, bf16[2,2,32,2048]{3,2,1,0:T(8,128)(2,1)S(1)}, u32[]{:S(2)}, u32[]{:S(2)}) collective-permute-start(bf16[2,2,32,2048]{3,2,1,0:T(8,128)(2,1)S(1)} %bitcast.178), channel_id=1, source_target_pairs={{0,4},{4,0},{8,12},{12,8},{16,20},{20,16},{24,28},{28,24},{1,5},{5... | collective-permute-start | bytes 1572872 | tf_op jit(solution)/shard_map/ppermute | solution.py:112
  217.3 28.6 %collective-permute-start.15 = (bf16[2,2,32,2048]{3,2,1,0:T(8,128)(2,1)S(1)}, bf16[2,2,32,2048]{3,2,1,0:T(8,128)(2,1)S(1)}, u32[]{:S(2)}, u32[]{:S(2)}) collective-permute-start(bf16[2,2,32,2048]{3,2,1,0:T(8,128)(2,1)S(1)} %bitcast.176), channel_id=1, source_target_pairs={{0,2},{1,3},{2,0},{3,1},{4,6},{5,7},{6,4},{7,5},{8,10},{9,11},{10,... | collective-permute-start | bytes 1572872 | tf_op jit(solution)/shard_map/ppermute | solution.py:117
  221.3 34.1 %collective-permute-start.31 = (bf16[2,2,32,2048]{3,2,1,0:T(8,128)(2,1)S(1)}, bf16[2,2,32,2048]{3,2,1,0:T(8,128)(2,1)S(1)}, u32[]{:S(2)}, u32[]{:S(2)}) collective-permute-start(bf16[2,2,32,2048]{3,2,1,0:T(8,128)(2,1)S(1)} %bitcast.177), channel_id=1, source_target_pairs={{0,4},{4,0},{8,12},{12,8},{16,20},{20,16},{24,28},{28,24},{1,5},{5... | collective-permute-start | bytes 1572872 | tf_op jit(solution)/shard_map/ppermute | solution.py:112
  223.0 34.1 %collective-permute-start.29 = (bf16[2,2,32,2048]{3,2,1,0:T(8,128)(2,1)S(1)}, bf16[2,2,32,2048]{3,2,1,0:T(8,128)(2,1)S(1)}, u32[]{:S(2)}, u32[]{:S(2)}) collective-permute-start(bf16[2,2,32,2048]{3,2,1,0:T(8,128)(2,1)S(1)} %bitcast.175), channel_id=1, source_target_pairs={{0,2},{1,3},{2,0},{3,1},{4,6},{5,7},{6,4},{7,5},{8,10},{9,11},{10,... | collective-permute-start | bytes 1572872 | tf_op jit(solution)/shard_map/ppermute | solution.py:117
  244.3 14.6 %collective-permute-start.18 = (bf16[2,32,2048]{2,1,0:T(8,128)(2,1)S(1)}, bf16[2,32,2048]{2,1,0:T(8,128)(2,1)S(1)}, u32[]{:S(2)}, u32[]{:S(2)}) collective-permute-start(bf16[2,32,2048]{2,1,0:T(8,128)(2,1)S(1)} %slice_bitcast_fusion.4), channel_id=1, source_target_pairs={{0,2},{1,3},{2,0},{3,1},{4,6},{5,7},{6,4},{7,5},{8,10},{9,11},{10,... | collective-permute-start | bytes 786440 | tf_op jit(solution)/shard_map/ppermute | solution.py:117
  246.0 15.0 %collective-permute-start.16 = (bf16[2,32,2048]{2,1,0:T(8,128)(2,1)S(1)}, bf16[2,32,2048]{2,1,0:T(8,128)(2,1)S(1)}, u32[]{:S(2)}, u32[]{:S(2)}) collective-permute-start(bf16[2,32,2048]{2,1,0:T(8,128)(2,1)S(1)} %slice_bitcast_fusion.6), channel_id=1, source_target_pairs={{0,4},{4,0},{8,12},{12,8},{16,20},{20,16},{24,28},{28,24},{1,5},{5... | collective-permute-start | bytes 786440 | tf_op jit(solution)/shard_map/ppermute | solution.py:112
  255.6 10.1 %collective-permute-start.32 = (bf16[2,32,2048]{2,1,0:T(8,128)(2,1)S(1)}, bf16[2,32,2048]{2,1,0:T(8,128)(2,1)S(1)}, u32[]{:S(2)}, u32[]{:S(2)}) collective-permute-start(bf16[2,32,2048]{2,1,0:T(8,128)(2,1)S(1)} %slice_bitcast_fusion), channel_id=1, source_target_pairs={{0,2},{1,3},{2,0},{3,1},{4,6},{5,7},{6,4},{7,5},{8,10},{9,11},{10,... | collective-permute-start | bytes 786440 | tf_op jit(solution)/shard_map/ppermute | solution.py:117
  257.3 8.4 %collective-permute-start.30 = (bf16[2,32,2048]{2,1,0:T(8,128)(2,1)S(1)}, bf16[2,32,2048]{2,1,0:T(8,128)(2,1)S(1)}, u32[]{:S(2)}, u32[]{:S(2)}) collective-permute-start(bf16[2,32,2048]{2,1,0:T(8,128)(2,1)S(1)} %slice_bitcast_fusion.2), channel_id=1, source_target_pairs={{0,4},{4,0},{8,12},{12,8},{16,20},{20,16},{24,28},{28,24},{1,5},{5... | collective-permute-start | bytes 786440 | tf_op jit(solution)/shard_map/ppermute | solution.py:112
  261.8 27.2 %collective-permute-start.19 = (bf16[64,2048]{1,0:T(8,128)(2,1)}, bf16[64,2048]{1,0:T(8,128)(2,1)}, u32[]{:S(2)}, u32[]{:S(2)}) collective-permute-start(bf16[64,2048]{1,0:T(8,128)(2,1)} %fusion.34), channel_id=1, source_target_pairs={{0,24},{4,28},{8,0},{12,4},{16,8},{20,12},{24,16},{28,20},{1,25},{... | collective-permute-start | bytes 786440 | tf_op jit(solution)/shard_map/ppermute | solution.py:94
  274.8 23.5 %copy-start.1 = (bf16[512,2048]{1,0:T(8,128)(2,1)S(1)}, bf16[512,2048]{1,0:T(8,128)(2,1)}, u32[]{:S(2)}) copy-start(bf16[512,2048]{1,0:T(8,128)(2,1)} %param.27) | copy-start | bytes 6291460
  274.8 22.6 %collective-permute-start.36 = (bf16[2,1,768,256]{3,2,1,0:T(8,128)(2,1)S(1)}, bf16[2,1,768,256]{3,2,1,0:T(8,128)(2,1)S(1)}, u32[]{:S(2)}, u32[]{:S(2)}) collective-permute-start(bf16[2,1,768,256]{3,2,1,0:T(8,128)(2,1)S(1)} %get-tuple-element.51), channel_id=1, source_target_pairs={{0,4},{4,0},{8,12},{12,8},{16,20},{20,16},{24,28},{28,24},{1,5},{5... | collective-permute-start | bytes 2359304 | tf_op jit(solution)/shard_map/ppermute | solution.py:99
  276.5 13.0 %collective-permute-start.33 = (bf16[64,2048]{1,0:T(8,128)(2,1)S(1)}, bf16[64,2048]{1,0:T(8,128)(2,1)S(1)}, u32[]{:S(2)}, u32[]{:S(2)}) collective-permute-start(bf16[64,2048]{1,0:T(8,128)(2,1)S(1)} %get-tuple-element.71), channel_id=1, source_target_pairs={{0,16},{4,20},{8,24},{12,28},{16,0},{20,4},{24,8},{28,12},{1,17},{... | collective-permute-start | bytes 786440 | tf_op jit(solution)/shard_map/ppermute | solution.py:94
  276.5 19.1 %collective-permute-start.34 = (bf16[64,2048]{1,0:T(8,128)(2,1)S(1)}, bf16[64,2048]{1,0:T(8,128)(2,1)S(1)}, u32[]{:S(2)}, u32[]{:S(2)}) collective-permute-start(bf16[64,2048]{1,0:T(8,128)(2,1)S(1)} %get-tuple-element.72), channel_id=1, source_target_pairs={{0,8},{4,12},{8,16},{12,20},{16,24},{20,28},{24,0},{28,4},{1,9},{5... | collective-permute-start | bytes 786440 | tf_op jit(solution)/shard_map/ppermute | solution.py:94
  (17 other events, 72.6 us)

commit v4 on v1

--- a/solution.py
+++ b/solution.py
@@ -203,9 +203,9 @@
     for begin in range(0, pair_count, 2):
         here = spread_tokens(pieces[begin : begin + 2])
         there = flip_core(here)
+        back = flip_core(run_experts(first_slot, there, slot_weights, 256))
         if begin + 2 >= pair_count:
-            there, arrived = together(there, arrived)
-        back = flip_core(run_experts(first_slot, there, slot_weights, 256))
+            here, arrived = together(here, arrived)
         mixed = run_experts(first_slot, here, slot_weights, 256)
         sums = gather_sums(add(mixed, back), 2)
         ready.append(sums)
@@ -406,7 +406,7 @@
     )
     layer_out = (residual + mixture).astype(jnp.bfloat16)
     second = trade_columns(after(take_chunks(held, index, size, size), first))
-    second = after(second, *ready)
+    first = after(first, *ready)
     replica_weights = collect_replicas((first, second), source_slot, slots_here)
     return (layer_out, replica_weights.reshape((1,) + slot_weights.shape[1:]))
 

time: 350 us -> 300 us (0.86)
  waiting for transfers between devices: 174 us -> 125 us
  starting transfers between devices: 60.8 us -> 69.2 us
  local copies, waits for them, and re-layouts: 35.4 us -> 31.4 us
  other arithmetic: 29.5 us -> 26 us
    ppermute x5, waiting for transfers between devices: 0.01 us -> 29.9 us  [swap(): return lax.ppermute(value, 'req', [(i, i ^ mask) for i in range(count)])]
    ppermute x9, waiting for transfers between devices: 77.3 us -> 49.9 us  [flip_pair(): return lax.ppermute(value, 'req', [(i, i ^ 1) for i in range(count)])]
    ppermute x9, waiting for transfers between devices: 34 us -> 10.1 us  [turn_pairs(): lax.ppermute(value, 'req', [(i, (i + 2 * step) % count) for i in range(co...]
    all_to_all x2, waiting for transfers between devices: 30.9 us -> 17.5 us  [trade_columns(): lax.all_to_all(outgoing, 'req', 0, 0, axis_index_groups=columns, tiled=True)]
    ppermute x9, waiting for transfers between devices: 30 us -> 17.4 us  [flip_chip(): return lax.ppermute(value, 'exp', [(i, i ^ 2) for i in range(count)])]
    ppermute x9, starting transfers between devices: 21.5 us -> 28.4 us  [turn_pairs(): lax.ppermute(value, 'req', [(i, (i + 2 * step) % count) for i in range(co...]
    unnamed x69 -> x57, local copies, waits for them, and re-layouts: 15.7 us -> 12.9 us
  transfers between devices with their start and end apart: 39 -> 39, of which waited for: 20 -> 17; matrix products, arithmetic and copies ran while one was open for 14% -> 16% of each run, Pallas kernels for 9% -> 11%
where the time goes in v4:
time: 300 us; the launch traced here: 298 us
  waiting for transfers between devices  125 us (42%)
  starting transfers between devices  69.2 us (23%)
  Pallas kernels  32 us (11%)
  local copies, waits for them, and re-layouts  31.4 us (10%)
  other arithmetic  26 us (9%)
  between operations  9.81 us (3%)
  matrix products  5.19 us (2%)
    ppermute x9, waiting for transfers between devices, flip_pair(): return lax.ppermute(value, 'req', [(i, i ^ 1) for i in range(count)])  49.9 us
    ppermute x5, waiting for transfers between devices, swap(): return lax.ppermute(value, 'req', [(i, i ^ mask) for i in range(count)])  29.9 us
    ppermute x9, starting transfers between devices, turn_pairs(): lax.ppermute(value, 'req', [(i, (i + 2 * step) % count) for i in range(co...  28.4 us
    pallas_call x4, Pallas kernels, run_experts(): pl.pallas_call(experts_kernel, out_shape=jax.ShapeDtypeStruct((count, wid...  22.4 us
    all_to_all x2, waiting for transfers between devices, trade_columns(): lax.all_to_all(outgoing, 'req', 0, 0, axis_index_groups=columns, tiled=True)  17.5 us
    ppermute x9, waiting for transfers between devices, flip_chip(): return lax.ppermute(value, 'exp', [(i, i ^ 2) for i in range(count)])  17.4 us
    unnamed x57, local copies, waits for them, and re-layouts  12.9 us
    ppermute x9, starting transfers between devices, flip_chip(): return lax.ppermute(value, 'exp', [(i, i ^ 2) for i in range(count)])  12.7 us
  transfers between devices with their start and end apart: 39, of which 17 were waited for; matrix products, arithmetic and copies ran while one was open for 16% of the time, Pallas kernels for 11%

profile of v4, /device:TPU:0, one launch (start us, length us, event | category | flops | bytes accessed | tf_op | source)
XLA Modules:
  0.0 298.5 jit_solution(13672999156492135155)
XLA Ops:
  0.6 1.7 fusion.71
  2.4 4.0 %collective-permute-start.1 = (bf16[2,2,32,512]{3,2,1,0:T(8,128)(2,1)}, bf16[2,2,32,512]{3,2,1,0:T(8,128)(2,1)}, u32[]{:S(2)}, u32[]{:S(2)}) collective-permute-start(bf16[2,2,32,512]{3,2,1,0:T(8,128)(2,1)} %get-tuple-element.82), channel_id=1, source_target_pairs={{0,16},{4,20},{8,24},{12,28},{16,0},{20,4},{24,8},{28,12},{1,17},{... | collective-permute-start | bytes 393224 | tf_op jit(solution)/shard_map/ppermute | solution.py:94
  8.0 2.2 collective-permute-start.2
  10.2 5.7 %dynamic-slice_bitcast_fusion = (bf16[2,1536,256]{2,1,0:T(8,128)(2,1)}, bf16[2,1536,256]{2,1,0:T(8,128)(2,1)}, bf16[2,1536,256]{2,1,0:T(8,128)(2,1)}, bf16[2,1536,256]{2,1,0:T(8,128)(2,1)}) fusion(bf16[2,4,1536,256]{3,2,1,0:T(8,128)(2,1)} %bitcast.154, s32[]{:T(128)S(6)} %select_n.262, s32[]{:T(128)S(6)} %select_n.256, s32[]{:T(128)S(6)} %select_n.248, ...), kind=kLoop, calls=%fused_computation.6 | loop fusion | bytes 12582928 | tf_op jit(solution)/shard_map/jit(dynamic_index_in_dim)/squeeze | solution.py:126
  16.0 1.6 collective-permute-start.4
  34.6 19.7 %collective-permute-done.3 = bf16[2,2,32,512]{3,2,1,0:T(8,128)(2,1)S(1)} collective-permute-done((bf16[2,2,32,512]{3,2,1,0:T(8,128)(2,1)S(1)}, bf16[2,2,32,512]{3,2,1,0:T(8,128)(2,1)S(1)}, u32[]{:S(2)}, u32[]{:S(2)}) %collective-permute-start.3) | collective-permute-done | bytes 131104 | tf_op jit(solution)/shard_map/ppermute | solution.py:112
  54.5 2.8 fusion.80
  57.3 1.7 convolution_convert_fusion
  61.3 2.7 collective-permute-start.20
  68.5 6.3 %collective-permute-done.7 = bf16[64,2048]{1,0:T(8,128)(2,1)S(1)} collective-permute-done((bf16[64,2048]{1,0:T(8,128)(2,1)S(1)}, bf16[64,2048]{1,0:T(8,128)(2,1)S(1)}, u32[]{:S(2)}, u32[]{:S(2)}) %collective-permute-start.7) | collective-permute-done | bytes 262176 | tf_op jit(solution)/shard_map/ppermute | solution.py:117
  77.2 3.2 %collective-permute-start.22 = (bf16[64,2176]{1,0:T(8,128)(2,1)S(1)}, bf16[64,2176]{1,0:T(8,128)(2,1)S(1)}, u32[]{:S(2)}, u32[]{:S(2)}) collective-permute-start(bf16[64,2176]{1,0:T(8,128)(2,1)S(1)} %concatenate.37), channel_id=1, source_target_pairs={{0,24},{4,28},{8,0},{12,4},{16,8},{20,12},{24,16},{28,20},{1,25},{... | collective-permute-start | bytes 835592 | tf_op jit(solution)/shard_map/ppermute | solution.py:94
  80.3 28.4 %collective-permute-done.20.refs_3_ = bf16[2,1536,256]{2,1,0:T(8,128)(2,1)} collective-permute-done((bf16[2,1536,256]{2,1,0:T(8,128)(2,1)}, bf16[2,1536,256]{2,1,0:T(8,128)(2,1)}, u32[]{:S(2)}, u32[]{:S(2)}) %collective-permute-start.20) | collective-permute-done | bytes 1572896 | tf_op jit(solution)/shard_map/ppermute | solution.py:99
  108.7 4.8 %shard_map.178 = bf16[8,768,256]{2,1,0:T(8,128)(2,1)S(1)} custom-call(s32[8]{0:T(128)S(1)} %fusion.52.index_ref, bf16[2,1536,256]{2,1,0:T(8,128)(2,1)S(1)} %copy-done.2, bf16[2,1536,256]{2,1,0:T(8,128)(2,1)} %collective-permute-done.4.refs_1_, bf16[2,1536,256]{2,1,0:T(8,128)(2,1)} %collective-permute-done.5.refs_2_, ...), custom_call_target="tpu_custom_call" | custom-call | bytes 6291456 | tf_op jit(solution)/shard_map/pallas_call | solution.py:254
  116.6 3.5 %collective-permute-done.21 = bf16[64,2176]{1,0:T(8,128)(2,1)S(1)} collective-permute-done((bf16[64,2176]{1,0:T(8,128)(2,1)S(1)}, bf16[64,2176]{1,0:T(8,128)(2,1)S(1)}, u32[]{:S(2)}, u32[]{:S(2)}) %collective-permute-start.21) | collective-permute-done | bytes 278560 | tf_op jit(solution)/shard_map/ppermute | solution.py:94
  121.8 2.8 collective-permute-done.11
  127.7 4.9 %all-to-all-start = ((bf16[4,2,768,256]{3,2,1,0:T(8,128)(2,1)}), bf16[4,2,768,256]{3,2,1,0:T(8,128)(2,1)}, u32[]{:S(2)}, u32[]{:S(2)}) async-start(bf16[4,2,768,256]{3,2,1,0:T(8,128)(2,1)} %bitcast.152), calls=%async_computation | async-start | bytes 6291456 | tf_op jit(solution)/shard_map/all_to_all | solution.py:274
  135.7 4.6 %collective-permute-done.12 = bf16[2,2,32,2176]{3,2,1,0:T(8,128)(2,1)} collective-permute-done((bf16[2,2,32,2176]{3,2,1,0:T(8,128)(2,1)S(1)}, bf16[2,2,32,2176]{3,2,1,0:T(8,128)(2,1)}, u32[]{:S(2)}, u32[]{:S(2)}) %collective-permute-start.12) | collective-permute-done | bytes 557088 | tf_op jit(solution)/shard_map/ppermute | solution.py:112
  140.4 3.0 pad_maximum_fusion.tok_ref
  145.9 4.3 %collective-permute-done.26 = bf16[2,2,32,2176]{3,2,1,0:T(8,128)(2,1)S(1)} collective-permute-done((bf16[2,2,32,2176]{3,2,1,0:T(8,128)(2,1)S(1)}, bf16[2,2,32,2176]{3,2,1,0:T(8,128)(2,1)S(1)}, u32[]{:S(2)}, u32[]{:S(2)}) %collective-permute-start.26) | collective-permute-done | bytes 557088 | tf_op jit(solution)/shard_map/ppermute | solution.py:112
  150.2 8.3 %collective-permute-done.24 = bf16[2,2,32,2176]{3,2,1,0:T(8,128)(2,1)S(1)} collective-permute-done((bf16[2,2,32,2176]{3,2,1,0:T(8,128)(2,1)S(1)}, bf16[2,2,32,2176]{3,2,1,0:T(8,128)(2,1)S(1)}, u32[]{:S(2)}, u32[]{:S(2)}) %collective-permute-start.24) | collective-permute-done | bytes 557088 | tf_op jit(solution)/shard_map/ppermute | solution.py:117
  160.0 2.8 copy-done.5
  162.8 6.1 %shard_map.177 = bf16[512,2048]{1,0:T(8,128)(2,1)} custom-call(s32[1]{0:T(128)} %bitcast.35.first_slot_ref, bf16[512,2176]{1,0:T(8,128)(2,1)} %collective-permute-done.13.tok_ref, bf16[2,3,2048,256]{3,2,1,0:T(8,128)(2,1)S(1)} %copy-done.5), custom_call_target="tpu_custom_call" | custom-call | flops 3221225472 | bytes 10485760 | tf_op jit(solution)/shard_map/pallas_call | solution.py:73
  169.4 6.0 %shard_map.180 = bf16[512,2048]{1,0:T(8,128)(2,1)} custom-call(s32[1]{0:T(128)} %bitcast.35.first_slot_ref, bf16[512,2176]{1,0:T(8,128)(2,1)} %collective-permute-done.27.tok_ref, bf16[2,3,2048,256]{3,2,1,0:T(8,128)(2,1)S(1)} %copy-done.5), custom_call_target="tpu_custom_call" | custom-call | flops 3221225472 | bytes 10485760 | tf_op jit(solution)/shard_map/pallas_call | solution.py:73
  177.4 4.8 %shard_map.181 = bf16[8,768,256]{2,1,0:T(8,128)(2,1)S(1)} custom-call(s32[8]{0:T(128)S(1)} %fusion.52.index_ref, bf16[2,1536,256]{2,1,0:T(8,128)(2,1)S(1)} %copy-done.2, bf16[2,1536,256]{2,1,0:T(8,128)(2,1)} %collective-permute-done.4.refs_1_, bf16[2,1536,256]{2,1,0:T(8,128)(2,1)} %collective-permute-done.5.refs_2_, ...), custom_call_target="tpu_custom_call" | custom-call | bytes 6291456 | tf_op jit(solution)/shard_map/pallas_call | solution.py:254
  182.2 1.6 copy-done.4
  183.8 2.8 copy-done.6
  186.6 5.1 %shard_map.176 = bf16[512,2048]{1,0:T(8,128)(2,1)S(1)} custom-call(s32[1]{0:T(128)} %bitcast.35.first_slot_ref, bf16[512,2176]{1,0:T(8,128)(2,1)} %pad_maximum_fusion.tok_ref, bf16[2,3,2048,256]{3,2,1,0:T(8,128)(2,1)S(1)} %copy-done.6), custom_call_target="tpu_custom_call" | custom-call | flops 3221225472 | bytes 10485760 | tf_op jit(solution)/shard_map/pallas_call | solution.py:73
  191.7 3.9 %all-to-all-done = bf16[4,2,768,256]{3,2,1,0:T(8,128)(2,1)} async-done(((bf16[4,2,768,256]{3,2,1,0:T(8,128)(2,1)}), bf16[4,2,768,256]{3,2,1,0:T(8,128)(2,1)}, u32[]{:S(2)}, u32[]{:S(2)}) %all-to-all-start) | async-done | bytes 3145760 | tf_op jit(solution)/shard_map/all_to_all | solution.py:274
  195.6 4.7 %all-to-all-start.1 = ((bf16[4,2,768,256]{3,2,1,0:T(8,128)(2,1)}), bf16[4,2,768,256]{3,2,1,0:T(8,128)(2,1)}, u32[]{:S(2)}, u32[]{:S(2)}) async-start(bf16[4,2,768,256]{3,2,1,0:T(8,128)(2,1)} %bitcast.153), calls=%async_computation.1 | async-start | bytes 6291456 | tf_op jit(solution)/shard_map/all_to_all | solution.py:274
  200.3 1.9 broadcast_in_dim.162
  202.1 2.4 constant_dynamic-slice_fusion.1
  206.1 2.8 copy-done.7
  208.9 5.2 %shard_map.179 = bf16[512,2048]{1,0:T(8,128)(2,1)S(1)} custom-call(s32[1]{0:T(128)} %bitcast.35.first_slot_ref, bf16[512,2176]{1,0:T(8,128)(2,1)} %pad_maximum_fusion.1.tok_ref, bf16[2,3,2048,256]{3,2,1,0:T(8,128)(2,1)S(1)} %copy-done.7), custom_call_target="tpu_custom_call" | custom-call | flops 3221225472 | bytes 10485760 | tf_op jit(solution)/shard_map/pallas_call | solution.py:73
  214.1 2.4 add_convert_fusion.1
  218.7 2.4 add_convert_fusion
  221.3 1.6 collective-permute-start.31
  225.9 10.3 %collective-permute-done.17 = bf16[2,2,32,2048]{3,2,1,0:T(8,128)(2,1)S(1)} collective-permute-done((bf16[2,2,32,2048]{3,2,1,0:T(8,128)(2,1)S(1)}, bf16[2,2,32,2048]{3,2,1,0:T(8,128)(2,1)S(1)}, u32[]{:S(2)}, u32[]{:S(2)}) %collective-permute-start.17) | collective-permute-done | bytes 524320 | tf_op jit(solution)/shard_map/ppermute | solution.py:112
  238.0 1.6 collective-permute-start.16
  239.6 7.8 %collective-permute-done.31 = bf16[2,2,32,2048]{3,2,1,0:T(8,128)(2,1)S(1)} collective-permute-done((bf16[2,2,32,2048]{3,2,1,0:T(8,128)(2,1)S(1)}, bf16[2,2,32,2048]{3,2,1,0:T(8,128)(2,1)S(1)}, u32[]{:S(2)}, u32[]{:S(2)}) %collective-permute-start.31) | collective-permute-done | bytes 524320 | tf_op jit(solution)/shard_map/ppermute | solution.py:112
  249.2 1.6 collective-permute-start.30
  251.0 2.1 collective-permute-done.16
  253.8 3.8 %collective-permute-start.19 = (bf16[64,2048]{1,0:T(8,128)(2,1)}, bf16[64,2048]{1,0:T(8,128)(2,1)}, u32[]{:S(2)}, u32[]{:S(2)}) collective-permute-start(bf16[64,2048]{1,0:T(8,128)(2,1)} %fusion.36), channel_id=1, source_target_pairs={{0,24},{4,28},{8,0},{12,4},{16,8},{20,12},{24,16},{28,20},{1,25},{... | collective-permute-start | bytes 786440 | tf_op jit(solution)/shard_map/ppermute | solution.py:94
  258.5 13.6 %all-to-all-done.1 = bf16[4,2,768,256]{3,2,1,0:T(8,128)(2,1)} async-done(((bf16[4,2,768,256]{3,2,1,0:T(8,128)(2,1)}), bf16[4,2,768,256]{3,2,1,0:T(8,128)(2,1)}, u32[]{:S(2)}, u32[]{:S(2)}) %all-to-all-start.1) | async-done | bytes 3145760 | tf_op jit(solution)/shard_map/all_to_all | solution.py:274
  272.1 2.4 constant_dynamic-slice_fusion
  274.5 1.8 collective-permute-start.36
  276.4 12.7 %collective-permute-start.34 = (bf16[64,2048]{1,0:T(8,128)(2,1)S(1)}, bf16[64,2048]{1,0:T(8,128)(2,1)S(1)}, u32[]{:S(2)}, u32[]{:S(2)}) collective-permute-start(bf16[64,2048]{1,0:T(8,128)(2,1)S(1)} %get-tuple-element.72), channel_id=1, source_target_pairs={{0,8},{4,12},{8,16},{12,20},{16,24},{20,28},{24,0},{28,4},{1,9},{5... | collective-permute-start | bytes 786440 | tf_op jit(solution)/shard_map/ppermute | solution.py:94
  289.3 6.5 %collective-permute-done.34 = bf16[64,2048]{1,0:T(8,128)(2,1)S(1)} collective-permute-done((bf16[64,2048]{1,0:T(8,128)(2,1)S(1)}, bf16[64,2048]{1,0:T(8,128)(2,1)S(1)}, u32[]{:S(2)}, u32[]{:S(2)}) %collective-permute-start.34) | collective-permute-done | bytes 262176 | tf_op jit(solution)/shard_map/ppermute | solution.py:94
  295.8 1.8 fusion.14
  (188 shorter events, 50.0 us)
Async XLA Ops:
  0.6 58.4 %copy-start = (bf16[512,2048]{1,0:T(8,128)(2,1)S(1)}, bf16[512,2048]{1,0:T(8,128)(2,1)}, u32[]{:S(2)}) copy-start(bf16[512,2048]{1,0:T(8,128)(2,1)} %param.27) | copy-start | bytes 6291460
  2.4 29.7 %collective-permute-start.1 = (bf16[2,2,32,512]{3,2,1,0:T(8,128)(2,1)}, bf16[2,2,32,512]{3,2,1,0:T(8,128)(2,1)}, u32[]{:S(2)}, u32[]{:S(2)}) collective-permute-start(bf16[2,2,32,512]{3,2,1,0:T(8,128)(2,1)} %get-tuple-element.82), channel_id=1, source_target_pairs={{0,16},{4,20},{8,24},{12,28},{16,0},{20,4},{24,8},{28,12},{1,17},{... | collective-permute-start | bytes 393224 | tf_op jit(solution)/shard_map/ppermute | solution.py:94
  6.4 25.7 %collective-permute-start = (bf16[2,2,32,512]{3,2,1,0:T(8,128)(2,1)}, bf16[2,2,32,512]{3,2,1,0:T(8,128)(2,1)}, u32[]{:S(2)}, u32[]{:S(2)}) collective-permute-start(bf16[2,2,32,512]{3,2,1,0:T(8,128)(2,1)} %get-tuple-element.82), channel_id=1, source_target_pairs={{0,8},{4,12},{8,16},{12,20},{16,24},{20,28},{24,0},{28,4},{1,9},{5... | collective-permute-start | bytes 393224 | tf_op jit(solution)/shard_map/ppermute | solution.py:94
  8.0 24.2 %collective-permute-start.2 = (bf16[2,2,32,512]{3,2,1,0:T(8,128)(2,1)}, bf16[2,2,32,512]{3,2,1,0:T(8,128)(2,1)}, u32[]{:S(2)}, u32[]{:S(2)}) collective-permute-start(bf16[2,2,32,512]{3,2,1,0:T(8,128)(2,1)} %get-tuple-element.82), channel_id=1, source_target_pairs={{0,24},{4,28},{8,0},{12,4},{16,8},{20,12},{24,16},{28,20},{1,25},{... | collective-permute-start | bytes 393224 | tf_op jit(solution)/shard_map/ppermute | solution.py:94
  10.2 8.9 %copy-start.13 = (bf16[256,512]{1,0:T(8,128)(2,1)S(1)}, bf16[256,512]{1,0:T(8,128)(2,1)}, u32[]{:S(2)}) copy-start(bf16[256,512]{1,0:T(8,128)(2,1)} %param.18) | copy-start | bytes 786436
  10.2 9.1 %copy-start.14 = (bf16[256,512]{1,0:T(8,128)(2,1)S(1)}, bf16[256,512]{1,0:T(8,128)(2,1)}, u32[]{:S(2)}) copy-start(bf16[256,512]{1,0:T(8,128)(2,1)} %param.19) | copy-start | bytes 786436
  15.9 43.1 %collective-permute-start.5 = (bf16[2,1536,256]{2,1,0:T(8,128)(2,1)}, bf16[2,1536,256]{2,1,0:T(8,128)(2,1)}, u32[]{:S(2)}, u32[]{:S(2)}) collective-permute-start(bf16[2,1536,256]{2,1,0:T(8,128)(2,1)} %get-tuple-element.49), channel_id=1, source_target_pairs={{0,8},{4,12},{8,0},{12,4},{16,24},{20,28},{24,16},{28,20},{1,9},{5... | collective-permute-start | bytes 4718600 | tf_op jit(solution)/shard_map/ppermute | solution.py:99
  16.0 43.1 %collective-permute-start.4 = (bf16[2,1536,256]{2,1,0:T(8,128)(2,1)}, bf16[2,1536,256]{2,1,0:T(8,128)(2,1)}, u32[]{:S(2)}, u32[]{:S(2)}) collective-permute-start(bf16[2,1536,256]{2,1,0:T(8,128)(2,1)} %get-tuple-element.50), channel_id=1, source_target_pairs={{0,4},{4,0},{8,12},{12,8},{16,20},{20,16},{24,28},{28,24},{1,5},{5... | collective-permute-start | bytes 4718600 | tf_op jit(solution)/shard_map/ppermute | solution.py:99
  33.3 21.0 %collective-permute-start.3 = (bf16[2,2,32,512]{3,2,1,0:T(8,128)(2,1)S(1)}, bf16[2,2,32,512]{3,2,1,0:T(8,128)(2,1)S(1)}, u32[]{:S(2)}, u32[]{:S(2)}) collective-permute-start(bf16[2,2,32,512]{3,2,1,0:T(8,128)(2,1)S(1)} %pad_maximum_fusion.12), channel_id=1, source_target_pairs={{0,4},{4,0},{8,12},{12,8},{16,20},{20,16},{24,28},{28,24},{1,5},{5... | collective-permute-start | bytes 393224 | tf_op jit(solution)/shard_map/ppermute | solution.py:112
  59.8 8.5 %copy-start.25 = (s32[8]{0:T(128)S(1)}, s32[8]{0:T(128)}, u32[]{:S(2)}) copy-start(s32[8]{0:T(128)} %param.32) | copy-start | bytes 100
  59.8 15.1 %copy-start.16 = (bf16[64,2048]{1,0:T(8,128)(2,1)S(1)}, bf16[64,2048]{1,0:T(8,128)(2,1)}, u32[]{:S(2)}) copy-start(bf16[64,2048]{1,0:T(8,128)(2,1)} %param.17) | copy-start | bytes 786436
  61.2 2.9 collective-permute-start.6
  61.3 47.4 %collective-permute-start.20 = (bf16[2,1536,256]{2,1,0:T(8,128)(2,1)}, bf16[2,1536,256]{2,1,0:T(8,128)(2,1)}, u32[]{:S(2)}, u32[]{:S(2)}) collective-permute-start(bf16[2,1536,256]{2,1,0:T(8,128)(2,1)} %get-tuple-element.48), channel_id=1, source_target_pairs={{0,12},{4,8},{8,4},{12,0},{16,28},{20,24},{24,20},{28,16},{1,13},{... | collective-permute-start | bytes 4718600 | tf_op jit(solution)/shard_map/ppermute | solution.py:99
  64.0 12.1 %copy-start.17 = (f32[2048]{0:T(1024)S(1)}, f32[2048]{0:T(1024)}, u32[]{:S(2)}) copy-start(f32[2048]{0:T(1024)} %param.28) | copy-start | bytes 24580
  66.4 42.3 %copy-start.2 = (bf16[2,1536,256]{2,1,0:T(8,128)(2,1)S(1)}, bf16[2,1536,256]{2,1,0:T(8,128)(2,1)}, u32[]{:S(2)}) copy-start(bf16[2,1536,256]{2,1,0:T(8,128)(2,1)} %get-tuple-element.47.refs_0_) | copy-start | bytes 4718596
  66.4 8.4 %collective-permute-start.7 = (bf16[64,2048]{1,0:T(8,128)(2,1)S(1)}, bf16[64,2048]{1,0:T(8,128)(2,1)S(1)}, u32[]{:S(2)}, u32[]{:S(2)}) collective-permute-start(bf16[64,2048]{1,0:T(8,128)(2,1)S(1)} %fusion.28), channel_id=1, source_target_pairs={{0,2},{1,3},{2,0},{3,1},{4,6},{5,7},{6,4},{7,5},{8,10},{9,11},{10,... | collective-permute-start | bytes 786440 | tf_op jit(solution)/shard_map/ppermute | solution.py:117
  76.4 37.2 %collective-permute-start.8 = (bf16[64,2176]{1,0:T(8,128)(2,1)S(1)}, bf16[64,2176]{1,0:T(8,128)(2,1)S(1)}, u32[]{:S(2)}, u32[]{:S(2)}) collective-permute-start(bf16[64,2176]{1,0:T(8,128)(2,1)S(1)} %concatenate.37), channel_id=1, source_target_pairs={{0,8},{4,12},{8,16},{12,20},{16,24},{20,28},{24,0},{28,4},{1,9},{5... | collective-permute-start | bytes 835592 | tf_op jit(solution)/shard_map/ppermute | solution.py:94
  77.2 43.0 %collective-permute-start.22 = (bf16[64,2176]{1,0:T(8,128)(2,1)S(1)}, bf16[64,2176]{1,0:T(8,128)(2,1)S(1)}, u32[]{:S(2)}, u32[]{:S(2)}) collective-permute-start(bf16[64,2176]{1,0:T(8,128)(2,1)S(1)} %concatenate.37), channel_id=1, source_target_pairs={{0,24},{4,28},{8,0},{12,4},{16,8},{20,12},{24,16},{28,20},{1,25},{... | collective-permute-start | bytes 835592 | tf_op jit(solution)/shard_map/ppermute | solution.py:94
  108.7 11.5 %collective-permute-start.21 = (bf16[64,2176]{1,0:T(8,128)(2,1)S(1)}, bf16[64,2176]{1,0:T(8,128)(2,1)S(1)}, u32[]{:S(2)}, u32[]{:S(2)}) collective-permute-start(bf16[64,2176]{1,0:T(8,128)(2,1)S(1)} %concatenate.37), channel_id=1, source_target_pairs={{0,16},{4,20},{8,24},{12,28},{16,0},{20,4},{24,8},{28,12},{1,17},{... | collective-permute-start | bytes 835592 | tf_op jit(solution)/shard_map/ppermute | solution.py:94
  113.5 12.7 %copy-start.3 = (bf16[8,768,256]{2,1,0:T(8,128)(2,1)}, bf16[8,768,256]{2,1,0:T(8,128)(2,1)S(1)}, u32[]{:S(2)}) copy-start(bf16[8,768,256]{2,1,0:T(8,128)(2,1)S(1)} %shard_map.178) | copy-start | bytes 9437188
  113.6 11.7 %collective-permute-start.9 = (bf16[2,32,2176]{2,1,0:T(8,128)(2,1)S(1)}, bf16[2,32,2176]{2,1,0:T(8,128)(2,1)S(1)}, u32[]{:S(2)}, u32[]{:S(2)}) collective-permute-start(bf16[2,32,2176]{2,1,0:T(8,128)(2,1)S(1)} %get-tuple-element.67), channel_id=1, source_target_pairs={{0,4},{4,0},{8,12},{12,8},{16,20},{20,16},{24,28},{28,24},{1,5},{5... | collective-permute-start | bytes 835592 | tf_op jit(solution)/shard_map/ppermute | solution.py:112
  115.1 9.4 %collective-permute-start.11 = (bf16[2,32,2176]{2,1,0:T(8,128)(2,1)S(1)}, bf16[2,32,2176]{2,1,0:T(8,128)(2,1)S(1)}, u32[]{:S(2)}, u32[]{:S(2)}) collective-permute-start(bf16[2,32,2176]{2,1,0:T(8,128)(2,1)S(1)} %get-tuple-element.68), channel_id=1, source_target_pairs={{0,2},{1,3},{2,0},{3,1},{4,6},{5,7},{6,4},{7,5},{8,10},{9,11},{10,... | collective-permute-start | bytes 835592 | tf_op jit(solution)/shard_map/ppermute | solution.py:117
  120.2 13.8 %collective-permute-start.25 = (bf16[2,32,2176]{2,1,0:T(8,128)(2,1)S(1)}, bf16[2,32,2176]{2,1,0:T(8,128)(2,1)}, u32[]{:S(2)}, u32[]{:S(2)}) collective-permute-start(bf16[2,32,2176]{2,1,0:T(8,128)(2,1)S(1)} %get-tuple-element.70), channel_id=1, source_target_pairs={{0,2},{1,3},{2,0},{3,1},{4,6},{5,7},{6,4},{7,5},{8,10},{9,11},{10,... | collective-permute-start | bytes 835592 | tf_op jit(solution)/shard_map/ppermute | solution.py:117
  124.6 15.7 %collective-permute-start.12 = (bf16[2,2,32,2176]{3,2,1,0:T(8,128)(2,1)S(1)}, bf16[2,2,32,2176]{3,2,1,0:T(8,128)(2,1)}, u32[]{:S(2)}, u32[]{:S(2)}) collective-permute-start(bf16[2,2,32,2176]{3,2,1,0:T(8,128)(2,1)S(1)} %pad_maximum_fusion.5), channel_id=1, source_target_pairs={{0,4},{4,0},{8,12},{12,8},{16,20},{20,16},{24,28},{28,24},{1,5},{5... | collective-permute-start | bytes 1671176 | tf_op jit(solution)/shard_map/ppermute | solution.py:112
  126.2 14.2 %collective-permute-start.10 = (bf16[2,2,32,2176]{3,2,1,0:T(8,128)(2,1)}, bf16[2,2,32,2176]{3,2,1,0:T(8,128)(2,1)}, u32[]{:S(2)}, u32[]{:S(2)}) collective-permute-start(bf16[2,2,32,2176]{3,2,1,0:T(8,128)(2,1)} %pad_maximum_fusion.4), channel_id=1, source_target_pairs={{0,2},{1,3},{2,0},{3,1},{4,6},{5,7},{6,4},{7,5},{8,10},{9,11},{10,... | collective-permute-start | bytes 1671176 | tf_op jit(solution)/shard_map/ppermute | solution.py:117
  127.7 67.9 %all-to-all-start = ((bf16[4,2,768,256]{3,2,1,0:T(8,128)(2,1)}), bf16[4,2,768,256]{3,2,1,0:T(8,128)(2,1)}, u32[]{:S(2)}, u32[]{:S(2)}) async-start(bf16[4,2,768,256]{3,2,1,0:T(8,128)(2,1)} %bitcast.152), calls=%async_computation | async-start | bytes 6291456 | tf_op jit(solution)/shard_map/all_to_all | solution.py:274
  132.5 11.7 %collective-permute-start.23 = (bf16[2,32,2176]{2,1,0:T(8,128)(2,1)S(1)}, bf16[2,32,2176]{2,1,0:T(8,128)(2,1)S(1)}, u32[]{:S(2)}, u32[]{:S(2)}) collective-permute-start(bf16[2,32,2176]{2,1,0:T(8,128)(2,1)S(1)} %get-tuple-element.69), channel_id=1, source_target_pairs={{0,4},{4,0},{8,12},{12,8},{16,20},{20,16},{24,28},{28,24},{1,5},{5... | collective-permute-start | bytes 835592 | tf_op jit(solution)/shard_map/ppermute | solution.py:112
  135.0 15.2 %collective-permute-start.26 = (bf16[2,2,32,2176]{3,2,1,0:T(8,128)(2,1)S(1)}, bf16[2,2,32,2176]{3,2,1,0:T(8,128)(2,1)S(1)}, u32[]{:S(2)}, u32[]{:S(2)}) collective-permute-start(bf16[2,2,32,2176]{3,2,1,0:T(8,128)(2,1)S(1)} %pad_maximum_fusion.7), channel_id=1, source_target_pairs={{0,4},{4,0},{8,12},{12,8},{16,20},{20,16},{24,28},{28,24},{1,5},{5... | collective-permute-start | bytes 1671176 | tf_op jit(solution)/shard_map/ppermute | solution.py:112
  143.3 16.7 %collective-permute-start.13 = (bf16[512,2176]{1,0:T(8,128)(2,1)}, bf16[512,2176]{1,0:T(8,128)(2,1)}, u32[]{:S(2)}, u32[]{:S(2)}) collective-permute-start(bf16[512,2176]{1,0:T(8,128)(2,1)} %pad_maximum_fusion.tok_ref), channel_id=1, source_target_pairs={{0,1},{1,0},{2,3},{3,2},{4,5},{5,4},{6,7},{7,6},{8,9},{9,8},{10,11... | collective-permute-start | bytes 6684680 | tf_op jit(solution)/shard_map/ppermute | solution.py:122
  144.3 14.2 %collective-permute-start.24 = (bf16[2,2,32,2176]{3,2,1,0:T(8,128)(2,1)S(1)}, bf16[2,2,32,2176]{3,2,1,0:T(8,128)(2,1)S(1)}, u32[]{:S(2)}, u32[]{:S(2)}) collective-permute-start(bf16[2,2,32,2176]{3,2,1,0:T(8,128)(2,1)S(1)} %pad_maximum_fusion.6), channel_id=1, source_target_pairs={{0,2},{1,3},{2,0},{3,1},{4,6},{5,7},{6,4},{7,5},{8,10},{9,11},{10,... | collective-permute-start | bytes 1671176 | tf_op jit(solution)/shard_map/ppermute | solution.py:117
  160.0 9.4 %collective-permute-start.27 = (bf16[512,2176]{1,0:T(8,128)(2,1)}, bf16[512,2176]{1,0:T(8,128)(2,1)}, u32[]{:S(2)}, u32[]{:S(2)}) collective-permute-start(bf16[512,2176]{1,0:T(8,128)(2,1)} %pad_maximum_fusion.1.tok_ref), channel_id=1, source_target_pairs={{0,1},{1,0},{2,3},{3,2},{4,5},{5,4},{6,7},{7,6},{8,9},{9,8},{10,11... | collective-permute-start | bytes 6684680 | tf_op jit(solution)/shard_map/ppermute | solution.py:122
  168.9 45.2 %collective-permute-start.14 = (bf16[512,2048]{1,0:T(8,128)(2,1)}, bf16[512,2048]{1,0:T(8,128)(2,1)}, u32[]{:S(2)}, u32[]{:S(2)}) collective-permute-start(bf16[512,2048]{1,0:T(8,128)(2,1)} %shard_map.177), channel_id=1, source_target_pairs={{0,1},{1,0},{2,3},{3,2},{4,5},{5,4},{6,7},{7,6},{8,9},{9,8},{10,11... | collective-permute-start | bytes 6291464 | tf_op jit(solution)/shard_map/ppermute | solution.py:122
  175.4 43.3 %collective-permute-start.28 = (bf16[512,2048]{1,0:T(8,128)(2,1)}, bf16[512,2048]{1,0:T(8,128)(2,1)}, u32[]{:S(2)}, u32[]{:S(2)}) collective-permute-start(bf16[512,2048]{1,0:T(8,128)(2,1)} %shard_map.180), channel_id=1, source_target_pairs={{0,1},{1,0},{2,3},{3,2},{4,5},{5,4},{6,7},{7,6},{8,9},{9,8},{10,11... | collective-permute-start | bytes 6291464 | tf_op jit(solution)/shard_map/ppermute | solution.py:122
  195.6 76.5 %all-to-all-start.1 = ((bf16[4,2,768,256]{3,2,1,0:T(8,128)(2,1)}), bf16[4,2,768,256]{3,2,1,0:T(8,128)(2,1)}, u32[]{:S(2)}, u32[]{:S(2)}) async-start(bf16[4,2,768,256]{3,2,1,0:T(8,128)(2,1)} %bitcast.153), calls=%async_computation.1 | async-start | bytes 6291456 | tf_op jit(solution)/shard_map/all_to_all | solution.py:274
  204.5 20.5 %collective-permute-start.35 = (bf16[2,1,768,256]{3,2,1,0:T(8,128)(2,1)S(1)}, bf16[2,1,768,256]{3,2,1,0:T(8,128)(2,1)S(1)}, u32[]{:S(2)}, u32[]{:S(2)}) collective-permute-start(bf16[2,1,768,256]{3,2,1,0:T(8,128)(2,1)S(1)} %get-tuple-element.53), channel_id=1, source_target_pairs={{0,4},{4,0},{8,12},{12,8},{16,20},{20,16},{24,28},{28,24},{1,5},{5... | collective-permute-start | bytes 2359304 | tf_op jit(solution)/shard_map/ppermute | solution.py:99
  216.7 19.5 %collective-permute-start.17 = (bf16[2,2,32,2048]{3,2,1,0:T(8,128)(2,1)S(1)}, bf16[2,2,32,2048]{3,2,1,0:T(8,128)(2,1)S(1)}, u32[]{:S(2)}, u32[]{:S(2)}) collective-permute-start(bf16[2,2,32,2048]{3,2,1,0:T(8,128)(2,1)S(1)} %bitcast.178), channel_id=1, source_target_pairs={{0,4},{4,0},{8,12},{12,8},{16,20},{20,16},{24,28},{28,24},{1,5},{5... | collective-permute-start | bytes 1572872 | tf_op jit(solution)/shard_map/ppermute | solution.py:112
  217.2 20.6 %collective-permute-start.15 = (bf16[2,2,32,2048]{3,2,1,0:T(8,128)(2,1)S(1)}, bf16[2,2,32,2048]{3,2,1,0:T(8,128)(2,1)S(1)}, u32[]{:S(2)}, u32[]{:S(2)}) collective-permute-start(bf16[2,2,32,2048]{3,2,1,0:T(8,128)(2,1)S(1)} %bitcast.176), channel_id=1, source_target_pairs={{0,2},{1,3},{2,0},{3,1},{4,6},{5,7},{6,4},{7,5},{8,10},{9,11},{10,... | collective-permute-start | bytes 1572872 | tf_op jit(solution)/shard_map/ppermute | solution.py:117
  221.3 26.1 %collective-permute-start.31 = (bf16[2,2,32,2048]{3,2,1,0:T(8,128)(2,1)S(1)}, bf16[2,2,32,2048]{3,2,1,0:T(8,128)(2,1)S(1)}, u32[]{:S(2)}, u32[]{:S(2)}) collective-permute-start(bf16[2,2,32,2048]{3,2,1,0:T(8,128)(2,1)S(1)} %bitcast.177), channel_id=1, source_target_pairs={{0,4},{4,0},{8,12},{12,8},{16,20},{20,16},{24,28},{28,24},{1,5},{5... | collective-permute-start | bytes 1572872 | tf_op jit(solution)/shard_map/ppermute | solution.py:112
  222.9 26.2 %collective-permute-start.29 = (bf16[2,2,32,2048]{3,2,1,0:T(8,128)(2,1)S(1)}, bf16[2,2,32,2048]{3,2,1,0:T(8,128)(2,1)S(1)}, u32[]{:S(2)}, u32[]{:S(2)}) collective-permute-start(bf16[2,2,32,2048]{3,2,1,0:T(8,128)(2,1)S(1)} %bitcast.175), channel_id=1, source_target_pairs={{0,2},{1,3},{2,0},{3,1},{4,6},{5,7},{6,4},{7,5},{8,10},{9,11},{10,... | collective-permute-start | bytes 1572872 | tf_op jit(solution)/shard_map/ppermute | solution.py:117
  236.4 14.5 %collective-permute-start.18 = (bf16[2,32,2048]{2,1,0:T(8,128)(2,1)S(1)}, bf16[2,32,2048]{2,1,0:T(8,128)(2,1)S(1)}, u32[]{:S(2)}, u32[]{:S(2)}) collective-permute-start(bf16[2,32,2048]{2,1,0:T(8,128)(2,1)S(1)} %slice_bitcast_fusion.4), channel_id=1, source_target_pairs={{0,2},{1,3},{2,0},{3,1},{4,6},{5,7},{6,4},{7,5},{8,10},{9,11},{10,... | collective-permute-start | bytes 786440 | tf_op jit(solution)/shard_map/ppermute | solution.py:117
  238.0 15.0 %collective-permute-start.16 = (bf16[2,32,2048]{2,1,0:T(8,128)(2,1)S(1)}, bf16[2,32,2048]{2,1,0:T(8,128)(2,1)S(1)}, u32[]{:S(2)}, u32[]{:S(2)}) collective-permute-start(bf16[2,32,2048]{2,1,0:T(8,128)(2,1)S(1)} %slice_bitcast_fusion.6), channel_id=1, source_target_pairs={{0,4},{4,0},{8,12},{12,8},{16,20},{20,16},{24,28},{28,24},{1,5},{5... | collective-permute-start | bytes 786440 | tf_op jit(solution)/shard_map/ppermute | solution.py:112
  247.6 10.0 %collective-permute-start.32 = (bf16[2,32,2048]{2,1,0:T(8,128)(2,1)S(1)}, bf16[2,32,2048]{2,1,0:T(8,128)(2,1)S(1)}, u32[]{:S(2)}, u32[]{:S(2)}) collective-permute-start(bf16[2,32,2048]{2,1,0:T(8,128)(2,1)S(1)} %slice_bitcast_fusion), channel_id=1, source_target_pairs={{0,2},{1,3},{2,0},{3,1},{4,6},{5,7},{6,4},{7,5},{8,10},{9,11},{10,... | collective-permute-start | bytes 786440 | tf_op jit(solution)/shard_map/ppermute | solution.py:117
  249.2 8.5 %collective-permute-start.30 = (bf16[2,32,2048]{2,1,0:T(8,128)(2,1)S(1)}, bf16[2,32,2048]{2,1,0:T(8,128)(2,1)S(1)}, u32[]{:S(2)}, u32[]{:S(2)}) collective-permute-start(bf16[2,32,2048]{2,1,0:T(8,128)(2,1)S(1)} %slice_bitcast_fusion.2), channel_id=1, source_target_pairs={{0,4},{4,0},{8,12},{12,8},{16,20},{20,16},{24,28},{28,24},{1,5},{5... | collective-permute-start | bytes 786440 | tf_op jit(solution)/shard_map/ppermute | solution.py:112
  253.8 35.3 %collective-permute-start.19 = (bf16[64,2048]{1,0:T(8,128)(2,1)}, bf16[64,2048]{1,0:T(8,128)(2,1)}, u32[]{:S(2)}, u32[]{:S(2)}) collective-permute-start(bf16[64,2048]{1,0:T(8,128)(2,1)} %fusion.36), channel_id=1, source_target_pairs={{0,24},{4,28},{8,0},{12,4},{16,8},{20,12},{24,16},{28,20},{1,25},{... | collective-permute-start | bytes 786440 | tf_op jit(solution)/shard_map/ppermute | solution.py:94
  274.5 24.0 %copy-start.1 = (bf16[512,2048]{1,0:T(8,128)(2,1)S(1)}, bf16[512,2048]{1,0:T(8,128)(2,1)}, u32[]{:S(2)}) copy-start(bf16[512,2048]{1,0:T(8,128)(2,1)} %param.27) | copy-start | bytes 6291460
  274.5 23.0 %collective-permute-start.36 = (bf16[2,1,768,256]{3,2,1,0:T(8,128)(2,1)S(1)}, bf16[2,1,768,256]{3,2,1,0:T(8,128)(2,1)S(1)}, u32[]{:S(2)}, u32[]{:S(2)}) collective-permute-start(bf16[2,1,768,256]{3,2,1,0:T(8,128)(2,1)S(1)} %get-tuple-element.51), channel_id=1, source_target_pairs={{0,4},{4,0},{8,12},{12,8},{16,20},{20,16},{24,28},{28,24},{1,5},{5... | collective-permute-start | bytes 2359304 | tf_op jit(solution)/shard_map/ppermute | solution.py:99
  276.3 13.0 %collective-permute-start.33 = (bf16[64,2048]{1,0:T(8,128)(2,1)S(1)}, bf16[64,2048]{1,0:T(8,128)(2,1)S(1)}, u32[]{:S(2)}, u32[]{:S(2)}) collective-permute-start(bf16[64,2048]{1,0:T(8,128)(2,1)S(1)} %get-tuple-element.71), channel_id=1, source_target_pairs={{0,16},{4,20},{8,24},{12,28},{16,0},{20,4},{24,8},{28,12},{1,17},{... | collective-permute-start | bytes 786440 | tf_op jit(solution)/shard_map/ppermute | solution.py:94
  276.4 19.3 %collective-permute-start.34 = (bf16[64,2048]{1,0:T(8,128)(2,1)S(1)}, bf16[64,2048]{1,0:T(8,128)(2,1)S(1)}, u32[]{:S(2)}, u32[]{:S(2)}) collective-permute-start(bf16[64,2048]{1,0:T(8,128)(2,1)S(1)} %get-tuple-element.72), channel_id=1, source_target_pairs={{0,8},{4,12},{8,16},{12,20},{16,24},{20,28},{24,0},{28,4},{1,9},{5... | collective-permute-start | bytes 786440 | tf_op jit(solution)/shard_map/ppermute | solution.py:94
  (17 other events, 72.7 us)

commit v5 on v3

--- a/solution.py
+++ b/solution.py
@@ -400,6 +400,7 @@
     slots_here = slot_weights.shape[0]
     index = chunk_index(source_slot, slots_here)
     size = held[0].shape[1] // 2
+    normed, *held[3:] = together(normed, *held[3:])
     mixture, first, mixed = mix(
         normed, codes, slot_weights, held, lambda held: take_chunks(held, index, 0, size)
     )

time: 299 us -> 307 us (1.027)
  waiting for transfers between devices: 127 us -> 136 us
  starting transfers between devices: 69 us -> 63.8 us
  Pallas kernels: 30 us -> 33.3 us
    ppermute x9, waiting for transfers between devices: 10.3 us -> 21.4 us  [turn_pairs(): lax.ppermute(value, 'req', [(i, (i + 2 * step) % count) for i in range(co...]
    ppermute x9, waiting for transfers between devices: 50.7 us -> 55.4 us  [flip_pair(): return lax.ppermute(value, 'req', [(i, i ^ 1) for i in range(count)])]
    ppermute x5, waiting for transfers between devices: 37.8 us -> 33.6 us  [swap(): return lax.ppermute(value, 'req', [(i, i ^ mask) for i in range(count)])]
    pallas_call x2, Pallas kernels: 7.71 us -> 11 us  [take_chunks(): pl.pallas_call(functools.partial(pick_kernel, slots_here), out_shape=jax....]
  transfers between devices with their start and end apart: 39 -> 39, of which waited for: 17 -> 18; matrix products, arithmetic and copies ran while one was open for 16% -> 15% of each run, Pallas kernels for 10% -> 11%
where the time goes in v5:
time: 307 us; the launch traced here: 306 us
  waiting for transfers between devices  136 us (44%)
  starting transfers between devices  63.8 us (21%)
  Pallas kernels  33.3 us (11%)
  local copies, waits for them, and re-layouts  31.6 us (10%)
  other arithmetic  26 us (8%)
  between operations  9.8 us (3%)
  matrix products  5.19 us (2%)
    ppermute x9, waiting for transfers between devices, flip_pair(): return lax.ppermute(value, 'req', [(i, i ^ 1) for i in range(count)])  55.4 us
    ppermute x5, waiting for transfers between devices, swap(): return lax.ppermute(value, 'req', [(i, i ^ mask) for i in range(count)])  33.6 us
    ppermute x9, starting transfers between devices, turn_pairs(): lax.ppermute(value, 'req', [(i, (i + 2 * step) % count) for i in range(co...  27.6 us
    pallas_call x4, Pallas kernels, run_experts(): pl.pallas_call(experts_kernel, out_shape=jax.ShapeDtypeStruct((count, wid...  22.3 us
    ppermute x9, waiting for transfers between devices, turn_pairs(): lax.ppermute(value, 'req', [(i, (i + 2 * step) % count) for i in range(co...  21.4 us
    ppermute x9, waiting for transfers between devices, flip_chip(): return lax.ppermute(value, 'exp', [(i, i ^ 2) for i in range(count)])  14 us
    unnamed x57, local copies, waits for them, and re-layouts  12.9 us
    all_to_all x2, waiting for transfers between devices, trade_columns(): lax.all_to_all(outgoing, 'req', 0, 0, axis_index_groups=columns, tiled=True)  12 us
  transfers between devices with their start and end apart: 39, of which 18 were waited for; matrix products, arithmetic and copies ran while one was open for 15% of the time, Pallas kernels for 11%

profile of v5, /device:TPU:0, one launch (start us, length us, event | category | flops | bytes accessed | tf_op | source)
XLA Modules:
  0.0 306.2 jit_solution(1462795585367452560)
XLA Ops:
  0.6 1.7 fusion.69
  2.4 4.0 %collective-permute-start.1 = (bf16[2,2,32,512]{3,2,1,0:T(8,128)(2,1)}, bf16[2,2,32,512]{3,2,1,0:T(8,128)(2,1)}, u32[]{:S(2)}, u32[]{:S(2)}) collective-permute-start(bf16[2,2,32,512]{3,2,1,0:T(8,128)(2,1)} %get-tuple-element.86), channel_id=1, source_target_pairs={{0,16},{4,20},{8,24},{12,28},{16,0},{20,4},{24,8},{28,12},{1,17},{... | collective-permute-start | bytes 393224 | tf_op jit(solution)/shard_map/ppermute | solution.py:94
  8.0 2.2 collective-permute-start.2
  10.2 5.7 %dynamic-slice_bitcast_fusion = (bf16[2,1536,256]{2,1,0:T(8,128)(2,1)}, bf16[2,1536,256]{2,1,0:T(8,128)(2,1)}, bf16[2,1536,256]{2,1,0:T(8,128)(2,1)}, bf16[2,1536,256]{2,1,0:T(8,128)(2,1)}) fusion(bf16[2,4,1536,256]{3,2,1,0:T(8,128)(2,1)} %bitcast.154, s32[]{:T(128)S(6)} %select_n.262, s32[]{:T(128)S(6)} %select_n.255, s32[]{:T(128)S(6)} %select_n.248, ...), kind=kLoop, calls=%fused_computation.6 | loop fusion | bytes 12582928 | tf_op jit(solution)/shard_map/jit(dynamic_index_in_dim)/squeeze | solution.py:126
  16.0 1.6 collective-permute-start.4
  34.6 19.7 %collective-permute-done.3 = bf16[2,2,32,512]{3,2,1,0:T(8,128)(2,1)S(1)} collective-permute-done((bf16[2,2,32,512]{3,2,1,0:T(8,128)(2,1)S(1)}, bf16[2,2,32,512]{3,2,1,0:T(8,128)(2,1)S(1)}, u32[]{:S(2)}, u32[]{:S(2)}) %collective-permute-start.3) | collective-permute-done | bytes 131104 | tf_op jit(solution)/shard_map/ppermute | solution.py:112
  54.5 2.8 fusion.78
  57.3 1.7 convolution_convert_fusion
  61.3 2.7 collective-permute-start.8
  68.5 6.3 %collective-permute-done.7 = bf16[64,2048]{1,0:T(8,128)(2,1)S(1)} collective-permute-done((bf16[64,2048]{1,0:T(8,128)(2,1)S(1)}, bf16[64,2048]{1,0:T(8,128)(2,1)S(1)}, u32[]{:S(2)}, u32[]{:S(2)}) %collective-permute-start.7) | collective-permute-done | bytes 262176 | tf_op jit(solution)/shard_map/ppermute | solution.py:117
  76.3 23.0 %collective-permute-done.8.refs_3_ = bf16[2,1536,256]{2,1,0:T(8,128)(2,1)} collective-permute-done((bf16[2,1536,256]{2,1,0:T(8,128)(2,1)}, bf16[2,1536,256]{2,1,0:T(8,128)(2,1)}, u32[]{:S(2)}, u32[]{:S(2)}) %collective-permute-start.8) | collective-permute-done | bytes 1572896 | tf_op jit(solution)/shard_map/ppermute | solution.py:99
  99.4 1.7 collective-permute-start.9
  101.1 2.2 collective-permute-start.22
  103.4 5.5 %shard_map.178 = bf16[8,768,256]{2,1,0:T(8,128)(2,1)S(1)} custom-call(s32[8]{0:T(128)S(1)} %fusion.50.index_ref, bf16[2,1536,256]{2,1,0:T(8,128)(2,1)S(1)} %copy-done.2, bf16[2,1536,256]{2,1,0:T(8,128)(2,1)} %collective-permute-done.4.refs_1_, bf16[2,1536,256]{2,1,0:T(8,128)(2,1)} %collective-permute-done.5.refs_2_, ...), custom_call_target="tpu_custom_call" | custom-call | bytes 6291456 | tf_op jit(solution)/shard_map/pallas_call | solution.py:253
  108.9 1.9 collective-permute-done.9
  110.9 1.6 collective-permute-start.10
  113.9 12.8 %collective-permute-done.21 = bf16[64,2176]{1,0:T(8,128)(2,1)S(1)} collective-permute-done((bf16[64,2176]{1,0:T(8,128)(2,1)S(1)}, bf16[64,2176]{1,0:T(8,128)(2,1)S(1)}, u32[]{:S(2)}, u32[]{:S(2)}) %collective-permute-start.21) | collective-permute-done | bytes 278560 | tf_op jit(solution)/shard_map/ppermute | solution.py:94
  131.4 4.9 %all-to-all-start = ((bf16[4,2,768,256]{3,2,1,0:T(8,128)(2,1)}), bf16[4,2,768,256]{3,2,1,0:T(8,128)(2,1)}, u32[]{:S(2)}, u32[]{:S(2)}) async-start(bf16[4,2,768,256]{3,2,1,0:T(8,128)(2,1)} %bitcast.152), calls=%async_computation | async-start | bytes 6291456 | tf_op jit(solution)/shard_map/all_to_all | solution.py:273
  139.5 4.7 %collective-permute-done.13 = bf16[2,2,32,2176]{3,2,1,0:T(8,128)(2,1)} collective-permute-done((bf16[2,2,32,2176]{3,2,1,0:T(8,128)(2,1)S(1)}, bf16[2,2,32,2176]{3,2,1,0:T(8,128)(2,1)}, u32[]{:S(2)}, u32[]{:S(2)}) %collective-permute-start.13) | collective-permute-done | bytes 557088 | tf_op jit(solution)/shard_map/ppermute | solution.py:112
  144.2 2.7 collective-permute-done.11
  146.9 3.0 pad_maximum_fusion.tok_ref
  151.5 8.6 %collective-permute-done.26 = bf16[2,2,32,2176]{3,2,1,0:T(8,128)(2,1)S(1)} collective-permute-done((bf16[2,2,32,2176]{3,2,1,0:T(8,128)(2,1)S(1)}, bf16[2,2,32,2176]{3,2,1,0:T(8,128)(2,1)S(1)}, u32[]{:S(2)}, u32[]{:S(2)}) %collective-permute-start.26) | collective-permute-done | bytes 557088 | tf_op jit(solution)/shard_map/ppermute | solution.py:112
  160.1 5.0 %collective-permute-done.24 = bf16[2,2,32,2176]{3,2,1,0:T(8,128)(2,1)S(1)} collective-permute-done((bf16[2,2,32,2176]{3,2,1,0:T(8,128)(2,1)S(1)}, bf16[2,2,32,2176]{3,2,1,0:T(8,128)(2,1)S(1)}, u32[]{:S(2)}, u32[]{:S(2)}) %collective-permute-start.24) | collective-permute-done | bytes 557088 | tf_op jit(solution)/shard_map/ppermute | solution.py:117
  166.6 2.8 copy-done.5
  169.3 6.1 %shard_map.177 = bf16[512,2048]{1,0:T(8,128)(2,1)} custom-call(s32[1]{0:T(128)} %bitcast.35.first_slot_ref, bf16[512,2176]{1,0:T(8,128)(2,1)} %collective-permute-done.14.tok_ref, bf16[2,3,2048,256]{3,2,1,0:T(8,128)(2,1)S(1)} %copy-done.5), custom_call_target="tpu_custom_call" | custom-call | flops 3221225472 | bytes 10485760 | tf_op jit(solution)/shard_map/pallas_call | solution.py:73
  175.9 6.0 %shard_map.180 = bf16[512,2048]{1,0:T(8,128)(2,1)} custom-call(s32[1]{0:T(128)} %bitcast.35.first_slot_ref, bf16[512,2176]{1,0:T(8,128)(2,1)} %collective-permute-done.27.tok_ref, bf16[2,3,2048,256]{3,2,1,0:T(8,128)(2,1)S(1)} %copy-done.5), custom_call_target="tpu_custom_call" | custom-call | flops 3221225472 | bytes 10485760 | tf_op jit(solution)/shard_map/pallas_call | solution.py:73
  183.9 5.5 %shard_map.181 = bf16[8,768,256]{2,1,0:T(8,128)(2,1)S(1)} custom-call(s32[8]{0:T(128)S(1)} %fusion.50.index_ref, bf16[2,1536,256]{2,1,0:T(8,128)(2,1)S(1)} %copy-done.2, bf16[2,1536,256]{2,1,0:T(8,128)(2,1)} %collective-permute-done.4.refs_1_, bf16[2,1536,256]{2,1,0:T(8,128)(2,1)} %collective-permute-done.5.refs_2_, ...), custom_call_target="tpu_custom_call" | custom-call | bytes 6291456 | tf_op jit(solution)/shard_map/pallas_call | solution.py:253
  189.4 1.6 copy-done.4
  191.0 2.8 copy-done.6
  193.8 5.1 %shard_map.176 = bf16[512,2048]{1,0:T(8,128)(2,1)S(1)} custom-call(s32[1]{0:T(128)} %bitcast.35.first_slot_ref, bf16[512,2176]{1,0:T(8,128)(2,1)} %pad_maximum_fusion.tok_ref, bf16[2,3,2048,256]{3,2,1,0:T(8,128)(2,1)S(1)} %copy-done.6), custom_call_target="tpu_custom_call" | custom-call | flops 3221225472 | bytes 10485760 | tf_op jit(solution)/shard_map/pallas_call | solution.py:73
  198.9 6.9 %all-to-all-done = bf16[4,2,768,256]{3,2,1,0:T(8,128)(2,1)} async-done(((bf16[4,2,768,256]{3,2,1,0:T(8,128)(2,1)}), bf16[4,2,768,256]{3,2,1,0:T(8,128)(2,1)}, u32[]{:S(2)}, u32[]{:S(2)}) %all-to-all-start) | async-done | bytes 3145760 | tf_op jit(solution)/shard_map/all_to_all | solution.py:273
  205.9 4.7 %all-to-all-start.1 = ((bf16[4,2,768,256]{3,2,1,0:T(8,128)(2,1)}), bf16[4,2,768,256]{3,2,1,0:T(8,128)(2,1)}, u32[]{:S(2)}, u32[]{:S(2)}) async-start(bf16[4,2,768,256]{3,2,1,0:T(8,128)(2,1)} %bitcast.153), calls=%async_computation.1 | async-start | bytes 6291456 | tf_op jit(solution)/shard_map/all_to_all | solution.py:273
  210.5 2.8 copy-done.7
  213.3 5.1 %shard_map.179 = bf16[512,2048]{1,0:T(8,128)(2,1)S(1)} custom-call(s32[1]{0:T(128)} %bitcast.35.first_slot_ref, bf16[512,2176]{1,0:T(8,128)(2,1)} %pad_maximum_fusion.1.tok_ref, bf16[2,3,2048,256]{3,2,1,0:T(8,128)(2,1)S(1)} %copy-done.7), custom_call_target="tpu_custom_call" | custom-call | flops 3221225472 | bytes 10485760 | tf_op jit(solution)/shard_map/pallas_call | solution.py:73
  218.4 1.9 broadcast_in_dim.162
  220.3 2.5 constant_dynamic-slice_fusion.1
  223.3 2.4 add_convert_fusion.1
  229.0 2.4 add_convert_fusion
  232.7 10.5 %collective-permute-done.35 = bf16[2,1,768,256]{3,2,1,0:T(8,128)(2,1)S(1)} collective-permute-done((bf16[2,1,768,256]{3,2,1,0:T(8,128)(2,1)S(1)}, bf16[2,1,768,256]{3,2,1,0:T(8,128)(2,1)S(1)}, u32[]{:S(2)}, u32[]{:S(2)}) %collective-permute-start.35) | collective-permute-done | bytes 786464 | tf_op jit(solution)/shard_map/ppermute | solution.py:99
  244.2 10.3 %collective-permute-done.18 = bf16[2,2,32,2048]{3,2,1,0:T(8,128)(2,1)S(1)} collective-permute-done((bf16[2,2,32,2048]{3,2,1,0:T(8,128)(2,1)S(1)}, bf16[2,2,32,2048]{3,2,1,0:T(8,128)(2,1)S(1)}, u32[]{:S(2)}, u32[]{:S(2)}) %collective-permute-start.18) | collective-permute-done | bytes 524320 | tf_op jit(solution)/shard_map/ppermute | solution.py:112
  256.9 8.8 %collective-permute-done.31 = bf16[2,2,32,2048]{3,2,1,0:T(8,128)(2,1)S(1)} collective-permute-done((bf16[2,2,32,2048]{3,2,1,0:T(8,128)(2,1)S(1)}, bf16[2,2,32,2048]{3,2,1,0:T(8,128)(2,1)S(1)}, u32[]{:S(2)}, u32[]{:S(2)}) %collective-permute-start.31) | collective-permute-done | bytes 524320 | tf_op jit(solution)/shard_map/ppermute | solution.py:112
  268.2 3.1 %collective-permute-done.17 = bf16[2,32,2048]{2,1,0:T(8,128)(2,1)S(1)} collective-permute-done((bf16[2,32,2048]{2,1,0:T(8,128)(2,1)S(1)}, bf16[2,32,2048]{2,1,0:T(8,128)(2,1)S(1)}, u32[]{:S(2)}, u32[]{:S(2)}) %collective-permute-start.17) | collective-permute-done | bytes 262176 | tf_op jit(solution)/shard_map/ppermute | solution.py:112
  272.1 3.8 %collective-permute-start.20 = (bf16[64,2048]{1,0:T(8,128)(2,1)}, bf16[64,2048]{1,0:T(8,128)(2,1)}, u32[]{:S(2)}, u32[]{:S(2)}) collective-permute-start(bf16[64,2048]{1,0:T(8,128)(2,1)} %fusion.34), channel_id=1, source_target_pairs={{0,24},{4,28},{8,0},{12,4},{16,8},{20,12},{24,16},{28,20},{1,25},{... | collective-permute-start | bytes 786440 | tf_op jit(solution)/shard_map/ppermute | solution.py:94
  276.8 5.1 %all-to-all-done.1 = bf16[4,2,768,256]{3,2,1,0:T(8,128)(2,1)} async-done(((bf16[4,2,768,256]{3,2,1,0:T(8,128)(2,1)}), bf16[4,2,768,256]{3,2,1,0:T(8,128)(2,1)}, u32[]{:S(2)}, u32[]{:S(2)}) %all-to-all-start.1) | async-done | bytes 3145760 | tf_op jit(solution)/shard_map/all_to_all | solution.py:273
  281.8 2.4 constant_dynamic-slice_fusion
  284.9 12.0 %collective-permute-start.34 = (bf16[64,2048]{1,0:T(8,128)(2,1)S(1)}, bf16[64,2048]{1,0:T(8,128)(2,1)S(1)}, u32[]{:S(2)}, u32[]{:S(2)}) collective-permute-start(bf16[64,2048]{1,0:T(8,128)(2,1)S(1)} %get-tuple-element.76), channel_id=1, source_target_pairs={{0,8},{4,12},{8,16},{12,20},{16,24},{20,28},{24,0},{28,4},{1,9},{5... | collective-permute-start | bytes 786440 | tf_op jit(solution)/shard_map/ppermute | solution.py:94
  297.8 5.7 %collective-permute-done.34 = bf16[64,2048]{1,0:T(8,128)(2,1)S(1)} collective-permute-done((bf16[64,2048]{1,0:T(8,128)(2,1)S(1)}, bf16[64,2048]{1,0:T(8,128)(2,1)S(1)}, u32[]{:S(2)}, u32[]{:S(2)}) %collective-permute-start.34) | collective-permute-done | bytes 262176 | tf_op jit(solution)/shard_map/ppermute | solution.py:94
  303.4 1.8 fusion.14
  (188 shorter events, 48.4 us)
Async XLA Ops:
  0.6 58.4 %copy-start = (bf16[512,2048]{1,0:T(8,128)(2,1)S(1)}, bf16[512,2048]{1,0:T(8,128)(2,1)}, u32[]{:S(2)}) copy-start(bf16[512,2048]{1,0:T(8,128)(2,1)} %param.27) | copy-start | bytes 6291460
  2.4 29.7 %collective-permute-start.1 = (bf16[2,2,32,512]{3,2,1,0:T(8,128)(2,1)}, bf16[2,2,32,512]{3,2,1,0:T(8,128)(2,1)}, u32[]{:S(2)}, u32[]{:S(2)}) collective-permute-start(bf16[2,2,32,512]{3,2,1,0:T(8,128)(2,1)} %get-tuple-element.86), channel_id=1, source_target_pairs={{0,16},{4,20},{8,24},{12,28},{16,0},{20,4},{24,8},{28,12},{1,17},{... | collective-permute-start | bytes 393224 | tf_op jit(solution)/shard_map/ppermute | solution.py:94
  6.4 25.7 %collective-permute-start = (bf16[2,2,32,512]{3,2,1,0:T(8,128)(2,1)}, bf16[2,2,32,512]{3,2,1,0:T(8,128)(2,1)}, u32[]{:S(2)}, u32[]{:S(2)}) collective-permute-start(bf16[2,2,32,512]{3,2,1,0:T(8,128)(2,1)} %get-tuple-element.86), channel_id=1, source_target_pairs={{0,8},{4,12},{8,16},{12,20},{16,24},{20,28},{24,0},{28,4},{1,9},{5... | collective-permute-start | bytes 393224 | tf_op jit(solution)/shard_map/ppermute | solution.py:94
  8.0 24.2 %collective-permute-start.2 = (bf16[2,2,32,512]{3,2,1,0:T(8,128)(2,1)}, bf16[2,2,32,512]{3,2,1,0:T(8,128)(2,1)}, u32[]{:S(2)}, u32[]{:S(2)}) collective-permute-start(bf16[2,2,32,512]{3,2,1,0:T(8,128)(2,1)} %get-tuple-element.86), channel_id=1, source_target_pairs={{0,24},{4,28},{8,0},{12,4},{16,8},{20,12},{24,16},{28,20},{1,25},{... | collective-permute-start | bytes 393224 | tf_op jit(solution)/shard_map/ppermute | solution.py:94
  10.2 8.9 %copy-start.13 = (bf16[256,512]{1,0:T(8,128)(2,1)S(1)}, bf16[256,512]{1,0:T(8,128)(2,1)}, u32[]{:S(2)}) copy-start(bf16[256,512]{1,0:T(8,128)(2,1)} %param.18) | copy-start | bytes 786436
  10.2 9.1 %copy-start.14 = (bf16[256,512]{1,0:T(8,128)(2,1)S(1)}, bf16[256,512]{1,0:T(8,128)(2,1)}, u32[]{:S(2)}) copy-start(bf16[256,512]{1,0:T(8,128)(2,1)} %param.19) | copy-start | bytes 786436
  15.9 43.1 %collective-permute-start.5 = (bf16[2,1536,256]{2,1,0:T(8,128)(2,1)}, bf16[2,1536,256]{2,1,0:T(8,128)(2,1)}, u32[]{:S(2)}, u32[]{:S(2)}) collective-permute-start(bf16[2,1536,256]{2,1,0:T(8,128)(2,1)} %get-tuple-element.53), channel_id=1, source_target_pairs={{0,8},{4,12},{8,0},{12,4},{16,24},{20,28},{24,16},{28,20},{1,9},{5... | collective-permute-start | bytes 4718600 | tf_op jit(solution)/shard_map/ppermute | solution.py:99
  16.0 43.1 %collective-permute-start.4 = (bf16[2,1536,256]{2,1,0:T(8,128)(2,1)}, bf16[2,1536,256]{2,1,0:T(8,128)(2,1)}, u32[]{:S(2)}, u32[]{:S(2)}) collective-permute-start(bf16[2,1536,256]{2,1,0:T(8,128)(2,1)} %get-tuple-element.54), channel_id=1, source_target_pairs={{0,4},{4,0},{8,12},{12,8},{16,20},{20,16},{24,28},{28,24},{1,5},{5... | collective-permute-start | bytes 4718600 | tf_op jit(solution)/shard_map/ppermute | solution.py:99
  33.3 21.0 %collective-permute-start.3 = (bf16[2,2,32,512]{3,2,1,0:T(8,128)(2,1)S(1)}, bf16[2,2,32,512]{3,2,1,0:T(8,128)(2,1)S(1)}, u32[]{:S(2)}, u32[]{:S(2)}) collective-permute-start(bf16[2,2,32,512]{3,2,1,0:T(8,128)(2,1)S(1)} %pad_maximum_fusion.12), channel_id=1, source_target_pairs={{0,4},{4,0},{8,12},{12,8},{16,20},{20,16},{24,28},{28,24},{1,5},{5... | collective-permute-start | bytes 393224 | tf_op jit(solution)/shard_map/ppermute | solution.py:112
  59.8 8.5 %copy-start.25 = (s32[8]{0:T(128)S(1)}, s32[8]{0:T(128)}, u32[]{:S(2)}) copy-start(s32[8]{0:T(128)} %param.32) | copy-start | bytes 100
  59.8 15.1 %copy-start.16 = (bf16[64,2048]{1,0:T(8,128)(2,1)S(1)}, bf16[64,2048]{1,0:T(8,128)(2,1)}, u32[]{:S(2)}) copy-start(bf16[64,2048]{1,0:T(8,128)(2,1)} %param.17) | copy-start | bytes 786436
  61.2 2.9 collective-permute-start.6
  61.3 38.0 %collective-permute-start.8 = (bf16[2,1536,256]{2,1,0:T(8,128)(2,1)}, bf16[2,1536,256]{2,1,0:T(8,128)(2,1)}, u32[]{:S(2)}, u32[]{:S(2)}) collective-permute-start(bf16[2,1536,256]{2,1,0:T(8,128)(2,1)} %get-tuple-element.52), channel_id=1, source_target_pairs={{0,12},{4,8},{8,4},{12,0},{16,28},{20,24},{24,20},{28,16},{1,13},{... | collective-permute-start | bytes 4718600 | tf_op jit(solution)/shard_map/ppermute | solution.py:99
  64.0 12.1 %copy-start.17 = (f32[2048]{0:T(1024)S(1)}, f32[2048]{0:T(1024)}, u32[]{:S(2)}) copy-start(f32[2048]{0:T(1024)} %param.28) | copy-start | bytes 24580
  66.4 37.0 %copy-start.2 = (bf16[2,1536,256]{2,1,0:T(8,128)(2,1)S(1)}, bf16[2,1536,256]{2,1,0:T(8,128)(2,1)}, u32[]{:S(2)}) copy-start(bf16[2,1536,256]{2,1,0:T(8,128)(2,1)} %get-tuple-element.51.refs_0_) | copy-start | bytes 4718596
  66.4 8.4 %collective-permute-start.7 = (bf16[64,2048]{1,0:T(8,128)(2,1)S(1)}, bf16[64,2048]{1,0:T(8,128)(2,1)S(1)}, u32[]{:S(2)}, u32[]{:S(2)}) collective-permute-start(bf16[64,2048]{1,0:T(8,128)(2,1)S(1)} %fusion.28), channel_id=1, source_target_pairs={{0,2},{1,3},{2,0},{3,1},{4,6},{5,7},{6,4},{7,5},{8,10},{9,11},{10,... | collective-permute-start | bytes 786440 | tf_op jit(solution)/shard_map/ppermute | solution.py:117
  99.4 11.4 %collective-permute-start.9 = (bf16[64,2176]{1,0:T(8,128)(2,1)S(1)}, bf16[64,2176]{1,0:T(8,128)(2,1)S(1)}, u32[]{:S(2)}, u32[]{:S(2)}) collective-permute-start(bf16[64,2176]{1,0:T(8,128)(2,1)S(1)} %concatenate.37), channel_id=1, source_target_pairs={{0,8},{4,12},{8,16},{12,20},{16,24},{20,28},{24,0},{28,4},{1,9},{5... | collective-permute-start | bytes 835592 | tf_op jit(solution)/shard_map/ppermute | solution.py:94
  101.1 25.6 %collective-permute-start.22 = (bf16[64,2176]{1,0:T(8,128)(2,1)S(1)}, bf16[64,2176]{1,0:T(8,128)(2,1)S(1)}, u32[]{:S(2)}, u32[]{:S(2)}) collective-permute-start(bf16[64,2176]{1,0:T(8,128)(2,1)S(1)} %concatenate.37), channel_id=1, source_target_pairs={{0,24},{4,28},{8,0},{12,4},{16,8},{20,12},{24,16},{28,20},{1,25},{... | collective-permute-start | bytes 835592 | tf_op jit(solution)/shard_map/ppermute | solution.py:94
  103.4 23.4 %collective-permute-start.21 = (bf16[64,2176]{1,0:T(8,128)(2,1)S(1)}, bf16[64,2176]{1,0:T(8,128)(2,1)S(1)}, u32[]{:S(2)}, u32[]{:S(2)}) collective-permute-start(bf16[64,2176]{1,0:T(8,128)(2,1)S(1)} %concatenate.37), channel_id=1, source_target_pairs={{0,16},{4,20},{8,24},{12,28},{16,0},{20,4},{24,8},{28,12},{1,17},{... | collective-permute-start | bytes 835592 | tf_op jit(solution)/shard_map/ppermute | solution.py:94
  108.9 22.0 %copy-start.3 = (bf16[8,768,256]{2,1,0:T(8,128)(2,1)}, bf16[8,768,256]{2,1,0:T(8,128)(2,1)S(1)}, u32[]{:S(2)}) copy-start(bf16[8,768,256]{2,1,0:T(8,128)(2,1)S(1)} %shard_map.178) | copy-start | bytes 9437188
  110.9 19.2 %collective-permute-start.10 = (bf16[2,32,2176]{2,1,0:T(8,128)(2,1)S(1)}, bf16[2,32,2176]{2,1,0:T(8,128)(2,1)S(1)}, u32[]{:S(2)}, u32[]{:S(2)}) collective-permute-start(bf16[2,32,2176]{2,1,0:T(8,128)(2,1)S(1)} %get-tuple-element.71), channel_id=1, source_target_pairs={{0,4},{4,0},{8,12},{12,8},{16,20},{20,16},{24,28},{28,24},{1,5},{5... | collective-permute-start | bytes 835592 | tf_op jit(solution)/shard_map/ppermute | solution.py:112
  112.4 15.9 %collective-permute-start.12 = (bf16[2,32,2176]{2,1,0:T(8,128)(2,1)S(1)}, bf16[2,32,2176]{2,1,0:T(8,128)(2,1)S(1)}, u32[]{:S(2)}, u32[]{:S(2)}) collective-permute-start(bf16[2,32,2176]{2,1,0:T(8,128)(2,1)S(1)} %get-tuple-element.72), channel_id=1, source_target_pairs={{0,2},{1,3},{2,0},{3,1},{4,6},{5,7},{6,4},{7,5},{8,10},{9,11},{10,... | collective-permute-start | bytes 835592 | tf_op jit(solution)/shard_map/ppermute | solution.py:117
  126.8 10.0 %collective-permute-start.25 = (bf16[2,32,2176]{2,1,0:T(8,128)(2,1)S(1)}, bf16[2,32,2176]{2,1,0:T(8,128)(2,1)}, u32[]{:S(2)}, u32[]{:S(2)}) collective-permute-start(bf16[2,32,2176]{2,1,0:T(8,128)(2,1)S(1)} %get-tuple-element.74), channel_id=1, source_target_pairs={{0,2},{1,3},{2,0},{3,1},{4,6},{5,7},{6,4},{7,5},{8,10},{9,11},{10,... | collective-permute-start | bytes 835592 | tf_op jit(solution)/shard_map/ppermute | solution.py:117
  128.5 15.7 %collective-permute-start.13 = (bf16[2,2,32,2176]{3,2,1,0:T(8,128)(2,1)S(1)}, bf16[2,2,32,2176]{3,2,1,0:T(8,128)(2,1)}, u32[]{:S(2)}, u32[]{:S(2)}) collective-permute-start(bf16[2,2,32,2176]{3,2,1,0:T(8,128)(2,1)S(1)} %pad_maximum_fusion.3), channel_id=1, source_target_pairs={{0,4},{4,0},{8,12},{12,8},{16,20},{20,16},{24,28},{28,24},{1,5},{5... | collective-permute-start | bytes 1671176 | tf_op jit(solution)/shard_map/ppermute | solution.py:112
  130.9 16.0 %collective-permute-start.11 = (bf16[2,2,32,2176]{3,2,1,0:T(8,128)(2,1)}, bf16[2,2,32,2176]{3,2,1,0:T(8,128)(2,1)}, u32[]{:S(2)}, u32[]{:S(2)}) collective-permute-start(bf16[2,2,32,2176]{3,2,1,0:T(8,128)(2,1)} %pad_maximum_fusion.2), channel_id=1, source_target_pairs={{0,2},{1,3},{2,0},{3,1},{4,6},{5,7},{6,4},{7,5},{8,10},{9,11},{10,... | collective-permute-start | bytes 1671176 | tf_op jit(solution)/shard_map/ppermute | solution.py:117
  131.4 74.4 %all-to-all-start = ((bf16[4,2,768,256]{3,2,1,0:T(8,128)(2,1)}), bf16[4,2,768,256]{3,2,1,0:T(8,128)(2,1)}, u32[]{:S(2)}, u32[]{:S(2)}) async-start(bf16[4,2,768,256]{3,2,1,0:T(8,128)(2,1)} %bitcast.152), calls=%async_computation | async-start | bytes 6291456 | tf_op jit(solution)/shard_map/all_to_all | solution.py:273
  136.3 13.7 %collective-permute-start.23 = (bf16[2,32,2176]{2,1,0:T(8,128)(2,1)S(1)}, bf16[2,32,2176]{2,1,0:T(8,128)(2,1)S(1)}, u32[]{:S(2)}, u32[]{:S(2)}) collective-permute-start(bf16[2,32,2176]{2,1,0:T(8,128)(2,1)S(1)} %get-tuple-element.73), channel_id=1, source_target_pairs={{0,4},{4,0},{8,12},{12,8},{16,20},{20,16},{24,28},{28,24},{1,5},{5... | collective-permute-start | bytes 835592 | tf_op jit(solution)/shard_map/ppermute | solution.py:112
  137.9 22.2 %collective-permute-start.26 = (bf16[2,2,32,2176]{3,2,1,0:T(8,128)(2,1)S(1)}, bf16[2,2,32,2176]{3,2,1,0:T(8,128)(2,1)S(1)}, u32[]{:S(2)}, u32[]{:S(2)}) collective-permute-start(bf16[2,2,32,2176]{3,2,1,0:T(8,128)(2,1)S(1)} %pad_maximum_fusion.5), channel_id=1, source_target_pairs={{0,4},{4,0},{8,12},{12,8},{16,20},{20,16},{24,28},{28,24},{1,5},{5... | collective-permute-start | bytes 1671176 | tf_op jit(solution)/shard_map/ppermute | solution.py:112
  149.8 16.7 %collective-permute-start.14 = (bf16[512,2176]{1,0:T(8,128)(2,1)}, bf16[512,2176]{1,0:T(8,128)(2,1)}, u32[]{:S(2)}, u32[]{:S(2)}) collective-permute-start(bf16[512,2176]{1,0:T(8,128)(2,1)} %pad_maximum_fusion.tok_ref), channel_id=1, source_target_pairs={{0,1},{1,0},{2,3},{3,2},{4,5},{5,4},{6,7},{7,6},{8,9},{9,8},{10,11... | collective-permute-start | bytes 6684680 | tf_op jit(solution)/shard_map/ppermute | solution.py:122
  150.1 14.9 %collective-permute-start.24 = (bf16[2,2,32,2176]{3,2,1,0:T(8,128)(2,1)S(1)}, bf16[2,2,32,2176]{3,2,1,0:T(8,128)(2,1)S(1)}, u32[]{:S(2)}, u32[]{:S(2)}) collective-permute-start(bf16[2,2,32,2176]{3,2,1,0:T(8,128)(2,1)S(1)} %pad_maximum_fusion.4), channel_id=1, source_target_pairs={{0,2},{1,3},{2,0},{3,1},{4,6},{5,7},{6,4},{7,5},{8,10},{9,11},{10,... | collective-permute-start | bytes 1671176 | tf_op jit(solution)/shard_map/ppermute | solution.py:117
  166.6 9.4 %collective-permute-start.27 = (bf16[512,2176]{1,0:T(8,128)(2,1)}, bf16[512,2176]{1,0:T(8,128)(2,1)}, u32[]{:S(2)}, u32[]{:S(2)}) collective-permute-start(bf16[512,2176]{1,0:T(8,128)(2,1)} %pad_maximum_fusion.1.tok_ref), channel_id=1, source_target_pairs={{0,1},{1,0},{2,3},{3,2},{4,5},{5,4},{6,7},{7,6},{8,9},{9,8},{10,11... | collective-permute-start | bytes 6684680 | tf_op jit(solution)/shard_map/ppermute | solution.py:122
  175.4 47.9 %collective-permute-start.15 = (bf16[512,2048]{1,0:T(8,128)(2,1)}, bf16[512,2048]{1,0:T(8,128)(2,1)}, u32[]{:S(2)}, u32[]{:S(2)}) collective-permute-start(bf16[512,2048]{1,0:T(8,128)(2,1)} %shard_map.177), channel_id=1, source_target_pairs={{0,1},{1,0},{2,3},{3,2},{4,5},{5,4},{6,7},{7,6},{8,9},{9,8},{10,11... | collective-permute-start | bytes 6291464 | tf_op jit(solution)/shard_map/ppermute | solution.py:122
  182.0 47.0 %collective-permute-start.28 = (bf16[512,2048]{1,0:T(8,128)(2,1)}, bf16[512,2048]{1,0:T(8,128)(2,1)}, u32[]{:S(2)}, u32[]{:S(2)}) collective-permute-start(bf16[512,2048]{1,0:T(8,128)(2,1)} %shard_map.180), channel_id=1, source_target_pairs={{0,1},{1,0},{2,3},{3,2},{4,5},{5,4},{6,7},{7,6},{8,9},{9,8},{10,11... | collective-permute-start | bytes 6291464 | tf_op jit(solution)/shard_map/ppermute | solution.py:122
  205.9 76.0 %all-to-all-start.1 = ((bf16[4,2,768,256]{3,2,1,0:T(8,128)(2,1)}), bf16[4,2,768,256]{3,2,1,0:T(8,128)(2,1)}, u32[]{:S(2)}, u32[]{:S(2)}) async-start(bf16[4,2,768,256]{3,2,1,0:T(8,128)(2,1)} %bitcast.153), calls=%async_computation.1 | async-start | bytes 6291456 | tf_op jit(solution)/shard_map/all_to_all | solution.py:273
  222.8 20.5 %collective-permute-start.35 = (bf16[2,1,768,256]{3,2,1,0:T(8,128)(2,1)S(1)}, bf16[2,1,768,256]{3,2,1,0:T(8,128)(2,1)S(1)}, u32[]{:S(2)}, u32[]{:S(2)}) collective-permute-start(bf16[2,1,768,256]{3,2,1,0:T(8,128)(2,1)S(1)} %get-tuple-element.57), channel_id=1, source_target_pairs={{0,4},{4,0},{8,12},{12,8},{16,20},{20,16},{24,28},{28,24},{1,5},{5... | collective-permute-start | bytes 2359304 | tf_op jit(solution)/shard_map/ppermute | solution.py:99
  225.9 28.6 %collective-permute-start.18 = (bf16[2,2,32,2048]{3,2,1,0:T(8,128)(2,1)S(1)}, bf16[2,2,32,2048]{3,2,1,0:T(8,128)(2,1)S(1)}, u32[]{:S(2)}, u32[]{:S(2)}) collective-permute-start(bf16[2,2,32,2048]{3,2,1,0:T(8,128)(2,1)S(1)} %bitcast.178), channel_id=1, source_target_pairs={{0,4},{4,0},{8,12},{12,8},{16,20},{20,16},{24,28},{28,24},{1,5},{5... | collective-permute-start | bytes 1572872 | tf_op jit(solution)/shard_map/ppermute | solution.py:112
  227.5 28.7 %collective-permute-start.16 = (bf16[2,2,32,2048]{3,2,1,0:T(8,128)(2,1)S(1)}, bf16[2,2,32,2048]{3,2,1,0:T(8,128)(2,1)S(1)}, u32[]{:S(2)}, u32[]{:S(2)}) collective-permute-start(bf16[2,2,32,2048]{3,2,1,0:T(8,128)(2,1)S(1)} %bitcast.176), channel_id=1, source_target_pairs={{0,2},{1,3},{2,0},{3,1},{4,6},{5,7},{6,4},{7,5},{8,10},{9,11},{10,... | collective-permute-start | bytes 1572872 | tf_op jit(solution)/shard_map/ppermute | solution.py:117
  231.6 34.1 %collective-permute-start.31 = (bf16[2,2,32,2048]{3,2,1,0:T(8,128)(2,1)S(1)}, bf16[2,2,32,2048]{3,2,1,0:T(8,128)(2,1)S(1)}, u32[]{:S(2)}, u32[]{:S(2)}) collective-permute-start(bf16[2,2,32,2048]{3,2,1,0:T(8,128)(2,1)S(1)} %bitcast.177), channel_id=1, source_target_pairs={{0,4},{4,0},{8,12},{12,8},{16,20},{20,16},{24,28},{28,24},{1,5},{5... | collective-permute-start | bytes 1572872 | tf_op jit(solution)/shard_map/ppermute | solution.py:112
  232.2 35.3 %collective-permute-start.29 = (bf16[2,2,32,2048]{3,2,1,0:T(8,128)(2,1)S(1)}, bf16[2,2,32,2048]{3,2,1,0:T(8,128)(2,1)S(1)}, u32[]{:S(2)}, u32[]{:S(2)}) collective-permute-start(bf16[2,2,32,2048]{3,2,1,0:T(8,128)(2,1)S(1)} %bitcast.175), channel_id=1, source_target_pairs={{0,2},{1,3},{2,0},{3,1},{4,6},{5,7},{6,4},{7,5},{8,10},{9,11},{10,... | collective-permute-start | bytes 1572872 | tf_op jit(solution)/shard_map/ppermute | solution.py:117
  254.6 13.5 %collective-permute-start.19 = (bf16[2,32,2048]{2,1,0:T(8,128)(2,1)S(1)}, bf16[2,32,2048]{2,1,0:T(8,128)(2,1)S(1)}, u32[]{:S(2)}, u32[]{:S(2)}) collective-permute-start(bf16[2,32,2048]{2,1,0:T(8,128)(2,1)S(1)} %slice_bitcast_fusion.4), channel_id=1, source_target_pairs={{0,2},{1,3},{2,0},{3,1},{4,6},{5,7},{6,4},{7,5},{8,10},{9,11},{10,... | collective-permute-start | bytes 786440 | tf_op jit(solution)/shard_map/ppermute | solution.py:117
  256.4 15.0 %collective-permute-start.17 = (bf16[2,32,2048]{2,1,0:T(8,128)(2,1)S(1)}, bf16[2,32,2048]{2,1,0:T(8,128)(2,1)S(1)}, u32[]{:S(2)}, u32[]{:S(2)}) collective-permute-start(bf16[2,32,2048]{2,1,0:T(8,128)(2,1)S(1)} %slice_bitcast_fusion.6), channel_id=1, source_target_pairs={{0,4},{4,0},{8,12},{12,8},{16,20},{20,16},{24,28},{28,24},{1,5},{5... | collective-permute-start | bytes 786440 | tf_op jit(solution)/shard_map/ppermute | solution.py:112
  265.9 10.0 %collective-permute-start.32 = (bf16[2,32,2048]{2,1,0:T(8,128)(2,1)S(1)}, bf16[2,32,2048]{2,1,0:T(8,128)(2,1)S(1)}, u32[]{:S(2)}, u32[]{:S(2)}) collective-permute-start(bf16[2,32,2048]{2,1,0:T(8,128)(2,1)S(1)} %slice_bitcast_fusion), channel_id=1, source_target_pairs={{0,2},{1,3},{2,0},{3,1},{4,6},{5,7},{6,4},{7,5},{8,10},{9,11},{10,... | collective-permute-start | bytes 786440 | tf_op jit(solution)/shard_map/ppermute | solution.py:117
  267.6 8.4 %collective-permute-start.30 = (bf16[2,32,2048]{2,1,0:T(8,128)(2,1)S(1)}, bf16[2,32,2048]{2,1,0:T(8,128)(2,1)S(1)}, u32[]{:S(2)}, u32[]{:S(2)}) collective-permute-start(bf16[2,32,2048]{2,1,0:T(8,128)(2,1)S(1)} %slice_bitcast_fusion.2), channel_id=1, source_target_pairs={{0,4},{4,0},{8,12},{12,8},{16,20},{20,16},{24,28},{28,24},{1,5},{5... | collective-permute-start | bytes 786440 | tf_op jit(solution)/shard_map/ppermute | solution.py:112
  272.1 24.7 %collective-permute-start.20 = (bf16[64,2048]{1,0:T(8,128)(2,1)}, bf16[64,2048]{1,0:T(8,128)(2,1)}, u32[]{:S(2)}, u32[]{:S(2)}) collective-permute-start(bf16[64,2048]{1,0:T(8,128)(2,1)} %fusion.34), channel_id=1, source_target_pairs={{0,24},{4,28},{8,0},{12,4},{16,8},{20,12},{24,16},{28,20},{1,25},{... | collective-permute-start | bytes 786440 | tf_op jit(solution)/shard_map/ppermute | solution.py:94
  284.2 21.9 %copy-start.1 = (bf16[512,2048]{1,0:T(8,128)(2,1)S(1)}, bf16[512,2048]{1,0:T(8,128)(2,1)}, u32[]{:S(2)}) copy-start(bf16[512,2048]{1,0:T(8,128)(2,1)} %param.27) | copy-start | bytes 6291460
  284.2 21.0 %collective-permute-start.36 = (bf16[2,1,768,256]{3,2,1,0:T(8,128)(2,1)S(1)}, bf16[2,1,768,256]{3,2,1,0:T(8,128)(2,1)S(1)}, u32[]{:S(2)}, u32[]{:S(2)}) collective-permute-start(bf16[2,1,768,256]{3,2,1,0:T(8,128)(2,1)S(1)} %get-tuple-element.55), channel_id=1, source_target_pairs={{0,4},{4,0},{8,12},{12,8},{16,20},{20,16},{24,28},{28,24},{1,5},{5... | collective-permute-start | bytes 2359304 | tf_op jit(solution)/shard_map/ppermute | solution.py:99
  284.8 13.0 %collective-permute-start.33 = (bf16[64,2048]{1,0:T(8,128)(2,1)S(1)}, bf16[64,2048]{1,0:T(8,128)(2,1)S(1)}, u32[]{:S(2)}, u32[]{:S(2)}) collective-permute-start(bf16[64,2048]{1,0:T(8,128)(2,1)S(1)} %get-tuple-element.75), channel_id=1, source_target_pairs={{0,16},{4,20},{8,24},{12,28},{16,0},{20,4},{24,8},{28,12},{1,17},{... | collective-permute-start | bytes 786440 | tf_op jit(solution)/shard_map/ppermute | solution.py:94
  284.9 18.5 %collective-permute-start.34 = (bf16[64,2048]{1,0:T(8,128)(2,1)S(1)}, bf16[64,2048]{1,0:T(8,128)(2,1)S(1)}, u32[]{:S(2)}, u32[]{:S(2)}) collective-permute-start(bf16[64,2048]{1,0:T(8,128)(2,1)S(1)} %get-tuple-element.76), channel_id=1, source_target_pairs={{0,8},{4,12},{8,16},{12,20},{16,24},{20,28},{24,0},{28,4},{1,9},{5... | collective-permute-start | bytes 786440 | tf_op jit(solution)/shard_map/ppermute | solution.py:94
  (17 other events, 72.2 us)
